TPU v7x, 32 devices: a whole 2x2x4 slice. The times are simulated.
32 devices in a mesh: dp: 2 (over y), seq: 16 (over z, x, core).
Axes of the slice: x: 2, y: 2, z: 4, core: 2. Of those that a mesh axis runs over, the one named last changes fastest.
Arguments:
- tokens: bfloat16 [4, 2048, 1024], P('dp', 'seq'), may hold values from -24 to 24
- doc_ids: int32 [4, 2048], P('dp'), may hold values from 0 to 3, as said below
- norm_attn: bfloat16 [1024], P(('dp', 'seq')), may hold values from 0.5 to 1.5
- norm_mlp: bfloat16 [1024], P(('dp', 'seq')), may hold values from 0.5 to 1.5
- w_qkv: bfloat16 [1024, 3072], P(('dp', 'seq')), may hold values from -0.1875 to 0.1875
- w_out: bfloat16 [1024, 1024], P(('dp', 'seq')), may hold values from -0.5 to 0.5
- w_in: bfloat16 [1024, 5248], P(('dp', 'seq')), may hold values from -0.1875 to 0.1875
- w_down: bfloat16 [1024, 2624], P(('dp', 'seq')), may hold values from -0.125 to 0.125
- cotangent: bfloat16 [4, 2048, 1024], P('dp', 'seq'), may hold values from -6 to 6
Outputs:
- layer_out: bfloat16 [4, 2048, 1024], P('dp', 'seq')
- input_grad: float32 [4, 2048, 1024], P('dp', 'seq')
- grad_norm_attn: float32 [1024], P(('dp', 'seq'))
- grad_norm_mlp: float32 [1024], P(('dp', 'seq'))
- grad_w_qkv: float32 [1024, 3072], P(('dp', 'seq'))
- grad_w_out: float32 [1024, 1024], P(('dp', 'seq'))
- grad_w_in: float32 [1024, 5248], P(('dp', 'seq'))
- grad_w_down: float32 [1024, 2624], P(('dp', 'seq'))
Inputs may be any that keep to these rules, and one draw needn't show every extreme that they name: `doc_ids`: along each stream the ids start at 0, never fall, and rise by at most one from one token to the next.
All inputs are finite; a program needn't handle non-finite values.
Results may differ from a plain program's by a relative error of at most 0.014.
Values may be sent and summed in bfloat16 or wider, within the bound.
No kernel may reach another device: no remote copies, remote signals or barrier semaphores. Data moves between devices by JAX's collectives and lax.ppermute only.
A program may use at most 192 MiB of HBM per device.

v0:
```python
import jax
import jax.numpy as jnp
from jax import lax
from jax.sharding import PartitionSpec as P

HD = 64
HALF = 64


NORM_EPSILON = 1e-05
ROPE_BASE = 10000.0


def with_halo(block, sides, width):
    for axis, dim in sides:
        count = lax.axis_size(axis)
        forward = [(i, i + 1) for i in range(count - 1)]
        backward = [(target, source) for source, target in forward]
        low = lax.ppermute(
            lax.slice_in_dim(block, block.shape[dim] - width, None, axis=dim), axis, forward
        )
        high = lax.ppermute(lax.slice_in_dim(block, 0, width, axis=dim), axis, backward)
        block = jnp.concatenate([low, block, high], axis=dim)
    return block


def from_behind(block, axis, distance):
    devices = range(lax.axis_size(axis))
    route = [(i - distance, i) for i in devices if i - distance in devices]
    return lax.ppermute(block, axis, route)


def layer_norm(values, gain_vec):
    row_mean = jnp.mean(values, -1, keepdims=True)
    centred = values - row_mean
    variance = jnp.mean(centred * centred, -1, keepdims=True)
    return centred * lax.rsqrt(variance + NORM_EPSILON) * gain_vec


def rotate(values, cosine, sine_table):
    half_width = values.shape[-1] // 2
    turned = jnp.concatenate([-values[..., half_width:], values[..., :half_width]], -1)
    return values * cosine + turned * sine_table


def gated_gelu(expanded):
    hidden_units = expanded.shape[-1] // 2
    return jax.nn.gelu(expanded[:, :hidden_units], approximate=False) * expanded[:, hidden_units:]


def contract_rows(left, right):
    return lax.dot_general(
        left, right, (((0,), (0,)), ((), ())), preferred_element_type=jnp.float32
    )


def contract_cols(left, right):
    return lax.dot_general(
        left, right, (((1,), (1,)), ((), ())), preferred_element_type=jnp.float32
    )


def window_scores(query_low, key_window, allowed):
    raw_scores = jnp.einsum(
        "sqhd,skhd->shqk", query_low, key_window, preferred_element_type=jnp.float32
    ) * HD ** (-0.5)
    return jnp.where(allowed, raw_scores, -1e30)


def shards(tokens, doc_ids, norm_attn, norm_mlp, w_qkv, w_out, w_in, w_down, cotangent):
    streams, block_len, model_width = tokens.shape
    head_count = model_width // HD
    window_len = block_len + 2 * HALF
    token_rows = streams * block_len
    gain_attn, gain_mlp, full_qkv, full_out, full_in, full_down = (
        lax.all_gather(norm_attn, ("dp", "seq"), axis=0, tiled=True),
        lax.all_gather(norm_mlp, ("dp", "seq"), axis=0, tiled=True),
        lax.all_gather(w_qkv, ("dp", "seq"), axis=0, tiled=True),
        lax.all_gather(w_out, ("dp", "seq"), axis=0, tiled=True),
        lax.all_gather(w_in, ("dp", "seq"), axis=0, tiled=True),
        lax.all_gather(w_down, ("dp", "seq"), axis=0, tiled=True),
    )
    block_start = lax.axis_index("seq") * block_len
    tokens_flat = tokens.astype(jnp.float32).reshape(token_rows, model_width)
    normed, norm_back_attn = jax.vjp(layer_norm, tokens_flat, gain_attn.astype(jnp.float32))
    normed_low = normed.astype(jnp.bfloat16)
    joined = jnp.dot(normed_low, full_qkv, preferred_element_type=jnp.float32)
    query_proj = joined[:, :model_width].reshape(streams, block_len, head_count, HD)
    key_proj = joined[:, model_width : 2 * model_width].reshape(streams, block_len, head_count, HD)
    value_low = (
        joined[:, 2 * model_width :]
        .reshape(streams, block_len, head_count, HD)
        .astype(jnp.bfloat16)
    )
    positions = (block_start + jnp.arange(block_len, dtype=jnp.int32)).astype(jnp.float32)
    frequency = ROPE_BASE ** (-(jnp.arange(HD // 2, dtype=jnp.float32) * 2.0 / HD))
    angles = positions[:, None] * frequency[None, :]
    angles = jnp.concatenate([angles, angles], -1)
    cosine = jnp.cos(angles)[:, None, :]
    sine_table = jnp.sin(angles)[:, None, :]

    def rotate_pair(query_in, key_in):
        return (rotate(query_in, cosine, sine_table), rotate(key_in, cosine, sine_table))

    (query_rot, key_rot), rope_back = jax.vjp(rotate_pair, query_proj, key_proj)
    query_low = query_rot.astype(jnp.bfloat16)
    kv_local = jnp.concatenate([key_rot.astype(jnp.bfloat16), value_low], -1).reshape(
        streams, block_len, 2 * model_width
    )
    window = with_halo(kv_local, (("seq", 1),), HALF)
    window = window.reshape(streams, window_len, head_count, 2 * HD)
    key_window = window[..., :HD]
    value_window = window[..., HD:]
    ids_padded = jnp.pad(doc_ids, ((0, 0), (HALF, HALF)), constant_values=-1)
    key_ids = lax.dynamic_slice_in_dim(ids_padded, block_start, window_len, 1)
    query_ids = lax.dynamic_slice_in_dim(doc_ids, block_start, block_len, 1)
    offsets = jnp.arange(window_len)[None, :] - jnp.arange(block_len)[:, None]
    nearby = (offsets >= 0) & (offsets <= 2 * HALF)
    allowed = (nearby[None] & (query_ids[:, :, None] == key_ids[:, None, :]))[:, None]
    scores = window_scores(query_low, key_window, allowed)
    row_peak = jnp.max(scores, -1, keepdims=True)
    log_total = row_peak + jnp.log(jnp.sum(jnp.exp(scores - row_peak), -1, keepdims=True))
    probabilities = jnp.exp(scores - log_total)
    attended = jnp.einsum(
        "shqk,skhd->sqhd",
        probabilities.astype(jnp.bfloat16),
        value_window,
        preferred_element_type=jnp.float32,
    )
    attended_low = attended.reshape(token_rows, model_width).astype(jnp.bfloat16)
    hidden = tokens_flat + jnp.dot(attended_low, full_out, preferred_element_type=jnp.float32)
    normed_mlp, norm_back_mlp = jax.vjp(layer_norm, hidden, gain_mlp.astype(jnp.float32))
    normed_mlp_low = normed_mlp.astype(jnp.bfloat16)
    expanded = jnp.dot(normed_mlp_low, full_in, preferred_element_type=jnp.float32)
    mixed, gelu_back = jax.vjp(gated_gelu, expanded)
    mixed_low = mixed.astype(jnp.bfloat16)
    output = (
        (hidden + contract_cols(mixed_low, full_down))
        .astype(jnp.bfloat16)
        .reshape(streams, block_len, model_width)
    )
    back_qkv, back_out, back_in, back_down = (
        lax.all_gather(w_qkv, ("dp", "seq"), axis=0, tiled=True),
        lax.all_gather(w_out, ("dp", "seq"), axis=0, tiled=True),
        lax.all_gather(w_in, ("dp", "seq"), axis=0, tiled=True),
        lax.all_gather(w_down, ("dp", "seq"), axis=0, tiled=True),
    )
    grad_output = cotangent.reshape(token_rows, model_width)
    grad_mixed = jnp.dot(grad_output, back_down, preferred_element_type=jnp.float32)
    (grad_expanded,) = gelu_back(grad_mixed)
    grad_expanded_low = grad_expanded.astype(jnp.bfloat16)
    grad_normed_mlp = contract_cols(grad_expanded_low, back_in)
    grad_hidden_norm, grad_gain_mlp = norm_back_mlp(grad_normed_mlp)
    grad_hidden = grad_output.astype(jnp.float32) + grad_hidden_norm
    grad_hidden_low = grad_hidden.astype(jnp.bfloat16)
    grad_attended = (
        contract_cols(grad_hidden_low, back_out)
        .reshape(streams, block_len, head_count, HD)
        .astype(jnp.bfloat16)
    )
    scores = window_scores(query_low, key_window, allowed)
    probabilities = jnp.exp(scores - log_total)
    grad_probs = jnp.einsum(
        "sqhd,skhd->shqk", grad_attended, value_window, preferred_element_type=jnp.float32
    )
    row_delta = jnp.sum(probabilities * grad_probs, -1, keepdims=True)
    grad_scores = (probabilities * (grad_probs - row_delta)).astype(jnp.bfloat16)
    grad_query = jnp.einsum(
        "shqk,skhd->sqhd", grad_scores, key_window, preferred_element_type=jnp.float32
    ) * HD ** (-0.5)
    grad_key_window = jnp.einsum(
        "shqk,sqhd->skhd", grad_scores, query_low, preferred_element_type=jnp.float32
    ) * HD ** (-0.5)
    grad_value_window = jnp.einsum(
        "shqk,sqhd->skhd",
        probabilities.astype(jnp.bfloat16),
        grad_attended,
        preferred_element_type=jnp.float32,
    )
    grad_window = jnp.concatenate([grad_key_window, grad_value_window], -1).reshape(
        streams, window_len, 2 * model_width
    )
    from_lower = from_behind(
        grad_window[:, HALF + block_len :].astype(jnp.bfloat16), "seq", 1
    ).astype(jnp.float32)
    from_upper = from_behind(grad_window[:, :HALF].astype(jnp.bfloat16), "seq", -1).astype(
        jnp.float32
    )
    centre = grad_window[:, HALF : HALF + block_len]
    centre = centre + jnp.pad(from_lower, ((0, 0), (0, block_len - HALF), (0, 0)))
    centre = centre + jnp.pad(from_upper, ((0, 0), (block_len - HALF, 0), (0, 0)))
    centre = centre.reshape(streams, block_len, head_count, 2 * HD)
    grad_query_proj, grad_key_proj = rope_back((grad_query, centre[..., :HD]))
    grad_joined = jnp.concatenate(
        [
            grad_query_proj.reshape(token_rows, model_width),
            grad_key_proj.reshape(token_rows, model_width),
            centre[..., HD:].reshape(token_rows, model_width),
        ],
        -1,
    ).astype(jnp.bfloat16)
    grad_normed = contract_cols(grad_joined, back_qkv)
    grad_tokens_norm, grad_gain_attn = norm_back_attn(grad_normed)
    grad_tokens = (grad_hidden + grad_tokens_norm).reshape(streams, block_len, model_width)

    def cut_vec(vector):
        return vector[:, None]

    shares = lax.psum_scatter(
        jnp.concatenate(
            [
                contract_rows(normed_low, grad_joined),
                contract_rows(attended_low, grad_hidden_low),
                contract_rows(normed_mlp_low, grad_expanded_low),
                contract_rows(grad_output, mixed_low),
                cut_vec(grad_gain_attn),
                cut_vec(grad_gain_mlp),
            ],
            -1,
        ),
        ("dp", "seq"),
        scatter_dimension=0,
        tiled=True,
    )
    hidden_units = full_down.shape[1]
    edge_one = 3 * model_width
    edge_two = edge_one + model_width
    edge_three = edge_two + 2 * hidden_units
    edge_four = edge_three + hidden_units
    return (
        output,
        grad_tokens,
        shares[:, edge_four],
        shares[:, edge_four + 1],
        shares[:, :edge_one],
        shares[:, edge_one:edge_two],
        shares[:, edge_two:edge_three],
        shares[:, edge_three:edge_four],
    )


def solution(mesh):
    placed = (
        P("dp", "seq", None),
        P("dp", None),
        P(("dp", "seq")),
        P(("dp", "seq")),
        P(("dp", "seq"), None),
        P(("dp", "seq"), None),
        P(("dp", "seq"), None),
        P(("dp", "seq"), None),
        P("dp", "seq", None),
    )
    return jax.shard_map(
        shards,
        mesh=mesh,
        in_specs=placed,
        out_specs=(
            P("dp", "seq", None),
            P("dp", "seq", None),
            P(("dp", "seq")),
            P(("dp", "seq")),
            P(("dp", "seq"), None),
            P(("dp", "seq"), None),
            P(("dp", "seq"), None),
            P(("dp", "seq"), None),
        ),
        check_vma=False,
    )
```

profile of v0, /device:TPU:0, one launch (start us, length us, event | category | flops | bytes accessed | tf_op | source)
XLA Modules:
  0.0 991.8 jit_solution(2626996023159294267)
XLA Ops:
  11.7 42.3 %all-reduce.11 = (bf16[1024]{0:T(1024)(128)(2,1)S(1)}, bf16[1024]{0:T(1024)(128)(2,1)S(1)}) all-reduce(bf16[1024]{0:T(1024)(128)(2,1)S(1)} %dynamic-update-slice, bf16[1024]{0:T(1024)(128)(2,1)S(1)} %dynamic-update-slice.1), channel_id=1, replica_groups=mesh['dp'=2,'seq'=16] {'dp','seq'}, use_global_device_ids=true, to_apply=%add.9 | all-reduce | flops 2048 | bytes 8192
  58.1 25.2 %all-gather.5.cloned.1.call-done = bf16[1024,3072]{1,0:T(8,128)(2,1)} async-done(((bf16[32,3072]{1,0:T(8,128)(2,1)}), bf16[1024,3072]{1,0:T(8,128)(2,1)}) %all-gather.5.cloned.1.call-update) | async-done | bytes 6291472 | tf_op jit(solution)/shard_map/all_gather | solution.py:78
  83.3 4.6 fusion.56
  91.9 2.7 fusion.50
  96.0 2.8 reshape.252
  98.8 2.3 copy.54
  107.8 4.0 collective-permute-start
  113.7 2.4 copy.60
  116.1 2.4 pad_maximum_fusion.1
  123.4 18.3 %all-gather.7.cloned.1.call-done = bf16[1024,1024]{1,0:T(8,128)(2,1)} async-done(((bf16[32,1024]{1,0:T(8,128)(2,1)}), bf16[1024,1024]{1,0:T(8,128)(2,1)}) %all-gather.7.cloned.1.call-update) | async-done | bytes 2097168 | tf_op jit(solution)/shard_map/all_gather | solution.py:79
  141.7 2.4 fusion.55
  144.4 86.7 %all-gather.9.cloned.1.call-done = bf16[1024,5248]{1,0:T(8,128)(2,1)} async-done(((bf16[32,5248]{1,0:T(8,128)(2,1)}), bf16[1024,5248]{1,0:T(8,128)(2,1)}) %all-gather.9.cloned.1.call-update) | async-done | bytes 10747920 | tf_op jit(solution)/shard_map/all_gather | solution.py:80
  231.2 8.9 fusion.47
  240.1 58.3 %all-gather.11.cloned.1.call-done = bf16[1024,2624]{1,0:T(8,128)(2,1)} async-done(((bf16[32,2624]{1,0:T(8,128)(2,1)}), bf16[1024,2624]{1,0:T(8,128)(2,1)}) %all-gather.11.cloned.1.call-update) | async-done | bytes 5373968 | tf_op jit(solution)/shard_map/all_gather | solution.py:81
  298.5 10.2 %fusion.22 = (f32[256,2624]{1,0:T(8,128)S(1)}, f32[256,2624]{1,0:T(8,128)S(1)}, f32[256,2624]{1,0:T(8,128)S(1)}) fusion(f32[256,5248]{1,0:T(8,128)} %fusion.47, bf16[256,1024]{1,0:T(8,128)(2,1)S(1)} %bitcast.109, bf16[1024,2624]{1,0:T(8,128)(2,1)} %all-gather.11.cloned.1.call-done), kind=kOutput, calls=%fused_computation.72 | convolution fusion | flops 1419395072 | bytes 16646144 | tf_op jit(solution)/shard_map/dot_general | solution.py:149
  308.7 2.6 multiply_add_fusion
  311.3 8.4 multiply_reduce_fusion.1
  320.9 2.6 fusion.24
  328.0 4.8 convolution_bitcast_fusion.1
  332.8 3.1 multiply_reduce_fusion
  336.9 9.1 fusion.29
  347.0 4.3 multiply_convert_fusion
  355.1 2.3 pad_maximum_fusion
  357.4 5.4 copy.74
  362.8 2.3 fusion.53
  365.1 2.6 convert.26
  371.3 5.8 convolution_bitcast_fusion
  378.8 2.9 copy.76
  387.3 6.4 fusion.57
  398.2 57.6 %concatenate.47 = f32[1024,11970]{1,0:T(8,128)} concatenate(f32[1024,3072]{1,0:T(8,128)} %fusion.57, f32[1024,1024]{1,0:T(8,128)} %fusion.24, f32[1024,5248]{1,0:T(8,128)} %fusion.29, f32[1024,2624]{1,0:T(8,128)} %convolution_bitcast_fusion, f32[1024,1]{1,0:T(8,128)} %copy.81, f32[1024,1]{1,0:T(8,128)} %copy.82), dimensions={1} | concatenate | bytes 98058240 | tf_op jit(solution)/shard_map/concatenate | solution.py:210
  455.9 5.6 fusion.10
  462.9 513.6 %reduce-scatter.2.cloned.1.call-done = f32[32,11970]{1,0:T(8,128)} async-done(((f32[1024,11970]{1,0:T(8,128)}), f32[32,11970]{1,0:T(8,128)}) %reduce-scatter.2.cloned.1.call-update) | async-done | bytes 1532176 | tf_op jit(solution)/shard_map/reduce_scatter | solution.py:209
  (164 shorter events, 64.0 us)
Async XLA Ops:
  7.2 76.1 %all-gather.5.cloned.1.call-start = ((), (), s32[]{:S(2)}) async-start(), calls=%async_computation.1 | async-start | bytes 6488064 | tf_op jit(solution)/shard_map/all_gather | solution.py:78
  7.9 133.8 %all-gather.7.cloned.1.call-start = ((), (), s32[]{:S(2)}) async-start(), calls=%async_computation.2 | async-start | bytes 2162688 | tf_op jit(solution)/shard_map/all_gather | solution.py:79
  8.6 222.5 %all-gather.9.cloned.1.call-start = ((), (), s32[]{:S(2)}) async-start(), calls=%async_computation.3 | async-start | bytes 11083776 | tf_op jit(solution)/shard_map/all_gather | solution.py:80
  9.4 289.1 %all-gather.11.cloned.1.call-start = ((), (), s32[]{:S(2)}) async-start(), calls=%async_computation.4 | async-start | bytes 5677056 | tf_op jit(solution)/shard_map/all_gather | solution.py:81
  10.0 966.6 %reduce-scatter.2.cloned.1.call-start = ((), (), s32[]{:S(2)}) async-start(), calls=%async_computation.5 | async-start | bytes 50823168 | tf_op jit(solution)/shard_map/reduce_scatter | solution.py:209
  58.1 29.8 %copy-start.27 = (bf16[256,1024]{1,0:T(8,128)(2,1)}, bf16[256,1024]{1,0:T(8,128)(2,1)S(1)}, u32[]{:S(2)}) copy-start(bf16[256,1024]{1,0:T(8,128)(2,1)S(1)} %multiply_convert_fusion.3) | copy-start | bytes 1572868
  101.9 16.6 %copy-start.16 = (bf16[2,128,16,64]{1,3,2,0:T(8,128)(2,1)}, bf16[2,128,16,64]{1,3,2,0:T(8,128)(2,1)S(1)}, u32[]{:S(2)}) copy-start(bf16[2,128,16,64]{1,3,2,0:T(8,128)(2,1)S(1)} %get-tuple-element.36) | copy-start | bytes 1572868
  102.5 9.4 copy-start.31
  105.4 10.7 %copy-start.19 = (bf16[2,128,16,64]{1,3,2,0:T(8,128)(2,1)S(1)}, bf16[2,128,16,64]{1,3,2,0:T(8,128)(2,1)}, u32[]{:S(2)}) copy-start(bf16[2,128,16,64]{1,3,2,0:T(8,128)(2,1)} %copy-done.18) | copy-start | bytes 1572868
  106.5 5.6 collective-permute-start.1
  107.8 5.9 collective-permute-start
  118.5 3.0 copy-start.4
  119.7 3.2 copy-start
  121.5 20.3 %copy-start.3 = (bf16[2,128,1024]{2,1,0:T(8,128)(2,1)S(1)}, bf16[2,128,1024]{2,1,0:T(8,128)(2,1)}, u32[]{:S(2)}) copy-start(bf16[2,128,1024]{2,1,0:T(8,128)(2,1)} %param.9) | copy-start | bytes 1572868
  144.4 154.0 %copy-start.12 = (bf16[2,128,1024]{2,1,0:T(8,128)(2,1)S(1)}, bf16[2,128,1024]{2,1,0:T(8,128)(2,1)}, u32[]{:S(2)}) copy-start(bf16[2,128,1024]{2,1,0:T(8,128)(2,1)} %param.17) | copy-start | bytes 1572868
  298.5 10.2 %slice-start = ((s8[5373952]{0:T(1024)(128)(4,1)}), s8[4194304]{0:T(1024)(128)(4,1)S(1)}, s32[]{:S(2)}) async-start(s8[5373952]{0:T(1024)(128)(4,1)} %bitcast.99), calls=%async_computation.6 | async-start | bytes 8388608
  298.5 10.2 %slice-start.1 = ((s8[5373952]{0:T(1024)(128)(4,1)}), s8[1179648]{0:T(1024)(128)(4,1)S(1)}, s32[]{:S(2)}) async-start(s8[5373952]{0:T(1024)(128)(4,1)} %bitcast.99), calls=%async_computation.7 | async-start | bytes 2359296
  311.3 8.4 copy-start.7
  328.0 4.8 copy-start.1
  328.0 4.8 copy-start.5
  332.8 3.1 copy-start.8
  332.8 4.1 copy-start.24
  347.0 4.3 copy-start.17
  351.8 3.3 copy-start.10
  365.1 6.2 copy-start.11
  365.1 6.2 copy-start.14
  367.8 9.4 collective-permute-start.2
  370.0 7.1 collective-permute-start.3
  371.3 5.8 copy-start.2
  386.5 7.2 slice-start.2
  387.3 6.4 slice-start.3
  455.9 5.6 copy-start.21
  (13 other events, 24.0 us)
Sparse Core Ops, SparseCore 0:
  10.9 72.3 all-gather.4
  86.1 55.5 all-gather.6
  144.6 86.5 all-gather.8
  233.9 64.5 all-gather.10
  456.0 520.5 reduce-scatter.1
where the time goes:
time: 1010 us; the launch traced here: 992 us
  waiting for transfers between devices  705 us (70%)
  local copies, waits for them, and re-layouts  111 us (11%)
  matrix products  79.7 us (8%)
  blocking collectives  42.3 us (4%)
  other arithmetic  29.8 us (3%)
  between operations  14.7 us (1%)
    reduce_scatter x1, waiting for transfers between devices, shards(): lax.psum_scatter(jnp.concatenate([contract_rows(normed_low, grad_joined),...  514 us
    all_gather x1, waiting for transfers between devices, shards(): lax.all_gather(w_in, ('dp', 'seq'), axis=0, tiled=True)  86.7 us
    all_gather x1, waiting for transfers between devices, shards(): lax.all_gather(w_down, ('dp', 'seq'), axis=0, tiled=True)  58.3 us
    concatenate x1, local copies, waits for them, and re-layouts, shards(): jnp.concatenate([contract_rows(normed_low, grad_joined), contract_rows(at...  57.6 us
    unnamed x1, blocking collectives  42.3 us
    all_gather x1, waiting for transfers between devices, shards(): lax.all_gather(w_qkv, ('dp', 'seq'), axis=0, tiled=True)  25.2 us
    dot_general x4, matrix products, contract_rows(): lax.dot_general(left, right, (((0,), (0,)), ((), ())), preferred_element_...  23.9 us
  transfers between devices with their start and end apart: 9, of which 5 were waited for; matrix products, arithmetic and copies ran while one was open for 6% of the time, Pallas kernels for 0%

commit v1 on v0

v1 whole, which is shorter than its diff:
```python
import functools

import jax
import jax.numpy as jnp
from jax import lax
from jax.experimental import pallas as pl
from jax.experimental.pallas import tpu as pltpu
from jax.sharding import Mesh, PartitionSpec as P

HD = 64
HALF = 64
LANES = 128
NORM_EPSILON = 1e-05
ROPE_BASE = 10000.0
CHIPS = ("dp", "outer", "inner")
F32 = jnp.float32
BF16 = jnp.bfloat16


def contract_cols(left, right):
    return lax.dot_general(left, right, (((1,), (1,)), ((), ())), preferred_element_type=F32)


def contract_rows(left, right):
    return lax.dot_general(left, right, (((0,), (0,)), ((), ())), preferred_element_type=F32)


def matmul(left, right):
    return jnp.dot(left, right, preferred_element_type=F32)


def swap(value):
    return lax.ppermute(value, "core", [(0, 1), (1, 0)])


def ordered(mine, other, axis):
    first = lax.axis_index("core") == 0
    return jnp.concatenate(
        [jnp.where(first, mine, other), jnp.where(first, other, mine)], axis=axis
    )


def normalise(values):
    centred = values - jnp.mean(values, -1, keepdims=True)
    scale = lax.rsqrt(jnp.mean(centred * centred, -1, keepdims=True) + NORM_EPSILON)
    return centred * scale, scale


def norm_back(unit, scale, gain, incoming):
    grad = incoming * gain
    return scale * (
        grad
        - jnp.mean(grad, -1, keepdims=True)
        - unit * jnp.mean(grad * unit, -1, keepdims=True)
    )


def turned(values):
    width = values.shape[-1]
    lane = lax.broadcasted_iota(jnp.int32, values.shape, values.ndim - 1)
    ahead = pltpu.roll(values, width - HD // 2, values.ndim - 1)
    behind = pltpu.roll(values, HD // 2, values.ndim - 1)
    return jnp.where(lane % HD < HD // 2, ahead, behind)


def project_kernel(rotated_tiles, normed_ref, weight_ref, cos_ref, sin_ref, out_ref):
    values = matmul(normed_ref[...], weight_ref[...])
    rotated = values * cos_ref[...] + turned(values) * sin_ref[...]
    keep = pl.program_id(0) >= rotated_tiles
    out_ref[...] = jnp.where(keep, values, rotated).astype(BF16)


def project(normed, weight, cosine, sine, columns):
    rows, depth = normed.shape
    tile = cosine.shape[1]
    return pl.pallas_call(
        functools.partial(project_kernel, 2 * columns // 3 // tile),
        grid=(columns // tile,),
        in_specs=[
            pl.BlockSpec((rows, depth), lambda j: (0, 0)),
            pl.BlockSpec((depth, tile), lambda j: (0, j)),
            pl.BlockSpec((rows, tile), lambda j: (0, 0)),
            pl.BlockSpec((rows, tile), lambda j: (0, 0)),
        ],
        out_specs=pl.BlockSpec((rows, tile), lambda j: (0, j)),
        out_shape=jax.ShapeDtypeStruct((rows, columns), BF16),
        compiler_params=pltpu.CompilerParams(vmem_limit_bytes=24 * 2**20),
        cost_estimate=pl.CostEstimate(
            flops=2 * rows * depth * columns,
            bytes_accessed=2 * (rows * depth + depth * columns + rows * columns),
            transcendentals=0,
        ),
    )(normed, weight, cosine, sine)


def head_masks():
    lane = lax.broadcasted_iota(jnp.int32, (1, LANES), 1)
    return [(lane // HD == head).astype(F32).astype(BF16) for head in range(LANES // HD)]


def block_mask(query_ids, key_ids):
    rows, width = query_ids.shape[0], key_ids.shape[1]
    offset = lax.broadcasted_iota(jnp.int32, (rows, width), 1) - lax.broadcasted_iota(
        jnp.int32, (rows, width), 0
    )
    return (offset >= 0) & (offset <= 2 * HALF) & (query_ids == key_ids)


def block_probs(query, keys, allowed):
    scores = jnp.where(allowed, contract_cols(query, keys) * HD**-0.5, -1e30)
    grown = jnp.exp(scores - jnp.max(scores, -1, keepdims=True))
    return grown / jnp.sum(grown, -1, keepdims=True)


def attend_kernel(block, q_ref, k_ref, v_ref, kl_ref, vl_ref, kh_ref, vh_ref, qid_ref, kid_ref, out_ref):
    keys = jnp.concatenate([kl_ref[0], k_ref[0], kh_ref[0]], 0)
    values = jnp.concatenate([vl_ref[0], v_ref[0], vh_ref[0]], 0)
    masks = head_masks()
    for start in range(0, q_ref.shape[1], block):
        span = slice(start, start + block + 2 * HALF)
        allowed = block_mask(qid_ref[0, start : start + block], kid_ref[0, :, span])
        query = q_ref[0, start : start + block]
        total = None
        for mask in masks:
            probs = block_probs(query * mask, keys[span], allowed)
            part = matmul(probs.astype(BF16), values[span]) * mask.astype(F32)
            total = part if total is None else total + part
        out_ref[0, start : start + block] = total.astype(BF16)


def attend_back_kernel(
    block, q_ref, k_ref, v_ref, kl_ref, vl_ref, kh_ref, vh_ref, qid_ref, kid_ref,
    grad_ref, cos_ref, sin_ref, dq_ref, mid_ref, low_ref, high_ref,
):
    keys = jnp.concatenate([kl_ref[0], k_ref[0], kh_ref[0]], 0)
    values = jnp.concatenate([vl_ref[0], v_ref[0], vh_ref[0]], 0)
    masks = head_masks()
    length = q_ref.shape[1]
    window = jnp.zeros((length + 2 * HALF, LANES), F32)
    grad_keys, grad_values = window, window
    for start in range(0, length, block):
        span = slice(start, start + block + 2 * HALF)
        allowed = block_mask(qid_ref[0, start : start + block], kid_ref[0, :, span])
        query_all = q_ref[0, start : start + block]
        grad_all = grad_ref[0, start : start + block]
        grad_query, part_keys, part_values = 0.0, 0.0, 0.0
        for mask in masks:
            query, grad = query_all * mask, grad_all * mask
            probs = block_probs(query, keys[span], allowed)
            grad_probs = contract_cols(grad, values[span])
            delta = jnp.sum(probs * grad_probs, -1, keepdims=True)
            grad_scores = (probs * (grad_probs - delta)).astype(BF16)
            grad_query += matmul(grad_scores, keys[span]) * mask.astype(F32)
            part_keys += contract_rows(grad_scores, query)
            part_values += contract_rows(probs.astype(BF16), grad)
        grad_query = grad_query * HD**-0.5
        rows = slice(start, start + block)
        dq_ref[0, rows] = (
            grad_query * cos_ref[rows] - turned(grad_query) * sin_ref[rows]
        ).astype(BF16)
        before, after = start, length - start - block

        def placed(part):
            pieces = [part]
            if before:
                pieces.insert(0, jnp.zeros((before, LANES), F32))
            if after:
                pieces.append(jnp.zeros((after, LANES), F32))
            return jnp.concatenate(pieces, 0)

        grad_keys += placed(part_keys)
        grad_values += placed(part_values)
    for index, total in enumerate((grad_keys * HD**-0.5, grad_values)):
        low_ref[0, index] = total[:HALF].astype(BF16)
        mid_ref[0, index] = total[HALF : HALF + length]
        high_ref[0, index] = total[HALF + length :].astype(BF16)


def attention_specs(length, groups):
    def at(rows, shift):
        return pl.BlockSpec((1, rows, LANES), lambda s, h: (s, 0, h + shift))

    return [
        at(length, 0),
        at(length, groups),
        at(length, 2 * groups),
        at(HALF, 0),
        at(HALF, groups),
        at(HALF, 0),
        at(HALF, groups),
        pl.BlockSpec((1, length, 1), lambda s, h: (s, 0, 0)),
        pl.BlockSpec((1, 1, length + 2 * HALF), lambda s, h: (s, 0, 0)),
    ]


def attend(block, joined, low, high, query_ids, key_ids):
    streams, length, columns = joined.shape
    groups = columns // 3 // LANES
    work = streams * groups * 2 * length * (block + 2 * HALF)
    return pl.pallas_call(
        functools.partial(attend_kernel, block),
        grid=(streams, groups),
        in_specs=attention_specs(length, groups),
        out_specs=pl.BlockSpec((1, length, LANES), lambda s, h: (s, 0, h)),
        out_shape=jax.ShapeDtypeStruct((streams, length, columns // 3), BF16),
        compiler_params=pltpu.CompilerParams(vmem_limit_bytes=24 * 2**20),
        cost_estimate=pl.CostEstimate(
            flops=4 * work * LANES, bytes_accessed=4 * joined.size, transcendentals=work
        ),
    )(joined, joined, joined, low, low, high, high, query_ids, key_ids)


def attend_back(block, joined, low, high, query_ids, key_ids, grad, cosine, sine):
    streams, length, columns = joined.shape
    groups = columns // 3 // LANES
    work = streams * groups * 2 * length * (block + 2 * HALF)

    def pair(rows):
        return pl.BlockSpec((1, 2, rows, LANES), lambda s, h: (s, 0, 0, h))

    def shape(rows, kind):
        return jax.ShapeDtypeStruct((streams, 2, rows, columns // 3), kind)

    return pl.pallas_call(
        functools.partial(attend_back_kernel, block),
        grid=(streams, groups),
        in_specs=attention_specs(length, groups)
        + [pl.BlockSpec((1, length, LANES), lambda s, h: (s, 0, h))]
        + [pl.BlockSpec((length, LANES), lambda s, h: (0, 0))] * 2,
        out_specs=[
            pl.BlockSpec((1, length, LANES), lambda s, h: (s, 0, h)),
            pair(length),
            pair(HALF),
            pair(HALF),
        ],
        out_shape=[
            jax.ShapeDtypeStruct((streams, length, columns // 3), BF16),
            shape(length, F32),
            shape(HALF, BF16),
            shape(HALF, BF16),
        ],
        compiler_params=pltpu.CompilerParams(vmem_limit_bytes=24 * 2**20),
        cost_estimate=pl.CostEstimate(
            flops=10 * work * LANES, bytes_accessed=8 * joined.size, transcendentals=work
        ),
    )(joined, joined, joined, low, low, high, high, query_ids, key_ids, grad, cosine, sine)


def join_kernel(dq_ref, mid_ref, low_ref, high_ref, cos_ref, sin_ref, out_ref):
    length, width = dq_ref.shape[1:]
    out_ref[0, :, :width] = dq_ref[0]
    cosine, sine = cos_ref[...], sin_ref[...]
    for index in range(2):
        for start in range(0, width, LANES):
            lanes = slice(start, start + LANES)
            total = mid_ref[0, index, :, lanes]
            total = total + jnp.concatenate(
                [
                    low_ref[0, index, :, lanes].astype(F32),
                    jnp.zeros((length - 2 * HALF, LANES), F32),
                    high_ref[0, index, :, lanes].astype(F32),
                ],
                0,
            )
            if index == 0:
                total = total * cosine - turned(total) * sine
            to = (1 + index) * width + start
            out_ref[0, :, to : to + LANES] = total.astype(BF16)


def join_grads(grad_query, mid, from_lower, from_upper, cosine, sine):
    streams, length, width = grad_query.shape
    return pl.pallas_call(
        join_kernel,
        grid=(streams,),
        in_specs=[
            pl.BlockSpec((1, length, width), lambda s: (s, 0, 0)),
            pl.BlockSpec((1, 2, length, width), lambda s: (s, 0, 0, 0)),
            pl.BlockSpec((1, 2, HALF, width), lambda s: (s, 0, 0, 0)),
            pl.BlockSpec((1, 2, HALF, width), lambda s: (s, 0, 0, 0)),
            pl.BlockSpec((length, LANES), lambda s: (0, 0)),
            pl.BlockSpec((length, LANES), lambda s: (0, 0)),
        ],
        out_specs=pl.BlockSpec((1, length, 3 * width), lambda s: (s, 0, 0)),
        out_shape=jax.ShapeDtypeStruct((streams, length, 3 * width), BF16),
        compiler_params=pltpu.CompilerParams(vmem_limit_bytes=24 * 2**20),
        cost_estimate=pl.CostEstimate(
            flops=8 * mid.size, bytes_accessed=8 * mid.size, transcendentals=0
        ),
    )(grad_query, mid, from_lower, from_upper, cosine, sine)


def chunk_kernel(pairs, picks_ref, *refs):
    lefts, rights, rest = refs[:pairs], refs[pairs : 2 * pairs], refs[2 * pairs :]
    adds, out_ref = rest[:-1], rest[-1]
    start = 0
    for left, right in zip(lefts, rights):
        columns = slice(start, start + right.shape[1])
        total = matmul(left[0, 0, 0], right[...])
        for add in adds:
            total = total + add[0, :, columns].astype(F32)
        out_ref[0, :, columns] = total.astype(BF16)
        start = columns.stop


def grad_chunks(lefts, rights, picks, adds):
    rows, depth = lefts[0].shape[3:]
    columns = sum(right.shape[1] for right in rights)
    fields = 3 + len(adds)
    table = [
        jnp.asarray(entry, jnp.int32)
        for index, pick in enumerate(picks)
        for entry in list(pick) + [where[index] for _, where in adds]
    ]
    count = len(picks)

    def left_at(i, table):
        return (table[i * fields], table[i * fields + 1], table[i * fields + 2], 0, 0)

    def add_at(position):
        return lambda i, table: (table[i * fields + 3 + position], 0, 0)

    return pl.pallas_call(
        functools.partial(chunk_kernel, len(lefts)),
        grid_spec=pltpu.PrefetchScalarGridSpec(
            num_scalar_prefetch=1,
            grid=(count,),
            in_specs=[pl.BlockSpec((1, 1, 1, rows, depth), left_at) for _ in lefts]
            + [pl.BlockSpec(right.shape, lambda i, table: (0, 0)) for right in rights]
            + [pl.BlockSpec((1, rows, columns), add_at(n)) for n in range(len(adds))],
            out_specs=pl.BlockSpec((1, rows, columns), lambda i, table: (i, 0, 0)),
        ),
        out_shape=jax.ShapeDtypeStruct((count, rows, columns), BF16),
        compiler_params=pltpu.CompilerParams(vmem_limit_bytes=40 * 2**20),
        cost_estimate=pl.CostEstimate(
            flops=2 * count * rows * depth * columns,
            bytes_accessed=2 * (depth * columns + (1 + len(adds)) * count * rows * columns),
            transcendentals=0,
        ),
    )(jnp.stack(table), *lefts, *rights, *[array for array, _ in adds])


def ring(axis, chunk):
    count, me = lax.axis_size(axis), lax.axis_index(axis)
    arrived = None
    for step in range(1, count):
        arrived = lax.ppermute(
            chunk((me + count - step) % count, arrived),
            axis,
            [(i, (i + 1) % count) for i in range(count)],
        )
    return arrived


def with_adds(*adds):
    return [add for add in adds if add[0] is not None]


def scatter_grads(lefts, rights):
    inner, outer, dp = (lax.axis_size(name) for name in ("inner", "outer", "dp"))
    x, z, y = (lax.axis_index(name) for name in ("inner", "outer", "dp"))
    chunks = functools.partial(grad_chunks, lefts, rights)
    all_x, all_y = list(range(inner)), list(range(dp))
    a_one = ring(
        "inner",
        lambda t, got: chunks([(t, i, 0) for i in all_y], with_adds((got, all_y))),
    )
    b_one = ring(
        "dp",
        lambda t, got: chunks([(i, t, 1) for i in all_x], with_adds((got, all_x))),
    )
    a_two = ring(
        "dp", lambda t, got: chunks([(x, t, 0)], with_adds((a_one, [t]), (got, [0])))
    )
    b_two = ring(
        "inner", lambda t, got: chunks([(t, y, 1)], with_adds((b_one, [t]), (got, [0])))
    )
    mine = [
        chunks([(x, y, 0)], with_adds((a_one, [y]), (a_two, [0]))),
        chunks([(x, y, 1)], with_adds((b_one, [x]), (b_two, [0]))),
    ]
    mine = [part.reshape(outer, -1, part.shape[-1]) for part in mine]

    def part(target):
        return jnp.stack(
            [lax.dynamic_index_in_dim(half, target, 0, keepdims=False) for half in mine]
        ).astype(F32)

    up = down = jnp.zeros((), F32)
    for step in range(1, outer):
        up = lax.ppermute(
            (part(jnp.clip(z + outer - step, 0, outer - 1)) + up).astype(BF16),
            "outer",
            [(i, i + 1) for i in range(step)],
        ).astype(F32)
        down = lax.ppermute(
            (part(jnp.clip(z - outer + step, 0, outer - 1)) + down).astype(BF16),
            "outer",
            [(outer - 1 - i, outer - 2 - i) for i in range(step)],
        ).astype(F32)
    return part(z) + up + down


def both_halves(total):
    core = lax.axis_index("core")
    mine = lax.dynamic_index_in_dim(total, core, 0, keepdims=False)
    other = swap(lax.dynamic_index_in_dim(total, 1 - core, 0, keepdims=False))
    return (
        jnp.where(core == 0, mine, other),
        jnp.where(core == 0, other, mine),
    )


def shards(tokens, doc_ids, norm_attn, norm_mlp, w_qkv, w_out, w_in, w_down, cotangent):
    streams, block, width = tokens.shape
    shard_rows = w_qkv.shape[0]
    inner, outer, dp = (lax.axis_size(name) for name in ("inner", "outer", "dp"))
    core = lax.axis_index("core")
    length = 2 * block
    rows = streams * length
    side = width // 2
    units = w_down.shape[1] // 2
    padded = -(-units // LANES) * LANES

    def halves(weight, parts, pad):
        size = weight.shape[1] // (2 * parts)
        cut = [weight[:, i * size : (i + 1) * size] for i in range(2 * parts)]
        if pad != size:
            cut = [jnp.pad(piece, ((0, 0), (0, pad - size))) for piece in cut]
        return cut[0::2], cut[1::2]

    def spread(pieces):
        low = jnp.concatenate([piece for one, _ in pieces for piece in one], 1)
        high = jnp.concatenate([piece for _, two in pieces for piece in two], 1)
        mine = jnp.where(core == 0, low, high)
        other = swap(jnp.where(core == 0, high, low))
        return lax.all_gather(ordered(mine, other, 0), CHIPS, axis=0, tiled=True)

    gains = jnp.pad(jnp.stack([norm_attn, norm_mlp], 1), ((0, 0), (0, LANES - 2)))
    first = spread([halves(w_qkv, 3, side), ([gains], [gains])])
    second = spread(
        [halves(w_out, 1, side), halves(w_in, 2, padded), halves(w_down, 1, padded)]
    )

    def both_blocks(value):
        return ordered(value, swap(value), 1).reshape(rows, width)

    tokens_low = both_blocks(tokens)
    grad_output = both_blocks(cotangent)

    gain_attn, gain_mlp = (first[:, 3 * side + i].astype(F32) for i in range(2))

    chip = lax.axis_index(("outer", "inner"))
    chips = outer * inner
    start = chip * length
    positions = (start + jnp.arange(length, dtype=jnp.int32)).astype(F32)
    frequency = ROPE_BASE ** (-(jnp.arange(HD // 2, dtype=F32) * 2.0 / HD))
    angles = positions[:, None] * frequency[None, :]
    cosine, sine = jnp.cos(angles), jnp.sin(angles)
    cosine = jnp.tile(cosine, (1, LANES // (HD // 2)))
    sine = jnp.tile(jnp.concatenate([-sine, sine], 1), (1, LANES // HD))
    wide_cosine, wide_sine = (jnp.tile(table, (streams, 2)) for table in (cosine, sine))

    values = tokens_low.astype(F32)
    unit_attn, scale_attn = normalise(values)
    normed_low = (unit_attn * gain_attn).astype(BF16)
    joined = project(normed_low, first, wide_cosine, wide_sine, 3 * side)
    joined = joined.reshape(streams, length, 3 * side)
    onward = [(i, i + 1) for i in range(chips - 1)]
    back = [(i + 1, i) for i in range(chips - 1)]
    low = lax.ppermute(joined[:, length - HALF :, side:], ("outer", "inner"), onward)
    high = lax.ppermute(joined[:, :HALF, side:], ("outer", "inner"), back)
    ids_padded = jnp.pad(doc_ids, ((0, 0), (HALF, HALF)), constant_values=-1)
    key_ids = lax.dynamic_slice_in_dim(ids_padded, start, length + 2 * HALF, 1)[:, None, :]
    query_ids = lax.dynamic_slice_in_dim(doc_ids, start, length, 1)[:, :, None]
    attended_half = attend(block, joined, low, high, query_ids, key_ids).reshape(rows, side)
    attended_low = ordered(attended_half, swap(attended_half), 1)
    out_half = second[:, :side]
    full_out = ordered(out_half, swap(out_half), 1)
    hidden = values + matmul(attended_low, full_out)
    unit_mlp, scale_mlp = normalise(hidden)
    normed_mlp_low = (unit_mlp * gain_mlp).astype(BF16)
    in_half = second[:, side : side + 2 * padded]
    down_half = second[:, side + 2 * padded :]
    expanded = matmul(normed_mlp_low, in_half)
    gate, up = expanded[:, :padded], expanded[:, padded:]
    below = 0.5 * (1.0 + lax.erf(gate * 0.5**0.5))
    active = gate * below
    mixed_low = (active * up).astype(BF16)

    grad_mixed = matmul(grad_output, down_half)
    density = jnp.exp(-0.5 * gate * gate) * (2.0 * jnp.pi) ** -0.5
    grad_expanded_low = jnp.concatenate(
        [
            (grad_mixed * up * (below + gate * density)).astype(BF16),
            (grad_mixed * active).astype(BF16),
        ],
        1,
    )

    def own_rows(value):
        value = value.reshape(streams, 2, block, width)
        mine = lax.dynamic_index_in_dim(value, core, 1, keepdims=False)
        other = lax.dynamic_index_in_dim(value, 1 - core, 1, keepdims=False)
        return mine, other

    def summed_rows(partial):
        mine, other = own_rows(partial)
        return mine + swap(other.astype(BF16)).astype(F32)

    output = (own_rows(hidden)[0] + summed_rows(contract_cols(mixed_low, down_half))).astype(BF16)

    def by_chunk(activations):
        cut = activations.reshape(rows, dp, outer, inner, 2, shard_rows)
        return cut.transpose(3, 1, 4, 2, 5, 0).reshape(inner, dp, 2, outer * shard_rows, rows)

    mlp_total = scatter_grads(
        [by_chunk(grad_output), by_chunk(normed_mlp_low)], [mixed_low, grad_expanded_low]
    )

    grad_normed_mlp = contract_cols(grad_expanded_low, in_half)
    grad_normed_mlp = grad_normed_mlp + swap(grad_normed_mlp.astype(BF16)).astype(F32)
    grad_hidden = grad_output.astype(F32) + norm_back(
        unit_mlp, scale_mlp, gain_mlp, grad_normed_mlp
    )
    grad_hidden_low = grad_hidden.astype(BF16)

    out_rows = lax.dynamic_slice_in_dim(full_out, core * side, side, 0)
    grad_attended = contract_cols(grad_hidden_low, out_rows).astype(BF16)
    grad_query, mid, to_lower, to_upper = attend_back(
        block, joined, low, high, query_ids, key_ids,
        grad_attended.reshape(streams, length, side), cosine, sine,
    )
    from_lower = lax.ppermute(to_upper, ("outer", "inner"), onward)
    from_upper = lax.ppermute(to_lower, ("outer", "inner"), back)
    grad_joined = join_grads(grad_query, mid, from_lower, from_upper, cosine, sine)
    grad_joined = grad_joined.reshape(rows, 3 * side)
    hidden_side = lax.dynamic_slice_in_dim(grad_hidden_low, core * side, side, 1)
    attn_total = scatter_grads(
        [by_chunk(normed_low), by_chunk(attended_low)], [grad_joined, hidden_side]
    )
    grad_normed = summed_rows(contract_cols(grad_joined, first[:, : 3 * side]))
    unit_mine, scale_mine = normalise(tokens.astype(F32))
    grad_tokens = own_rows(grad_hidden)[0] + norm_back(
        unit_mine, scale_mine, gain_attn, grad_normed
    )

    def interleaved(pair, start, parts, stride, size):
        cuts = []
        for i in range(parts):
            first_column = start + i * stride
            cuts += [half[:, first_column : first_column + size] for half in pair]
        return jnp.concatenate(cuts, 1)

    pair = both_halves(mlp_total)
    grad_down = interleaved(pair, 0, 1, padded, units)
    grad_in = interleaved(pair, padded, 2, padded, units)
    pair = both_halves(attn_total)
    grad_qkv = interleaved(pair, 0, 3, side, side)
    grad_out = interleaved(pair, 3 * side, 1, side, side)

    def gain_grad(weight, grad, gain):
        return jnp.sum(weight.astype(F32) * grad, -1) / gain.astype(F32)

    return (
        output,
        grad_tokens,
        gain_grad(w_qkv, grad_qkv, norm_attn),
        gain_grad(w_in, grad_in, norm_mlp),
        grad_qkv,
        grad_out,
        grad_in,
        grad_down,
    )


def solution(mesh):
    dp, seq = mesh.shape["dp"], mesh.shape["seq"]
    chips = seq // 2
    outer = 4 if chips % 4 == 0 else 1
    fine = Mesh(
        mesh.devices.reshape(dp, outer, chips // outer, 2), ("dp", "outer", "inner", "core")
    )
    line = ("outer", "inner", "core")
    every = ("dp",) + line
    token = P("dp", line, None)
    vector = P(every)
    matrix = P(every, None)
    return jax.shard_map(
        shards,
        mesh=fine,
        in_specs=(token, P("dp", None), vector, vector, matrix, matrix, matrix, matrix, token),
        out_specs=(token, token, vector, vector, matrix, matrix, matrix, matrix),
        check_vma=False,
    )
```

time: 1010 us -> 507 us (0.50); the launches traced: 992 us -> 505 us
  waiting for transfers between devices: 705 us -> 287 us
  local copies, waits for them, and re-layouts: 111 us -> 42.7 us
  matrix products: 79.7 us -> 19.5 us
  Pallas kernels: 0 us -> 55.4 us
  starting transfers between devices: 9.01 us -> 53.9 us
  blocking collectives: 42.3 us -> 0 us
    reduce_scatter x1 -> x0, waiting for transfers between devices: 514 us -> none  [shards(): lax.psum_scatter(jnp.concatenate([contract_rows(normed_low, grad_joined),...]
    ppermute x4 -> x35, waiting for transfers between devices: 0.01 us -> 104 us  [the longest x8 68.4 us: ring(): lax.ppermute(chunk((me + count - step) % count, arrived), axis, [(i, (i +...]
    pallas_call x0 -> x16, Pallas kernels: none -> 55.4 us  [the longest x12 25.6 us: grad_chunks(): pl.pallas_call(functools.partial(chunk_kernel, len(lefts)), grid_spec=plt...]
    concatenate x2, local copies, waits for them, and re-layouts: 57.7 us -> 2.44 us  [the longest x1 2.16 us: ordered(): jnp.concatenate([jnp.where(first, mine, other), jnp.where(first, other, m...]
    dot_general x14 -> x3, matrix products: 63.1 us -> 12 us  [matmul(): return jnp.dot(left, right, preferred_element_type=F32)]
    ppermute x4 -> x35, starting transfers between devices: 8.82 us -> 53.9 us  [the longest x6 27.1 us: scatter_grads(): lax.ppermute((part(jnp.clip(z + outer - step, 0, outer - 1)) + up).astype...]
    unnamed x1 -> x0, blocking collectives: 42.3 us -> none
    reshape x5 -> x1, local copies, waits for them, and re-layouts: 11.9 us -> 1 us  [shards(): attend(block, joined, low, high, query_ids, key_ids).reshape(rows, side)]
  transfers between devices with their start and end apart: 9 -> 37, of which waited for: 5 -> 15; matrix products, arithmetic and copies ran while one was open for 6% -> 10% of each run, Pallas kernels for 0% -> 8%
where the time goes in v1:
time: 507 us; the launch traced here: 505 us
  waiting for transfers between devices  287 us (57%)
  Pallas kernels  55.4 us (11%)
  starting transfers between devices  53.9 us (11%)
  local copies, waits for them, and re-layouts  42.7 us (8%)
  other arithmetic  31.1 us (6%)
  matrix products  19.5 us (4%)
  between operations  15.5 us (3%)
    all_gather x2, waiting for transfers between devices, spread(): return lax.all_gather(ordered(mine, other, 0), CHIPS, axis=0, tiled=True)  183 us
    ppermute x8, waiting for transfers between devices, ring(): lax.ppermute(chunk((me + count - step) % count, arrived), axis, [(i, (i +...  68.4 us
    ppermute x6, starting transfers between devices, scatter_grads(): lax.ppermute((part(jnp.clip(z + outer - step, 0, outer - 1)) + up).astype...  27.1 us
    pallas_call x12, Pallas kernels, grad_chunks(): pl.pallas_call(functools.partial(chunk_kernel, len(lefts)), grid_spec=plt...  25.6 us
    ppermute x6, waiting for transfers between devices, scatter_grads(): lax.ppermute((part(jnp.clip(z + outer - step, 0, outer - 1)) + up).astype...  22.8 us
    pallas_call x1, Pallas kernels, attend_back(): pl.pallas_call(functools.partial(attend_back_kernel, block), grid=(stream...  15.3 us
    unnamed x144, local copies, waits for them, and re-layouts  14.5 us
    dot_general x3, matrix products, matmul(): return jnp.dot(left, right, preferred_element_type=F32)  12 us
  transfers between devices with their start and end apart: 37, of which 15 were waited for; matrix products, arithmetic and copies ran while one was open for 10% of the time, Pallas kernels for 8%

profile of v1, /device:TPU:0, one launch (start us, length us, event | category | flops | bytes accessed | tf_op | source)
XLA Modules:
  0.0 505.2 jit_solution(1241666411021991641)
XLA Ops:
  20.3 64.1 %all-gather.3.cloned.1.call-done.weight_ref = bf16[1024,1664]{1,0:T(8,128)(2,1)} async-done(((bf16[64,1664]{1,0:T(8,128)(2,1)}), bf16[1024,1664]{1,0:T(8,128)(2,1)}) %all-gather.3.cloned.1.call-update) | async-done | bytes 3407888 | tf_op jit(solution)/shard_map/all_gather | solution.py:437
  88.7 4.3 shard_map.152
  93.1 3.5 collective-permute-start.2
  99.5 118.8 %all-gather.5.cloned.1.call-done = bf16[1024,4736]{1,0:T(8,128)(2,1)} async-done(((bf16[64,4736]{1,0:T(8,128)(2,1)}), bf16[1024,4736]{1,0:T(8,128)(2,1)}) %all-gather.5.cloned.1.call-update) | async-done | bytes 9699344 | tf_op jit(solution)/shard_map/all_gather | solution.py:437
  222.1 8.2 %shard_map.153 = bf16[2,256,512]{2,1,0:T(8,128)(2,1)S(1)} custom-call(bf16[2,256,1536]{2,1,0:T(8,128)(2,1)S(1)} %bitcast.114, bf16[2,256,1536]{2,1,0:T(8,128)(2,1)S(1)} %bitcast.115, bf16[2,256,1536]{2,1,0:T(8,128)(2,1)S(1)} %bitcast.116, bf16[2,64,1024]{2,1,0:T(8,128)(2,1)S(1)} %collective-permute-done.2.kl_ref.vl_ref, ...), custom_call_target="tpu_custom_call" | custom-call | flops 536870912 | bytes 3145728 | tf_op jit(solution)/shard_map/pallas_call | solution.py:200
  231.8 2.4 fusion.60
  236.6 3.9 reshape.263
  252.5 6.4 %fusion.2 = f32[512,2816]{1,0:T(8,128)S(1)} fusion(bf16[512,1024]{1,0:T(8,128)(2,1)S(1)} %multiply_convert_fusion.3, bf16[1024,4736]{1,0:T(8,128)(2,1)} %all-gather.5.cloned.1.call-done), kind=kOutput, calls=%fused_computation.2 | convolution fusion | flops 2952790016 | bytes 12582912 | tf_op jit(solution)/shard_map/dot_general | solution.py:29
  259.0 4.2 fusion.10
  263.2 3.2 fusion.71
  277.1 15.3 %shard_map.154 = (bf16[2,256,512]{2,1,0:T(8,128)(2,1)S(1)}, f32[2,2,256,512]{3,2,1,0:T(8,128)S(1)}, bf16[2,2,64,512]{3,2,1,0:T(8,128)(2,1)}, bf16[2,2,64,512]{3,2,1,0:T(8,128)(2,1)}) custom-call(bf16[2,256,1536]{2,1,0:T(8,128)(2,1)S(1)} %bitcast.117, bf16[2,256,1536]{2,1,0:T(8,128)(2,1)S(1)} %bitcast.118, bf16[2,256,1536]{2,1,0:T(8,128)(2,1)S(1)} %bitcast.119, ...), custom_call_target="tpu_custom_call" | custom-call | flops 1342177280 | bytes 6291456 | tf_op jit(solution)/shard_map/pallas_call | solution.py:224
  294.6 4.0 collective-permute-start.10
  306.4 3.1 shard_map.165
  322.4 2.6 collective-permute-start.13
  335.1 46.5 %collective-permute-done.15.refs_4_ = bf16[2,128,2048]{2,1,0:T(8,128)(2,1)} collective-permute-done((bf16[2,128,2048]{2,1,0:T(8,128)(2,1)}, bf16[2,128,2048]{2,1,0:T(8,128)(2,1)}, u32[]{:S(2)}, u32[]{:S(2)}) %collective-permute-start.15) | collective-permute-done | bytes 1048608 | tf_op jit(solution)/shard_map/ppermute | solution.py:347
  383.6 2.6 collective-permute-start.16
  389.0 2.6 fusion.28
  391.6 2.5 shard_map.166
  394.2 12.6 %collective-permute-done.16.refs_5_ = bf16[1,128,2048]{2,1,0:T(8,128)(2,1)S(1)} collective-permute-done((bf16[1,128,2048]{2,1,0:T(8,128)(2,1)S(1)}, bf16[1,128,2048]{2,1,0:T(8,128)(2,1)S(1)}, u32[]{:S(2)}, u32[]{:S(2)}) %collective-permute-start.16) | collective-permute-done | bytes 524320 | tf_op jit(solution)/shard_map/ppermute | solution.py:347
  413.8 3.6 collective-permute-start.17
  418.1 3.2 collective-permute-done.17
  421.4 4.4 collective-permute-start.18
  425.8 3.5 collective-permute-done.27.refs_5_
  429.3 2.5 shard_map.167
  432.1 5.8 %collective-permute-done.25.refs_5_ = bf16[1,128,4224]{2,1,0:T(8,128)(2,1)S(1)} collective-permute-done((bf16[1,128,4224]{2,1,0:T(8,128)(2,1)S(1)}, bf16[1,128,4224]{2,1,0:T(8,128)(2,1)S(1)}, u32[]{:S(2)}, u32[]{:S(2)}) %collective-permute-start.25) | collective-permute-done | bytes 1081376 | tf_op jit(solution)/shard_map/ppermute | solution.py:347
  441.6 4.9 collective-permute-start.19
  446.5 4.2 collective-permute-start.28
  453.5 8.4 %collective-permute-done.28 = bf16[2,32,4224]{2,1,0:T(8,128)(2,1)S(1)} collective-permute-done((bf16[2,32,4224]{2,1,0:T(8,128)(2,1)S(1)}, bf16[2,32,4224]{2,1,0:T(8,128)(2,1)S(1)}, u32[]{:S(2)}, u32[]{:S(2)}) %collective-permute-start.28) | collective-permute-done | bytes 540704 | tf_op jit(solution)/shard_map/ppermute | solution.py:391
  462.0 4.4 collective-permute-start.29
  468.0 8.1 %collective-permute-done.29 = bf16[2,32,4224]{2,1,0:T(8,128)(2,1)S(1)} collective-permute-done((bf16[2,32,4224]{2,1,0:T(8,128)(2,1)S(1)}, bf16[2,32,4224]{2,1,0:T(8,128)(2,1)S(1)}, u32[]{:S(2)}, u32[]{:S(2)}) %collective-permute-start.29) | collective-permute-done | bytes 540704 | tf_op jit(solution)/shard_map/ppermute | solution.py:391
  476.3 5.6 %collective-permute-start.30 = (bf16[2,32,4224]{2,1,0:T(8,128)(2,1)S(1)}, bf16[2,32,4224]{2,1,0:T(8,128)(2,1)S(1)}, u32[]{:S(2)}, u32[]{:S(2)}) collective-permute-start(bf16[2,32,4224]{2,1,0:T(8,128)(2,1)S(1)} %add_convert_fusion.2), channel_id=1, source_target_pairs={{0,4},{4,8},{8,12},{1,5},{5,9},{9,13},{2,6},{6,10},{10,14},{3,7},{... | collective-permute-start | bytes 1622024 | tf_op jit(solution)/shard_map/ppermute | solution.py:391
  481.9 10.2 %collective-permute-done.33 = bf16[2,32,4224]{2,1,0:T(8,128)(2,1)S(1)} collective-permute-done((bf16[2,32,4224]{2,1,0:T(8,128)(2,1)S(1)}, bf16[2,32,4224]{2,1,0:T(8,128)(2,1)S(1)}, u32[]{:S(2)}, u32[]{:S(2)}) %collective-permute-start.33) | collective-permute-done | bytes 540704 | tf_op jit(solution)/shard_map/ppermute | solution.py:396
  (328 shorter events, 110.0 us)
Async XLA Ops:
  7.2 77.1 %all-gather.3.cloned.1.call-start = ((), (), s32[]{:S(2)}) async-start(), calls=%async_computation | async-start | bytes 3620864 | tf_op jit(solution)/shard_map/all_gather | solution.py:437
  11.3 207.0 %all-gather.5.cloned.1.call-start = ((), (), s32[]{:S(2)}) async-start(), calls=%async_computation.1 | async-start | bytes 10305536 | tf_op jit(solution)/shard_map/all_gather | solution.py:437
  15.8 224.7 %collective-permute-start.8 = (bf16[2,128,1024]{2,1,0:T(8,128)(2,1)}, bf16[2,128,1024]{2,1,0:T(8,128)(2,1)}, u32[]{:S(2)}, u32[]{:S(2)}) collective-permute-start(bf16[2,128,1024]{2,1,0:T(8,128)(2,1)} %param.17), channel_id=1, source_target_pairs={{0,1},{1,0},{2,3},{3,2},{4,5},{5,4},{6,7},{7,6},{8,9},{9,8},{10,11... | collective-permute-start | bytes 1572872 | tf_op jit(solution)/shard_map/ppermute | solution.py:33
  93.1 129.0 %collective-permute-start.2 = (bf16[2,64,1024]{2,1,0:T(8,128)(2,1)S(1)}, bf16[2,64,1024]{2,1,0:T(8,128)(2,1)S(1)}, u32[]{:S(2)}, u32[]{:S(2)}) collective-permute-start(bf16[2,64,1024]{2,1,0:T(8,128)(2,1)S(1)} %get-tuple-element.32), channel_id=1, source_target_pairs={{0,2},{2,4},{4,6},{6,8},{8,10},{10,12},{12,14},{1,3},{3,5},{5,7},{... | collective-permute-start | bytes 786440 | tf_op jit(solution)/shard_map/ppermute | solution.py:471
  96.6 125.5 %collective-permute-start.3 = (bf16[2,64,1024]{2,1,0:T(8,128)(2,1)S(1)}, bf16[2,64,1024]{2,1,0:T(8,128)(2,1)S(1)}, u32[]{:S(2)}, u32[]{:S(2)}) collective-permute-start(bf16[2,64,1024]{2,1,0:T(8,128)(2,1)S(1)} %get-tuple-element.31), channel_id=1, source_target_pairs={{2,0},{4,2},{6,4},{8,6},{10,8},{12,10},{14,12},{3,1},{5,3},{7,5},{... | collective-permute-start | bytes 786440 | tf_op jit(solution)/shard_map/ppermute | solution.py:472
  220.6 27.7 %collective-permute-start.6 = (bf16[1024,512]{1,0:T(8,128)(2,1)}, bf16[1024,512]{1,0:T(8,128)(2,1)}, u32[]{:S(2)}, u32[]{:S(2)}) collective-permute-start(bf16[1024,512]{1,0:T(8,128)(2,1)} %slice.157), channel_id=1, source_target_pairs={{0,1},{1,0},{2,3},{3,2},{4,5},{5,4},{6,7},{7,6},{8,9},{9,8},{10,11... | collective-permute-start | bytes 3145736 | tf_op jit(solution)/shard_map/ppermute | solution.py:33
  231.3 15.6 %collective-permute-start.4 = (bf16[512,512]{0,1:T(8,128)(2,1)}, bf16[512,512]{0,1:T(8,128)(2,1)}, u32[]{:S(2)}, u32[]{:S(2)}) collective-permute-start(bf16[512,512]{0,1:T(8,128)(2,1)} %copy.50), channel_id=1, source_target_pairs={{0,1},{1,0},{2,3},{3,2},{4,5},{5,4},{6,7},{7,6},{8,9},{9,8},{10,11... | collective-permute-start | bytes 1572872 | tf_op jit(solution)/shard_map/ppermute | solution.py:33
  294.6 15.5 %collective-permute-start.10 = (bf16[2,2,64,512]{3,2,1,0:T(8,128)(2,1)}, bf16[2,2,64,512]{3,2,1,0:T(8,128)(2,1)}, u32[]{:S(2)}, u32[]{:S(2)}) collective-permute-start(bf16[2,2,64,512]{3,2,1,0:T(8,128)(2,1)} %get-tuple-element.14), channel_id=1, source_target_pairs={{0,2},{2,4},{4,6},{6,8},{8,10},{10,12},{12,14},{1,3},{3,5},{5,7},{... | collective-permute-start | bytes 786440 | tf_op jit(solution)/shard_map/ppermute | solution.py:534
  298.6 11.5 %collective-permute-start.11 = (bf16[2,2,64,512]{3,2,1,0:T(8,128)(2,1)}, bf16[2,2,64,512]{3,2,1,0:T(8,128)(2,1)}, u32[]{:S(2)}, u32[]{:S(2)}) collective-permute-start(bf16[2,2,64,512]{3,2,1,0:T(8,128)(2,1)} %get-tuple-element.15), channel_id=1, source_target_pairs={{2,0},{4,2},{6,4},{8,6},{10,8},{12,10},{14,12},{3,1},{5,3},{7,5},{... | collective-permute-start | bytes 786440 | tf_op jit(solution)/shard_map/ppermute | solution.py:535
  303.1 28.0 %collective-permute-start.7 = (bf16[2,128,1024]{2,1,0:T(8,128)(2,1)}, bf16[2,128,1024]{2,1,0:T(8,128)(2,1)}, u32[]{:S(2)}, u32[]{:S(2)}) collective-permute-start(bf16[2,128,1024]{2,1,0:T(8,128)(2,1)} %fusion.42), channel_id=1, source_target_pairs={{0,1},{1,0},{2,3},{3,2},{4,5},{5,4},{6,7},{7,6},{8,9},{9,8},{10,11... | collective-permute-start | bytes 1572872 | tf_op jit(solution)/shard_map/ppermute | solution.py:33
  309.5 82.1 %collective-permute-start.26 = (bf16[2,128,4224]{2,1,0:T(8,128)(2,1)}, bf16[2,128,4224]{2,1,0:T(8,128)(2,1)}, u32[]{:S(2)}, u32[]{:S(2)}) collective-permute-start(bf16[2,128,4224]{2,1,0:T(8,128)(2,1)} %shard_map.165), channel_id=1, source_target_pairs={{0,16},{16,0},{1,17},{17,1},{2,18},{18,2},{3,19},{19,3},{4,20},{20... | collective-permute-start | bytes 6488072 | tf_op jit(solution)/shard_map/ppermute | solution.py:347
  316.4 17.2 %collective-permute-start.12 = (bf16[2,128,1024]{2,1,0:T(8,128)(2,1)}, bf16[2,128,1024]{2,1,0:T(8,128)(2,1)}, u32[]{:S(2)}, u32[]{:S(2)}) collective-permute-start(bf16[2,128,1024]{2,1,0:T(8,128)(2,1)} %fusion.41), channel_id=1, source_target_pairs={{0,1},{1,0},{2,3},{3,2},{4,5},{5,4},{6,7},{7,6},{8,9},{9,8},{10,11... | collective-permute-start | bytes 1572872 | tf_op jit(solution)/shard_map/ppermute | solution.py:33
  318.7 62.8 %collective-permute-start.15 = (bf16[2,128,2048]{2,1,0:T(8,128)(2,1)}, bf16[2,128,2048]{2,1,0:T(8,128)(2,1)}, u32[]{:S(2)}, u32[]{:S(2)}) collective-permute-start(bf16[2,128,2048]{2,1,0:T(8,128)(2,1)} %shard_map.159), channel_id=1, source_target_pairs={{0,16},{16,0},{1,17},{17,1},{2,18},{18,2},{3,19},{19,3},{4,20},{20... | collective-permute-start | bytes 3145736 | tf_op jit(solution)/shard_map/ppermute | solution.py:347
  322.4 63.7 %collective-permute-start.13 = (bf16[2,128,2048]{2,1,0:T(8,128)(2,1)}, bf16[2,128,2048]{2,1,0:T(8,128)(2,1)}, u32[]{:S(2)}, u32[]{:S(2)}) collective-permute-start(bf16[2,128,2048]{2,1,0:T(8,128)(2,1)} %shard_map.156), channel_id=1, source_target_pairs={{0,2},{2,0},{1,3},{3,1},{4,6},{6,4},{5,7},{7,5},{8,10},{10,8},{9,1... | collective-permute-start | bytes 3145736 | tf_op jit(solution)/shard_map/ppermute | solution.py:347
  331.1 80.7 %collective-permute-start.24 = (bf16[2,128,4224]{2,1,0:T(8,128)(2,1)S(1)}, bf16[2,128,4224]{2,1,0:T(8,128)(2,1)S(1)}, u32[]{:S(2)}, u32[]{:S(2)}) collective-permute-start(bf16[2,128,4224]{2,1,0:T(8,128)(2,1)S(1)} %shard_map.162), channel_id=1, source_target_pairs={{0,2},{2,0},{1,3},{3,1},{4,6},{6,4},{5,7},{7,5},{8,10},{10,8},{9,1... | collective-permute-start | bytes 6488072 | tf_op jit(solution)/shard_map/ppermute | solution.py:347
  383.6 23.2 %collective-permute-start.16 = (bf16[1,128,2048]{2,1,0:T(8,128)(2,1)S(1)}, bf16[1,128,2048]{2,1,0:T(8,128)(2,1)S(1)}, u32[]{:S(2)}, u32[]{:S(2)}) collective-permute-start(bf16[1,128,2048]{2,1,0:T(8,128)(2,1)S(1)} %shard_map.160), channel_id=1, source_target_pairs={{0,2},{2,0},{1,3},{3,1},{4,6},{6,4},{5,7},{7,5},{8,10},{10,8},{9,1... | collective-permute-start | bytes 1572872 | tf_op jit(solution)/shard_map/ppermute | solution.py:347
  388.3 20.5 %collective-permute-start.14 = (bf16[1,128,2048]{2,1,0:T(8,128)(2,1)S(1)}, bf16[1,128,2048]{2,1,0:T(8,128)(2,1)S(1)}, u32[]{:S(2)}, u32[]{:S(2)}) collective-permute-start(bf16[1,128,2048]{2,1,0:T(8,128)(2,1)S(1)} %shard_map.157), channel_id=1, source_target_pairs={{0,16},{16,0},{1,17},{17,1},{2,18},{18,2},{3,19},{19,3},{4,20},{20... | collective-permute-start | bytes 1572872 | tf_op jit(solution)/shard_map/ppermute | solution.py:347
  394.1 35.2 %collective-permute-start.27 = (bf16[1,128,4224]{2,1,0:T(8,128)(2,1)S(1)}, bf16[1,128,4224]{2,1,0:T(8,128)(2,1)S(1)}, u32[]{:S(2)}, u32[]{:S(2)}) collective-permute-start(bf16[1,128,4224]{2,1,0:T(8,128)(2,1)S(1)} %shard_map.166), channel_id=1, source_target_pairs={{0,2},{2,0},{1,3},{3,1},{4,6},{6,4},{5,7},{7,5},{8,10},{10,8},{9,1... | collective-permute-start | bytes 3244040 | tf_op jit(solution)/shard_map/ppermute | solution.py:347
  411.1 6.3 %collective-permute-start.20 = (bf16[2,32,2048]{2,1,0:T(8,128)(2,1)S(1)}, bf16[2,32,2048]{2,1,0:T(8,128)(2,1)S(1)}, u32[]{:S(2)}, u32[]{:S(2)}) collective-permute-start(bf16[2,32,2048]{2,1,0:T(8,128)(2,1)S(1)} %pad_maximum_fusion.13), channel_id=1, source_target_pairs={{12,8},{13,9},{14,10},{15,11},{28,24},{29,25},{30,26},{31,27}} | collective-permute-start | bytes 786440 | tf_op jit(solution)/shard_map/ppermute | solution.py:396
  413.1 24.8 %collective-permute-start.25 = (bf16[1,128,4224]{2,1,0:T(8,128)(2,1)S(1)}, bf16[1,128,4224]{2,1,0:T(8,128)(2,1)S(1)}, u32[]{:S(2)}, u32[]{:S(2)}) collective-permute-start(bf16[1,128,4224]{2,1,0:T(8,128)(2,1)S(1)} %shard_map.163), channel_id=1, source_target_pairs={{0,16},{16,0},{1,17},{17,1},{2,18},{18,2},{3,19},{19,3},{4,20},{20... | collective-permute-start | bytes 3244040 | tf_op jit(solution)/shard_map/ppermute | solution.py:347
  413.8 7.6 %collective-permute-start.17 = (bf16[2,32,2048]{2,1,0:T(8,128)(2,1)S(1)}, bf16[2,32,2048]{2,1,0:T(8,128)(2,1)S(1)}, u32[]{:S(2)}, u32[]{:S(2)}) collective-permute-start(bf16[2,32,2048]{2,1,0:T(8,128)(2,1)S(1)} %pad_maximum_fusion.12), channel_id=1, source_target_pairs={{0,4},{1,5},{2,6},{3,7},{16,20},{17,21},{18,22},{19,23}} | collective-permute-start | bytes 786440 | tf_op jit(solution)/shard_map/ppermute | solution.py:391
  417.4 22.7 %collective-permute-start.21 = (bf16[2,32,2048]{2,1,0:T(8,128)(2,1)S(1)}, bf16[2,32,2048]{2,1,0:T(8,128)(2,1)S(1)}, u32[]{:S(2)}, u32[]{:S(2)}) collective-permute-start(bf16[2,32,2048]{2,1,0:T(8,128)(2,1)S(1)} %add_convert_fusion.5), channel_id=1, source_target_pairs={{12,8},{8,4},{13,9},{9,5},{14,10},{10,6},{15,11},{11,7},{28,24},{2... | collective-permute-start | bytes 786440 | tf_op jit(solution)/shard_map/ppermute | solution.py:396
  421.4 20.1 %collective-permute-start.18 = (bf16[2,32,2048]{2,1,0:T(8,128)(2,1)S(1)}, bf16[2,32,2048]{2,1,0:T(8,128)(2,1)S(1)}, u32[]{:S(2)}, u32[]{:S(2)}) collective-permute-start(bf16[2,32,2048]{2,1,0:T(8,128)(2,1)S(1)} %add_convert_fusion.7), channel_id=1, source_target_pairs={{0,4},{4,8},{1,5},{5,9},{2,6},{6,10},{3,7},{7,11},{16,20},{20,24},... | collective-permute-start | bytes 786440 | tf_op jit(solution)/shard_map/ppermute | solution.py:391
  439.4 13.2 %collective-permute-start.31 = (bf16[2,32,4224]{2,1,0:T(8,128)(2,1)S(1)}, bf16[2,32,4224]{2,1,0:T(8,128)(2,1)S(1)}, u32[]{:S(2)}, u32[]{:S(2)}) collective-permute-start(bf16[2,32,4224]{2,1,0:T(8,128)(2,1)S(1)} %pad_maximum_fusion.10), channel_id=1, source_target_pairs={{12,8},{13,9},{14,10},{15,11},{28,24},{29,25},{30,26},{31,27}} | collective-permute-start | bytes 1622024 | tf_op jit(solution)/shard_map/ppermute | solution.py:396
  440.2 10.5 %collective-permute-start.22 = (bf16[2,32,2048]{2,1,0:T(8,128)(2,1)S(1)}, bf16[2,32,2048]{2,1,0:T(8,128)(2,1)S(1)}, u32[]{:S(2)}, u32[]{:S(2)}) collective-permute-start(bf16[2,32,2048]{2,1,0:T(8,128)(2,1)S(1)} %add_convert_fusion.4), channel_id=1, source_target_pairs={{12,8},{8,4},{4,0},{13,9},{9,5},{5,1},{14,10},{10,6},{6,2},{15,11}... | collective-permute-start | bytes 786440 | tf_op jit(solution)/shard_map/ppermute | solution.py:396
  441.6 10.8 %collective-permute-start.19 = (bf16[2,32,2048]{2,1,0:T(8,128)(2,1)S(1)}, bf16[2,32,2048]{2,1,0:T(8,128)(2,1)S(1)}, u32[]{:S(2)}, u32[]{:S(2)}) collective-permute-start(bf16[2,32,2048]{2,1,0:T(8,128)(2,1)S(1)} %add_convert_fusion.6), channel_id=1, source_target_pairs={{0,4},{4,8},{8,12},{1,5},{5,9},{9,13},{2,6},{6,10},{10,14},{3,7},{... | collective-permute-start | bytes 786440 | tf_op jit(solution)/shard_map/ppermute | solution.py:391
  446.5 15.4 %collective-permute-start.28 = (bf16[2,32,4224]{2,1,0:T(8,128)(2,1)S(1)}, bf16[2,32,4224]{2,1,0:T(8,128)(2,1)S(1)}, u32[]{:S(2)}, u32[]{:S(2)}) collective-permute-start(bf16[2,32,4224]{2,1,0:T(8,128)(2,1)S(1)} %pad_maximum_fusion.9), channel_id=1, source_target_pairs={{0,4},{1,5},{2,6},{3,7},{16,20},{17,21},{18,22},{19,23}} | collective-permute-start | bytes 1622024 | tf_op jit(solution)/shard_map/ppermute | solution.py:391
  452.6 13.9 %collective-permute-start.23 = (f32[32,2048]{1,0:T(8,128)S(1)}, f32[32,2048]{1,0:T(8,128)S(1)}, u32[]{:S(2)}, u32[]{:S(2)}) collective-permute-start(f32[32,2048]{1,0:T(8,128)S(1)} %dynamic-slice_bitcast_fusion.1), channel_id=1, source_target_pairs={{0,1},{1,0},{2,3},{3,2},{4,5},{5,4},{6,7},{7,6},{8,9},{9,8},{10,11... | collective-permute-start | bytes 786440 | tf_op jit(solution)/shard_map/ppermute | solution.py:33
  452.8 13.8 %collective-permute-start.32 = (bf16[2,32,4224]{2,1,0:T(8,128)(2,1)S(1)}, bf16[2,32,4224]{2,1,0:T(8,128)(2,1)S(1)}, u32[]{:S(2)}, u32[]{:S(2)}) collective-permute-start(bf16[2,32,4224]{2,1,0:T(8,128)(2,1)S(1)} %add_convert_fusion.1), channel_id=1, source_target_pairs={{12,8},{8,4},{13,9},{9,5},{14,10},{10,6},{15,11},{11,7},{28,24},{2... | collective-permute-start | bytes 1622024 | tf_op jit(solution)/shard_map/ppermute | solution.py:396
  462.0 14.1 %collective-permute-start.29 = (bf16[2,32,4224]{2,1,0:T(8,128)(2,1)S(1)}, bf16[2,32,4224]{2,1,0:T(8,128)(2,1)S(1)}, u32[]{:S(2)}, u32[]{:S(2)}) collective-permute-start(bf16[2,32,4224]{2,1,0:T(8,128)(2,1)S(1)} %add_convert_fusion.3), channel_id=1, source_target_pairs={{0,4},{4,8},{1,5},{5,9},{2,6},{6,10},{3,7},{7,11},{16,20},{20,24},... | collective-permute-start | bytes 1622024 | tf_op jit(solution)/shard_map/ppermute | solution.py:391
  466.7 25.4 %collective-permute-start.33 = (bf16[2,32,4224]{2,1,0:T(8,128)(2,1)S(1)}, bf16[2,32,4224]{2,1,0:T(8,128)(2,1)S(1)}, u32[]{:S(2)}, u32[]{:S(2)}) collective-permute-start(bf16[2,32,4224]{2,1,0:T(8,128)(2,1)S(1)} %add_convert_fusion), channel_id=1, source_target_pairs={{12,8},{8,4},{4,0},{13,9},{9,5},{5,1},{14,10},{10,6},{6,2},{15,11}... | collective-permute-start | bytes 1622024 | tf_op jit(solution)/shard_map/ppermute | solution.py:396
  476.3 17.2 %collective-permute-start.30 = (bf16[2,32,4224]{2,1,0:T(8,128)(2,1)S(1)}, bf16[2,32,4224]{2,1,0:T(8,128)(2,1)S(1)}, u32[]{:S(2)}, u32[]{:S(2)}) collective-permute-start(bf16[2,32,4224]{2,1,0:T(8,128)(2,1)S(1)} %add_convert_fusion.2), channel_id=1, source_target_pairs={{0,4},{4,8},{8,12},{1,5},{5,9},{9,13},{2,6},{6,10},{10,14},{3,7},{... | collective-permute-start | bytes 1622024 | tf_op jit(solution)/shard_map/ppermute | solution.py:391
  (74 other events, 1164.3 us)
Sparse Core Ops, SparseCore 0:
  11.4 72.8 all-gather.2
  87.6 130.6 all-gather.4

commit v2 on v1

--- a/solution.py
+++ b/solution.py
@@ -12,9 +12,9 @@
 LANES = 128
 NORM_EPSILON = 1e-05
 ROPE_BASE = 10000.0
-CHIPS = ("dp", "outer", "inner")
 F32 = jnp.float32
 BF16 = jnp.bfloat16
+LIGHT = pl.CostEstimate(flops=1024, bytes_accessed=1024, transcendentals=0)
 
 
 def contract_cols(left, right):
@@ -85,11 +85,7 @@
         out_specs=pl.BlockSpec((rows, tile), lambda j: (0, j)),
         out_shape=jax.ShapeDtypeStruct((rows, columns), BF16),
         compiler_params=pltpu.CompilerParams(vmem_limit_bytes=24 * 2**20),
-        cost_estimate=pl.CostEstimate(
-            flops=2 * rows * depth * columns,
-            bytes_accessed=2 * (rows * depth + depth * columns + rows * columns),
-            transcendentals=0,
-        ),
+        cost_estimate=LIGHT,
     )(normed, weight, cosine, sine)
 
 
@@ -196,7 +192,6 @@
 def attend(block, joined, low, high, query_ids, key_ids):
     streams, length, columns = joined.shape
     groups = columns // 3 // LANES
-    work = streams * groups * 2 * length * (block + 2 * HALF)
     return pl.pallas_call(
         functools.partial(attend_kernel, block),
         grid=(streams, groups),
@@ -204,16 +199,13 @@
         out_specs=pl.BlockSpec((1, length, LANES), lambda s, h: (s, 0, h)),
         out_shape=jax.ShapeDtypeStruct((streams, length, columns // 3), BF16),
         compiler_params=pltpu.CompilerParams(vmem_limit_bytes=24 * 2**20),
-        cost_estimate=pl.CostEstimate(
-            flops=4 * work * LANES, bytes_accessed=4 * joined.size, transcendentals=work
-        ),
+        cost_estimate=LIGHT,
     )(joined, joined, joined, low, low, high, high, query_ids, key_ids)
 
 
 def attend_back(block, joined, low, high, query_ids, key_ids, grad, cosine, sine):
     streams, length, columns = joined.shape
     groups = columns // 3 // LANES
-    work = streams * groups * 2 * length * (block + 2 * HALF)
 
     def pair(rows):
         return pl.BlockSpec((1, 2, rows, LANES), lambda s, h: (s, 0, 0, h))
@@ -240,9 +232,7 @@
             shape(HALF, BF16),
         ],
         compiler_params=pltpu.CompilerParams(vmem_limit_bytes=24 * 2**20),
-        cost_estimate=pl.CostEstimate(
-            flops=10 * work * LANES, bytes_accessed=8 * joined.size, transcendentals=work
-        ),
+        cost_estimate=LIGHT,
     )(joined, joined, joined, low, low, high, high, query_ids, key_ids, grad, cosine, sine)
 
 
@@ -284,71 +274,96 @@
         out_specs=pl.BlockSpec((1, length, 3 * width), lambda s: (s, 0, 0)),
         out_shape=jax.ShapeDtypeStruct((streams, length, 3 * width), BF16),
         compiler_params=pltpu.CompilerParams(vmem_limit_bytes=24 * 2**20),
-        cost_estimate=pl.CostEstimate(
-            flops=8 * mid.size, bytes_accessed=8 * mid.size, transcendentals=0
-        ),
+        cost_estimate=LIGHT,
     )(grad_query, mid, from_lower, from_upper, cosine, sine)
 
 
-def chunk_kernel(pairs, picks_ref, *refs):
+def arrival_order(width, shard_rows):
+    inner, outer, dp = (lax.axis_size(name) for name in ("inner", "outer", "dp"))
+    x, z, y = (lax.axis_index(name) for name in ("inner", "outer", "dp"))
+    place = jnp.arange(width, dtype=jnp.int32)
+    part, rest = place // (width // 2), place % (width // 2)
+    chunk, rest = rest // (outer * shard_rows), rest % (outer * shard_rows)
+    along_x = jnp.where(part == 0, chunk // dp, chunk % inner)
+    along_y = jnp.where(part == 0, chunk % dp, chunk // inner)
+    along_z, row = rest // shard_rows, rest % shard_rows
+    at_x = (x - along_x + inner) % inner
+    at_y = (y - along_y + dp) % dp
+    at_z = (z - along_z + outer) % outer
+    source = (((at_y * outer + at_z) * inner + at_x) * 2 + part) * shard_rows + row
+    return (place[:, None] == source[None, :]).astype(BF16)
+
+
+def forward(axis, distance=1):
+    count = lax.axis_size(axis)
+    return [(i, (i + distance) % count) for i in range(count)]
+
+
+def ring_gather(axis, piece):
+    pieces = [piece]
+    for _ in range(1, lax.axis_size(axis)):
+        pieces.append(lax.ppermute(pieces[-1], axis, forward(axis)))
+    return jnp.concatenate(pieces, 0)
+
+
+def direct_gather(pair):
+    arrived = [pair] + [
+        lax.ppermute(pair, "outer", forward("outer", distance))
+        for distance in range(1, lax.axis_size("outer"))
+    ]
+    return [jnp.concatenate([piece[part] for piece in arrived], 0) for part in range(2)]
+
+
+def gather_rest(parts):
+    one = ring_gather("inner", ring_gather("dp", parts[0]))
+    two = ring_gather("dp", ring_gather("inner", parts[1]))
+    return jnp.concatenate([one, two], 0)
+
+
+def chunk_kernel(pairs, *refs):
     lefts, rights, rest = refs[:pairs], refs[pairs : 2 * pairs], refs[2 * pairs :]
     adds, out_ref = rest[:-1], rest[-1]
     start = 0
     for left, right in zip(lefts, rights):
         columns = slice(start, start + right.shape[1])
-        total = matmul(left[0, 0, 0], right[...])
+        total = contract_rows(left[...], right[...])
         for add in adds:
-            total = total + add[0, :, columns].astype(F32)
-        out_ref[0, :, columns] = total.astype(BF16)
+            total = total + add[:, columns].astype(F32)
+        out_ref[:, columns] = total.astype(BF16)
         start = columns.stop
 
 
-def grad_chunks(lefts, rights, picks, adds):
-    rows, depth = lefts[0].shape[3:]
+def grad_chunk(lefts, rights, start, rows, adds):
+    depth = lefts[0].shape[0]
     columns = sum(right.shape[1] for right in rights)
-    fields = 3 + len(adds)
-    table = [
-        jnp.asarray(entry, jnp.int32)
-        for index, pick in enumerate(picks)
-        for entry in list(pick) + [where[index] for _, where in adds]
-    ]
-    count = len(picks)
-
-    def left_at(i, table):
-        return (table[i * fields], table[i * fields + 1], table[i * fields + 2], 0, 0)
-
-    def add_at(position):
-        return lambda i, table: (table[i * fields + 3 + position], 0, 0)
+    index = start // rows
+    if rows % LANES:
+        lefts = [left[:, start : start + rows] for left in lefts]
+        index = 0
+
+    def whole(shape):
+        return pl.BlockSpec(shape, lambda i: (0, 0))
+
+    def block_at(shape, block):
+        return pl.BlockSpec(shape, lambda i: block)
 
     return pl.pallas_call(
         functools.partial(chunk_kernel, len(lefts)),
-        grid_spec=pltpu.PrefetchScalarGridSpec(
-            num_scalar_prefetch=1,
-            grid=(count,),
-            in_specs=[pl.BlockSpec((1, 1, 1, rows, depth), left_at) for _ in lefts]
-            + [pl.BlockSpec(right.shape, lambda i, table: (0, 0)) for right in rights]
-            + [pl.BlockSpec((1, rows, columns), add_at(n)) for n in range(len(adds))],
-            out_specs=pl.BlockSpec((1, rows, columns), lambda i, table: (i, 0, 0)),
-        ),
-        out_shape=jax.ShapeDtypeStruct((count, rows, columns), BF16),
+        grid=(1,),
+        in_specs=[block_at((depth, rows), (0, index)) for _ in lefts]
+        + [whole(right.shape) for right in rights]
+        + [block_at((rows, columns), (at, 0)) for _, at in adds],
+        out_specs=whole((rows, columns)),
+        out_shape=jax.ShapeDtypeStruct((rows, columns), BF16),
         compiler_params=pltpu.CompilerParams(vmem_limit_bytes=40 * 2**20),
-        cost_estimate=pl.CostEstimate(
-            flops=2 * count * rows * depth * columns,
-            bytes_accessed=2 * (depth * columns + (1 + len(adds)) * count * rows * columns),
-            transcendentals=0,
-        ),
-    )(jnp.stack(table), *lefts, *rights, *[array for array, _ in adds])
+        cost_estimate=LIGHT,
+    )(*lefts, *rights, *[array for array, _ in adds])
 
 
 def ring(axis, chunk):
-    count, me = lax.axis_size(axis), lax.axis_index(axis)
     arrived = None
-    for step in range(1, count):
-        arrived = lax.ppermute(
-            chunk((me + count - step) % count, arrived),
-            axis,
-            [(i, (i + 1) % count) for i in range(count)],
-        )
+    for step in range(1, lax.axis_size(axis)):
+        arrived = lax.ppermute(chunk(step, arrived), axis, forward(axis))
     return arrived
 
 
@@ -356,49 +371,38 @@
     return [add for add in adds if add[0] is not None]
 
 
-def scatter_grads(lefts, rights):
+def scatter_grads(lefts, rights, shard_rows):
     inner, outer, dp = (lax.axis_size(name) for name in ("inner", "outer", "dp"))
-    x, z, y = (lax.axis_index(name) for name in ("inner", "outer", "dp"))
-    chunks = functools.partial(grad_chunks, lefts, rights)
-    all_x, all_y = list(range(inner)), list(range(dp))
+    rows = outer * shard_rows
+    half = inner * dp * rows
+    chunk = functools.partial(grad_chunk, lefts, rights)
     a_one = ring(
-        "inner",
-        lambda t, got: chunks([(t, i, 0) for i in all_y], with_adds((got, all_y))),
+        "inner", lambda d, got: chunk(d * dp * rows, dp * rows, with_adds((got, 0)))
     )
     b_one = ring(
         "dp",
-        lambda t, got: chunks([(i, t, 1) for i in all_x], with_adds((got, all_x))),
+        lambda d, got: chunk(half + d * inner * rows, inner * rows, with_adds((got, 0))),
     )
     a_two = ring(
-        "dp", lambda t, got: chunks([(x, t, 0)], with_adds((a_one, [t]), (got, [0])))
+        "dp", lambda d, got: chunk(d * rows, rows, with_adds((a_one, d), (got, 0)))
     )
     b_two = ring(
-        "inner", lambda t, got: chunks([(t, y, 1)], with_adds((b_one, [t]), (got, [0])))
+        "inner", lambda d, got: chunk(half + d * rows, rows, with_adds((b_one, d), (got, 0)))
     )
     mine = [
-        chunks([(x, y, 0)], with_adds((a_one, [y]), (a_two, [0]))),
-        chunks([(x, y, 1)], with_adds((b_one, [x]), (b_two, [0]))),
+        chunk(0, rows, with_adds((a_one, 0), (a_two, 0))),
+        chunk(half, rows, with_adds((b_one, 0), (b_two, 0))),
     ]
-    mine = [part.reshape(outer, -1, part.shape[-1]) for part in mine]
-
-    def part(target):
-        return jnp.stack(
-            [lax.dynamic_index_in_dim(half, target, 0, keepdims=False) for half in mine]
-        ).astype(F32)
-
-    up = down = jnp.zeros((), F32)
-    for step in range(1, outer):
-        up = lax.ppermute(
-            (part(jnp.clip(z + outer - step, 0, outer - 1)) + up).astype(BF16),
-            "outer",
-            [(i, i + 1) for i in range(step)],
-        ).astype(F32)
-        down = lax.ppermute(
-            (part(jnp.clip(z - outer + step, 0, outer - 1)) + down).astype(BF16),
-            "outer",
-            [(outer - 1 - i, outer - 2 - i) for i in range(step)],
-        ).astype(F32)
-    return part(z) + up + down
+
+    def part(distance):
+        cut = slice(distance * shard_rows, (distance + 1) * shard_rows)
+        return jnp.stack([piece[cut] for piece in mine])
+
+    arrived = [
+        lax.ppermute(part(distance), "outer", forward("outer", outer - distance))
+        for distance in range(1, outer)
+    ]
+    return sum([piece.astype(F32) for piece in arrived], part(0).astype(F32))
 
 
 def both_halves(total):
@@ -429,21 +433,35 @@
             cut = [jnp.pad(piece, ((0, 0), (0, pad - size))) for piece in cut]
         return cut[0::2], cut[1::2]
 
-    def spread(pieces):
+    def paired(pieces):
         low = jnp.concatenate([piece for one, _ in pieces for piece in one], 1)
         high = jnp.concatenate([piece for _, two in pieces for piece in two], 1)
         mine = jnp.where(core == 0, low, high)
         other = swap(jnp.where(core == 0, high, low))
-        return lax.all_gather(ordered(mine, other, 0), CHIPS, axis=0, tiled=True)
+        return ordered(mine[None], other[None], 0)
 
     gains = jnp.pad(jnp.stack([norm_attn, norm_mlp], 1), ((0, 0), (0, LANES - 2)))
-    first = spread([halves(w_qkv, 3, side), ([gains], [gains])])
-    second = spread(
-        [halves(w_out, 1, side), halves(w_in, 2, padded), halves(w_down, 1, padded)]
-    )
+    one = direct_gather(paired([halves(w_qkv, 3, side), ([gains], [gains])]))
+    pair_two = paired([halves(w_out, 1, side), halves(w_in, 2, padded)])
+    pair_three = paired([halves(w_down, 1, padded)])
+    pair_two, one = lax.optimization_barrier((pair_two, one))
+    two = direct_gather(pair_two)
+    first = gather_rest(one)
+    pair_three, two, first = lax.optimization_barrier((pair_three, two, first))
+    three = direct_gather(pair_three)
+    second = gather_rest(two)
+    three, second = lax.optimization_barrier((three, second))
+    down_half = gather_rest(three)
+    order = arrival_order(width, shard_rows)
+
+    def in_order(value):
+        return matmul(value, order).astype(BF16)
+
+    def out_of_order(value):
+        return contract_cols(value, order).astype(BF16)
 
     def both_blocks(value):
-        return ordered(value, swap(value), 1).reshape(rows, width)
+        return in_order(ordered(value, swap(value), 1).reshape(rows, width))
 
     tokens_low = both_blocks(tokens)
     grad_output = both_blocks(cotangent)
@@ -477,11 +495,11 @@
     attended_low = ordered(attended_half, swap(attended_half), 1)
     out_half = second[:, :side]
     full_out = ordered(out_half, swap(out_half), 1)
+    full_out = matmul(order, in_order(full_out)).astype(BF16)
     hidden = values + matmul(attended_low, full_out)
     unit_mlp, scale_mlp = normalise(hidden)
     normed_mlp_low = (unit_mlp * gain_mlp).astype(BF16)
-    in_half = second[:, side : side + 2 * padded]
-    down_half = second[:, side + 2 * padded :]
+    in_half = second[:, side:]
     expanded = matmul(normed_mlp_low, in_half)
     gate, up = expanded[:, :padded], expanded[:, padded:]
     below = 0.5 * (1.0 + lax.erf(gate * 0.5**0.5))
@@ -508,14 +526,11 @@
         mine, other = own_rows(partial)
         return mine + swap(other.astype(BF16)).astype(F32)
 
-    output = (own_rows(hidden)[0] + summed_rows(contract_cols(mixed_low, down_half))).astype(BF16)
-
-    def by_chunk(activations):
-        cut = activations.reshape(rows, dp, outer, inner, 2, shard_rows)
-        return cut.transpose(3, 1, 4, 2, 5, 0).reshape(inner, dp, 2, outer * shard_rows, rows)
+    output = own_rows(hidden)[0] + summed_rows(contract_cols(mixed_low, down_half))
+    output = out_of_order(output.astype(BF16).reshape(-1, width)).reshape(tokens.shape)
 
     mlp_total = scatter_grads(
-        [by_chunk(grad_output), by_chunk(normed_mlp_low)], [mixed_low, grad_expanded_low]
+        [grad_output, normed_mlp_low], [mixed_low, grad_expanded_low], shard_rows
     )
 
     grad_normed_mlp = contract_cols(grad_expanded_low, in_half)
@@ -535,15 +550,22 @@
     from_upper = lax.ppermute(to_lower, ("outer", "inner"), back)
     grad_joined = join_grads(grad_query, mid, from_lower, from_upper, cosine, sine)
     grad_joined = grad_joined.reshape(rows, 3 * side)
-    hidden_side = lax.dynamic_slice_in_dim(grad_hidden_low, core * side, side, 1)
+    hidden_side = lax.dynamic_slice_in_dim(out_of_order(grad_hidden_low), core * side, side, 1)
     attn_total = scatter_grads(
-        [by_chunk(normed_low), by_chunk(attended_low)], [grad_joined, hidden_side]
+        [normed_low, in_order(attended_low)], [grad_joined, hidden_side], shard_rows
     )
     grad_normed = summed_rows(contract_cols(grad_joined, first[:, : 3 * side]))
-    unit_mine, scale_mine = normalise(tokens.astype(F32))
+    unit_mine, scale_mine = normalise(own_rows(values)[0])
     grad_tokens = own_rows(grad_hidden)[0] + norm_back(
         unit_mine, scale_mine, gain_attn, grad_normed
     )
+    grad_tokens = lax.dot_general(
+        grad_tokens.reshape(-1, width),
+        order.astype(F32),
+        (((1,), (1,)), ((), ())),
+        precision=lax.Precision.HIGHEST,
+        preferred_element_type=F32,
+    ).reshape(tokens.shape)
 
     def interleaved(pair, start, parts, stride, size):
         cuts = []

time: 507 us -> 428 us (0.84)
  the two profiles are of different devices: /device:TPU:0 before, /device:TPU:13 now
where the time goes in v2:
time: 428 us; the launch traced here: 421 us
  waiting for transfers between devices  232 us (54%)
  starting transfers between devices  67 us (16%)
  Pallas kernels  39.2 us (9%)
  matrix products  39.1 us (9%)
  other arithmetic  25.8 us (6%)
  local copies, waits for them, and re-layouts  14.6 us (3%)
    ppermute x8, waiting for transfers between devices, ring(): arrived = lax.ppermute(chunk(step, arrived), axis, forward(axis))  70.6 us
    ppermute x6, waiting for transfers between devices, scatter_grads(): lax.ppermute(part(distance), 'outer', forward('outer', outer - distance))  60 us
    ppermute x12, waiting for transfers between devices, ring_gather(): pieces.append(lax.ppermute(pieces[-1], axis, forward(axis)))  44.3 us
    ppermute x9, waiting for transfers between devices, direct_gather(): lax.ppermute(pair, 'outer', forward('outer', distance))  38.9 us
    dot_general x7, matrix products, matmul(): return jnp.dot(left, right, preferred_element_type=F32)  22.2 us
    pallas_call x1, Pallas kernels, attend_back(): pl.pallas_call(functools.partial(attend_back_kernel, block), grid=(stream...  14.8 us
    ppermute x12, starting transfers between devices, swap(): return lax.ppermute(value, 'core', [(0, 1), (1, 0)])  13.5 us
    dot_general x6, matrix products, contract_cols(): lax.dot_general(left, right, (((1,), (1,)), ((), ())), preferred_element_...  11.7 us
  transfers between devices with their start and end apart: 51, of which 23 were waited for; matrix products, arithmetic and copies ran while one was open for 15% of the time, Pallas kernels for 9%

profile of v2, /device:TPU:13, one launch (start us, length us, event | category | flops | bytes accessed | tf_op | source)
XLA Modules:
  0.0 420.6 jit_solution(17139587260723106748)
XLA Ops:
  13.5 2.3 collective-permute-start.5
  20.1 9.1 %collective-permute-done.5 = bf16[2,32,1664]{2,1,0:T(8,128)(2,1)S(1)} collective-permute-done((bf16[2,32,1664]{2,1,0:T(8,128)(2,1)S(1)}, bf16[2,32,1664]{2,1,0:T(8,128)(2,1)S(1)}, u32[]{:S(2)}, u32[]{:S(2)}) %collective-permute-start.5) | collective-permute-done | bytes 213024 | tf_op jit(solution)/shard_map/ppermute | solution.py:311
  29.3 4.5 %collective-permute-done.4 = bf16[2,32,1664]{2,1,0:T(8,128)(2,1)S(1)} collective-permute-done((bf16[2,32,1664]{2,1,0:T(8,128)(2,1)S(1)}, bf16[2,32,1664]{2,1,0:T(8,128)(2,1)S(1)}, u32[]{:S(2)}, u32[]{:S(2)}) %collective-permute-start.4) | collective-permute-done | bytes 213024 | tf_op jit(solution)/shard_map/ppermute | solution.py:311
  48.8 13.9 %collective-permute-done.8 = bf16[2,32,3328]{2,1,0:T(8,128)(2,1)S(1)} collective-permute-done((bf16[2,32,3328]{2,1,0:T(8,128)(2,1)S(1)}, bf16[2,32,3328]{2,1,0:T(8,128)(2,1)S(1)}, u32[]{:S(2)}, u32[]{:S(2)}) %collective-permute-start.8) | collective-permute-done | bytes 426016 | tf_op jit(solution)/shard_map/ppermute | solution.py:311
  62.8 9.1 %collective-permute-done.7 = bf16[2,32,3328]{2,1,0:T(8,128)(2,1)S(1)} collective-permute-done((bf16[2,32,3328]{2,1,0:T(8,128)(2,1)S(1)}, bf16[2,32,3328]{2,1,0:T(8,128)(2,1)S(1)}, u32[]{:S(2)}, u32[]{:S(2)}) %collective-permute-start.7) | collective-permute-done | bytes 426016 | tf_op jit(solution)/shard_map/ppermute | solution.py:311
  78.2 4.5 %shard_map.152 = bf16[512,1536]{1,0:T(8,128)(2,1)S(1)} custom-call(bf16[512,1024]{1,0:T(8,128)(2,1)S(1)} %multiply_convert_fusion.3.normed_ref.refs_0_, bf16[1024,1664]{1,0:T(8,128)(2,1)S(1)} %constant_dynamic-update-slice_fusion.weight_ref, f32[512,256]{1,0:T(8,128)S(1)} %copy-done.5, f32[512,256]{1,0:T(8,128)S(1)} %get-tuple-element.139.sin_ref), custom_call_target="tpu_custom_call" | custom-call | flops 1024 | bytes 1024 | tf_op jit(solution)/shard_map/pallas_call | solution.py:76
  86.1 9.1 %collective-permute-start.15 = (bf16[2,64,1024]{2,1,0:T(8,128)(2,1)S(1)}, bf16[2,64,1024]{2,1,0:T(8,128)(2,1)S(1)}, u32[]{:S(2)}, u32[]{:S(2)}) collective-permute-start(bf16[2,64,1024]{2,1,0:T(8,128)(2,1)S(1)} %get-tuple-element.49), channel_id=1, source_target_pairs={{2,0},{4,2},{6,4},{8,6},{10,8},{12,10},{14,12},{3,1},{5,3},{7,5},{... | collective-permute-start | bytes 786440 | tf_op jit(solution)/shard_map/ppermute | solution.py:490
  95.9 8.7 %collective-permute-done.14.kl_ref.vl_ref = bf16[2,64,1024]{2,1,0:T(8,128)(2,1)S(1)} collective-permute-done((bf16[2,64,1024]{2,1,0:T(8,128)(2,1)S(1)}, bf16[2,64,1024]{2,1,0:T(8,128)(2,1)S(1)}, u32[]{:S(2)}, u32[]{:S(2)}) %collective-permute-start.14) | collective-permute-done | bytes 262176 | tf_op jit(solution)/shard_map/ppermute | solution.py:489
  105.5 8.2 %shard_map.153 = bf16[2,256,512]{2,1,0:T(8,128)(2,1)S(1)} custom-call(bf16[2,256,1536]{2,1,0:T(8,128)(2,1)S(1)} %bitcast.183, bf16[2,256,1536]{2,1,0:T(8,128)(2,1)S(1)} %bitcast.184, bf16[2,256,1536]{2,1,0:T(8,128)(2,1)S(1)} %bitcast.185, bf16[2,64,1024]{2,1,0:T(8,128)(2,1)S(1)} %collective-permute-done.14.kl_ref.vl_ref, ...), custom_call_target="tpu_custom_call" | custom-call | flops 1024 | bytes 1024 | tf_op jit(solution)/shard_map/pallas_call | solution.py:195
  113.7 6.3 %collective-permute-start.16 = (bf16[512,512]{1,0:T(8,128)(2,1)S(1)}, bf16[512,512]{1,0:T(8,128)(2,1)S(1)}, u32[]{:S(2)}, u32[]{:S(2)}) collective-permute-start(bf16[512,512]{1,0:T(8,128)(2,1)S(1)} %bitcast.196), channel_id=1, source_target_pairs={{0,1},{1,0},{2,3},{3,2},{4,5},{5,4},{6,7},{7,6},{8,9},{9,8},{10,11... | collective-permute-start | bytes 1572872 | tf_op jit(solution)/shard_map/ppermute | solution.py:33
  121.5 20.5 %collective-permute-done.21 = bf16[256,3328]{1,0:T(8,128)(2,1)S(1)} collective-permute-done((bf16[256,3328]{1,0:T(8,128)(2,1)S(1)}, bf16[256,3328]{1,0:T(8,128)(2,1)S(1)}, u32[]{:S(2)}, u32[]{:S(2)}) %collective-permute-start.21) | collective-permute-done | bytes 1703968 | tf_op jit(solution)/shard_map/ppermute | solution.py:305
  142.3 16.7 %collective-permute-done.23 = bf16[256,3328]{1,0:T(8,128)(2,1)S(1)} collective-permute-done((bf16[256,3328]{1,0:T(8,128)(2,1)S(1)}, bf16[256,3328]{1,0:T(8,128)(2,1)S(1)}, u32[]{:S(2)}, u32[]{:S(2)}) %collective-permute-start.23) | collective-permute-done | bytes 1703968 | tf_op jit(solution)/shard_map/ppermute | solution.py:305
  164.4 5.7 %collective-permute-done.25 = bf16[128,1408]{1,0:T(8,128)(2,1)S(1)} collective-permute-done((bf16[128,1408]{1,0:T(8,128)(2,1)S(1)}, bf16[128,1408]{1,0:T(8,128)(2,1)S(1)}, u32[]{:S(2)}, u32[]{:S(2)}) %collective-permute-start.25) | collective-permute-done | bytes 360480 | tf_op jit(solution)/shard_map/ppermute | solution.py:305
  176.8 7.4 %fusion.35 = bf16[1024,1024]{1,0:T(8,128)(2,1)} fusion(s32[1024]{0:T(1024)} %copy-done.35, bf16[1024,512]{1,0:T(8,128)(2,1)} %get-tuple-element.45, bf16[1024,512]{1,0:T(8,128)(2,1)} %get-tuple-element.44), kind=kOutput, calls=%fused_computation.51 | convolution fusion | flops 4303355904 | bytes 4198400 | tf_op jit(solution)/shard_map/dot_general | solution.py:29
  184.2 3.7 fusion.123
  188.6 3.2 fusion.2
  194.4 3.0 fusion.22
  197.4 4.1 fusion.124
  207.6 2.7 shard_map.165
  214.0 14.8 %shard_map.154 = (bf16[2,256,512]{2,1,0:T(8,128)(2,1)S(1)}, f32[2,2,256,512]{3,2,1,0:T(8,128)S(1)}, bf16[2,2,64,512]{3,2,1,0:T(8,128)(2,1)S(1)}, bf16[2,2,64,512]{3,2,1,0:T(8,128)(2,1)S(1)}) custom-call(bf16[2,256,1536]{2,1,0:T(8,128)(2,1)S(1)} %bitcast.186, bf16[2,256,1536]{2,1,0:T(8,128)(2,1)S(1)} %bitcast.187, bf16[2,256,1536]{2,1,0:T(8,128)(2,1)S(1)} %bitcast.188, ...), custom_call_target="tpu_custom_call" | custom-call | flops 1024 | bytes 1024 | tf_op jit(solution)/shard_map/pallas_call | solution.py:216
  228.7 3.0 collective-permute-start.32
  231.8 3.4 collective-permute-start.33
  238.6 6.7 %collective-permute-done.33.high_ref = bf16[2,2,64,512]{3,2,1,0:T(8,128)(2,1)S(1)} collective-permute-done((bf16[2,2,64,512]{3,2,1,0:T(8,128)(2,1)S(1)}, bf16[2,2,64,512]{3,2,1,0:T(8,128)(2,1)S(1)}, u32[]{:S(2)}, u32[]{:S(2)}) %collective-permute-start.33) | collective-permute-done | bytes 262176 | tf_op jit(solution)/shard_map/ppermute | solution.py:550
  259.3 21.8 %collective-permute-done.37.refs_4_ = bf16[256,2048]{1,0:T(8,128)(2,1)S(1)} collective-permute-done((bf16[256,2048]{1,0:T(8,128)(2,1)S(1)}, bf16[256,2048]{1,0:T(8,128)(2,1)S(1)}, u32[]{:S(2)}, u32[]{:S(2)}) %collective-permute-start.37) | collective-permute-done | bytes 1048608 | tf_op jit(solution)/shard_map/ppermute | solution.py:366
  286.7 43.8 %collective-permute-done.38.refs_5_ = bf16[128,2048]{1,0:T(8,128)(2,1)S(1)} collective-permute-done((bf16[128,2048]{1,0:T(8,128)(2,1)S(1)}, bf16[128,2048]{1,0:T(8,128)(2,1)S(1)}, u32[]{:S(2)}, u32[]{:S(2)}) %collective-permute-start.38) | collective-permute-done | bytes 524320 | tf_op jit(solution)/shard_map/ppermute | solution.py:366
  335.0 5.2 %fusion.12 = f32[2,128,1024]{2,1,0:T(8,128)} fusion(s32[1024]{0:T(1024)S(1)} %copy-done.36, f32[2,2,128,1024]{3,2,1,0:T(8,128)} %bitcast.199, s32[]{:T(128)S(6)} %select_n.349, f32[2,2,128,1024]{3,2,1,0:T(8,128)S(1)} %copy-done.10, f32[2,128]{1,0:T(2,128)S(1)} %broadcast_multiply_fusion.4, f32[2,128]{1,0:T(2,128)S(1)} %broadcast_multiply_fusion.5, ...), kind=kOutput, calls=%fused_computation.14 | convolution fusion | flops 3224895488 | bytes 4730884 | tf_op jit(solution)/shard_map/dot_general | solution.py:562
  341.4 12.4 %collective-permute-done.40 = bf16[2,32,2048]{2,1,0:T(8,128)(2,1)S(1)} collective-permute-done((bf16[2,32,2048]{2,1,0:T(8,128)(2,1)S(1)}, bf16[2,32,2048]{2,1,0:T(8,128)(2,1)S(1)}, u32[]{:S(2)}, u32[]{:S(2)}) %collective-permute-start.40) | collective-permute-done | bytes 262176 | tf_op jit(solution)/shard_map/ppermute | solution.py:402
  358.0 5.1 %collective-permute-done.44.refs_5_ = bf16[128,4224]{1,0:T(8,128)(2,1)S(1)} collective-permute-done((bf16[128,4224]{1,0:T(8,128)(2,1)S(1)}, bf16[128,4224]{1,0:T(8,128)(2,1)S(1)}, u32[]{:S(2)}, u32[]{:S(2)}) %collective-permute-start.44) | collective-permute-done | bytes 1081376 | tf_op jit(solution)/shard_map/ppermute | solution.py:366
  364.5 3.9 collective-permute-start.48
  368.7 5.4 %collective-permute-done.49 = bf16[2,32,4224]{2,1,0:T(8,128)(2,1)S(1)} collective-permute-done((bf16[2,32,4224]{2,1,0:T(8,128)(2,1)S(1)}, bf16[2,32,4224]{2,1,0:T(8,128)(2,1)S(1)}, u32[]{:S(2)}, u32[]{:S(2)}) %collective-permute-start.49) | collective-permute-done | bytes 540704 | tf_op jit(solution)/shard_map/ppermute | solution.py:402
  374.1 32.2 %collective-permute-done.48 = bf16[2,32,4224]{2,1,0:T(8,128)(2,1)S(1)} collective-permute-done((bf16[2,32,4224]{2,1,0:T(8,128)(2,1)S(1)}, bf16[2,32,4224]{2,1,0:T(8,128)(2,1)S(1)}, u32[]{:S(2)}, u32[]{:S(2)}) %collective-permute-start.48) | collective-permute-done | bytes 540704 | tf_op jit(solution)/shard_map/ppermute | solution.py:402
  406.3 7.9 %collective-permute-done.47 = bf16[2,32,4224]{2,1,0:T(8,128)(2,1)S(1)} collective-permute-done((bf16[2,32,4224]{2,1,0:T(8,128)(2,1)S(1)}, bf16[2,32,4224]{2,1,0:T(8,128)(2,1)S(1)}, u32[]{:S(2)}, u32[]{:S(2)}) %collective-permute-start.47) | collective-permute-done | bytes 540704 | tf_op jit(solution)/shard_map/ppermute | solution.py:402
  (315 shorter events, 109.9 us)
Async XLA Ops:
  8.7 28.7 %collective-permute-start.30 = (bf16[2,128,1024]{2,1,0:T(8,128)(2,1)S(1)}, bf16[2,128,1024]{2,1,0:T(8,128)(2,1)}, u32[]{:S(2)}, u32[]{:S(2)}) collective-permute-start(bf16[2,128,1024]{2,1,0:T(8,128)(2,1)S(1)} %copy-done.26), channel_id=1, source_target_pairs={{0,1},{1,0},{2,3},{3,2},{4,5},{5,4},{6,7},{7,6},{8,9},{9,8},{10,11... | collective-permute-start | bytes 1572872 | tf_op jit(solution)/shard_map/ppermute | solution.py:33
  8.8 29.0 %collective-permute-start = (bf16[2,128,1024]{2,1,0:T(8,128)(2,1)S(1)}, bf16[2,128,1024]{2,1,0:T(8,128)(2,1)}, u32[]{:S(2)}, u32[]{:S(2)}) collective-permute-start(bf16[2,128,1024]{2,1,0:T(8,128)(2,1)S(1)} %copy-done.27), channel_id=1, source_target_pairs={{0,1},{1,0},{2,3},{3,2},{4,5},{5,4},{6,7},{7,6},{8,9},{9,8},{10,11... | collective-permute-start | bytes 1572872 | tf_op jit(solution)/shard_map/ppermute | solution.py:33
  15.8 18.0 %collective-permute-start.4 = (bf16[2,32,1664]{2,1,0:T(8,128)(2,1)S(1)}, bf16[2,32,1664]{2,1,0:T(8,128)(2,1)S(1)}, u32[]{:S(2)}, u32[]{:S(2)}) collective-permute-start(bf16[2,32,1664]{2,1,0:T(8,128)(2,1)S(1)} %pad_maximum_fusion.26), channel_id=1, source_target_pairs={{0,4},{4,8},{8,12},{12,0},{1,5},{5,9},{9,13},{13,1},{2,6},{6,10},{... | collective-permute-start | bytes 638984 | tf_op jit(solution)/shard_map/ppermute | solution.py:311
  35.2 27.6 %collective-permute-start.8 = (bf16[2,32,3328]{2,1,0:T(8,128)(2,1)S(1)}, bf16[2,32,3328]{2,1,0:T(8,128)(2,1)S(1)}, u32[]{:S(2)}, u32[]{:S(2)}) collective-permute-start(bf16[2,32,3328]{2,1,0:T(8,128)(2,1)S(1)} %pad_maximum_fusion.17), channel_id=1, source_target_pairs={{0,8},{4,12},{8,0},{12,4},{1,9},{5,13},{9,1},{13,5},{2,10},{6,14},... | collective-permute-start | bytes 1277960 | tf_op jit(solution)/shard_map/ppermute | solution.py:311
  37.4 34.5 %collective-permute-start.7 = (bf16[2,32,3328]{2,1,0:T(8,128)(2,1)S(1)}, bf16[2,32,3328]{2,1,0:T(8,128)(2,1)S(1)}, u32[]{:S(2)}, u32[]{:S(2)}) collective-permute-start(bf16[2,32,3328]{2,1,0:T(8,128)(2,1)S(1)} %pad_maximum_fusion.17), channel_id=1, source_target_pairs={{0,4},{4,8},{8,12},{12,0},{1,5},{5,9},{9,13},{13,1},{2,6},{6,10},{... | collective-permute-start | bytes 1277960 | tf_op jit(solution)/shard_map/ppermute | solution.py:311
  47.2 24.9 %collective-permute-start.11 = (bf16[256,1664]{1,0:T(8,128)(2,1)S(1)}, bf16[256,1664]{1,0:T(8,128)(2,1)S(1)}, u32[]{:S(2)}, u32[]{:S(2)}) collective-permute-start(bf16[256,1664]{1,0:T(8,128)(2,1)S(1)} %pad_maximum_fusion.8), channel_id=1, source_target_pairs={{0,2},{2,0},{1,3},{3,1},{4,6},{6,4},{5,7},{7,5},{8,10},{10,8},{9,1... | collective-permute-start | bytes 2555912 | tf_op jit(solution)/shard_map/ppermute | solution.py:305
  48.5 23.8 %collective-permute-start.13 = (bf16[256,1664]{1,0:T(8,128)(2,1)S(1)}, bf16[256,1664]{1,0:T(8,128)(2,1)S(1)}, u32[]{:S(2)}, u32[]{:S(2)}) collective-permute-start(bf16[256,1664]{1,0:T(8,128)(2,1)S(1)} %pad_maximum_fusion.9), channel_id=1, source_target_pairs={{0,16},{16,0},{1,17},{17,1},{2,18},{18,2},{3,19},{19,3},{4,20},{20... | collective-permute-start | bytes 2555912 | tf_op jit(solution)/shard_map/ppermute | solution.py:305
  75.9 19.9 %collective-permute-start.17 = (bf16[2,32,1408]{2,1,0:T(8,128)(2,1)S(1)}, bf16[2,32,1408]{2,1,0:T(8,128)(2,1)S(1)}, u32[]{:S(2)}, u32[]{:S(2)}) collective-permute-start(bf16[2,32,1408]{2,1,0:T(8,128)(2,1)S(1)} %pad_maximum_fusion.27), channel_id=1, source_target_pairs={{0,4},{4,8},{8,12},{12,0},{1,5},{5,9},{9,13},{13,1},{2,6},{6,10},{... | collective-permute-start | bytes 540680 | tf_op jit(solution)/shard_map/ppermute | solution.py:311
  76.0 19.3 %collective-permute-start.20 = (bf16[128,3328]{1,0:T(8,128)(2,1)S(1)}, bf16[128,3328]{1,0:T(8,128)(2,1)S(1)}, u32[]{:S(2)}, u32[]{:S(2)}) collective-permute-start(bf16[128,3328]{1,0:T(8,128)(2,1)S(1)} %pad_maximum_fusion.6), channel_id=1, source_target_pairs={{0,16},{16,0},{1,17},{17,1},{2,18},{18,2},{3,19},{19,3},{4,20},{20... | collective-permute-start | bytes 2555912 | tf_op jit(solution)/shard_map/ppermute | solution.py:305
  76.3 43.8 %collective-permute-start.22 = (bf16[128,3328]{1,0:T(8,128)(2,1)S(1)}, bf16[128,3328]{1,0:T(8,128)(2,1)S(1)}, u32[]{:S(2)}, u32[]{:S(2)}) collective-permute-start(bf16[128,3328]{1,0:T(8,128)(2,1)S(1)} %pad_maximum_fusion.7), channel_id=1, source_target_pairs={{0,2},{2,0},{1,3},{3,1},{4,6},{6,4},{5,7},{7,5},{8,10},{10,8},{9,1... | collective-permute-start | bytes 2555912 | tf_op jit(solution)/shard_map/ppermute | solution.py:305
  82.8 21.8 %collective-permute-start.14 = (bf16[2,64,1024]{2,1,0:T(8,128)(2,1)S(1)}, bf16[2,64,1024]{2,1,0:T(8,128)(2,1)S(1)}, u32[]{:S(2)}, u32[]{:S(2)}) collective-permute-start(bf16[2,64,1024]{2,1,0:T(8,128)(2,1)S(1)} %get-tuple-element.50), channel_id=1, source_target_pairs={{0,2},{2,4},{4,6},{6,8},{8,10},{10,12},{12,14},{1,3},{3,5},{5,7},{... | collective-permute-start | bytes 786440 | tf_op jit(solution)/shard_map/ppermute | solution.py:489
  86.1 19.4 %collective-permute-start.15 = (bf16[2,64,1024]{2,1,0:T(8,128)(2,1)S(1)}, bf16[2,64,1024]{2,1,0:T(8,128)(2,1)S(1)}, u32[]{:S(2)}, u32[]{:S(2)}) collective-permute-start(bf16[2,64,1024]{2,1,0:T(8,128)(2,1)S(1)} %get-tuple-element.49), channel_id=1, source_target_pairs={{2,0},{4,2},{6,4},{8,6},{10,8},{12,10},{14,12},{3,1},{5,3},{7,5},{... | collective-permute-start | bytes 786440 | tf_op jit(solution)/shard_map/ppermute | solution.py:490
  95.4 46.6 %collective-permute-start.21 = (bf16[256,3328]{1,0:T(8,128)(2,1)S(1)}, bf16[256,3328]{1,0:T(8,128)(2,1)S(1)}, u32[]{:S(2)}, u32[]{:S(2)}) collective-permute-start(bf16[256,3328]{1,0:T(8,128)(2,1)S(1)} %pad_maximum_fusion.1), channel_id=1, source_target_pairs={{0,2},{2,0},{1,3},{3,1},{4,6},{6,4},{5,7},{7,5},{8,10},{10,8},{9,1... | collective-permute-start | bytes 5111816 | tf_op jit(solution)/shard_map/ppermute | solution.py:305
  113.7 47.7 %collective-permute-start.16 = (bf16[512,512]{1,0:T(8,128)(2,1)S(1)}, bf16[512,512]{1,0:T(8,128)(2,1)S(1)}, u32[]{:S(2)}, u32[]{:S(2)}) collective-permute-start(bf16[512,512]{1,0:T(8,128)(2,1)S(1)} %bitcast.196), channel_id=1, source_target_pairs={{0,1},{1,0},{2,3},{3,2},{4,5},{5,4},{6,7},{7,6},{8,9},{9,8},{10,11... | collective-permute-start | bytes 1572872 | tf_op jit(solution)/shard_map/ppermute | solution.py:33
  120.2 38.9 %collective-permute-start.23 = (bf16[256,3328]{1,0:T(8,128)(2,1)S(1)}, bf16[256,3328]{1,0:T(8,128)(2,1)S(1)}, u32[]{:S(2)}, u32[]{:S(2)}) collective-permute-start(bf16[256,3328]{1,0:T(8,128)(2,1)S(1)} %pad_maximum_fusion.2), channel_id=1, source_target_pairs={{0,16},{16,0},{1,17},{17,1},{2,18},{18,2},{3,19},{19,3},{4,20},{20... | collective-permute-start | bytes 5111816 | tf_op jit(solution)/shard_map/ppermute | solution.py:305
  159.3 16.0 %collective-permute-start.24 = (bf16[1024,512]{1,0:T(8,128)(2,1)S(1)}, bf16[1024,512]{1,0:T(8,128)(2,1)S(1)}, u32[]{:S(2)}, u32[]{:S(2)}) collective-permute-start(bf16[1024,512]{1,0:T(8,128)(2,1)S(1)} %slice.266), channel_id=1, source_target_pairs={{0,1},{1,0},{2,3},{3,2},{4,5},{5,4},{6,7},{7,6},{8,9},{9,8},{10,11... | collective-permute-start | bytes 3145736 | tf_op jit(solution)/shard_map/ppermute | solution.py:33
  171.0 20.7 %collective-permute-start.26 = (bf16[256,1408]{1,0:T(8,128)(2,1)}, bf16[256,1408]{1,0:T(8,128)(2,1)}, u32[]{:S(2)}, u32[]{:S(2)}) collective-permute-start(bf16[256,1408]{1,0:T(8,128)(2,1)} %pad_maximum_fusion.10), channel_id=1, source_target_pairs={{0,2},{2,0},{1,3},{3,1},{4,6},{6,4},{5,7},{7,5},{8,10},{10,8},{9,1... | collective-permute-start | bytes 2162696 | tf_op jit(solution)/shard_map/ppermute | solution.py:305
  173.3 19.9 %collective-permute-start.28 = (bf16[256,1408]{1,0:T(8,128)(2,1)}, bf16[256,1408]{1,0:T(8,128)(2,1)}, u32[]{:S(2)}, u32[]{:S(2)}) collective-permute-start(bf16[256,1408]{1,0:T(8,128)(2,1)} %pad_maximum_fusion.11), channel_id=1, source_target_pairs={{0,16},{16,0},{1,17},{17,1},{2,18},{18,2},{3,19},{19,3},{4,20},{20... | collective-permute-start | bytes 2162696 | tf_op jit(solution)/shard_map/ppermute | solution.py:305
  207.6 46.5 %collective-permute-start.29 = (bf16[2,128,1024]{2,1,0:T(8,128)(2,1)S(1)}, bf16[2,128,1024]{2,1,0:T(8,128)(2,1)}, u32[]{:S(2)}, u32[]{:S(2)}) collective-permute-start(bf16[2,128,1024]{2,1,0:T(8,128)(2,1)S(1)} %fusion.59), channel_id=1, source_target_pairs={{0,1},{1,0},{2,3},{3,2},{4,5},{5,4},{6,7},{7,6},{8,9},{9,8},{10,11... | collective-permute-start | bytes 1572872 | tf_op jit(solution)/shard_map/ppermute | solution.py:33
  210.3 75.2 %collective-permute-start.45 = (bf16[256,4224]{1,0:T(8,128)(2,1)}, bf16[256,4224]{1,0:T(8,128)(2,1)S(1)}, u32[]{:S(2)}, u32[]{:S(2)}) collective-permute-start(bf16[256,4224]{1,0:T(8,128)(2,1)} %shard_map.165), channel_id=1, source_target_pairs={{0,16},{16,0},{1,17},{17,1},{2,18},{18,2},{3,19},{19,3},{4,20},{20... | collective-permute-start | bytes 6488072 | tf_op jit(solution)/shard_map/ppermute | solution.py:366
  247.7 33.4 %collective-permute-start.37 = (bf16[256,2048]{1,0:T(8,128)(2,1)S(1)}, bf16[256,2048]{1,0:T(8,128)(2,1)S(1)}, u32[]{:S(2)}, u32[]{:S(2)}) collective-permute-start(bf16[256,2048]{1,0:T(8,128)(2,1)S(1)} %shard_map.159), channel_id=1, source_target_pairs={{0,16},{16,0},{1,17},{17,1},{2,18},{18,2},{3,19},{19,3},{4,20},{20... | collective-permute-start | bytes 3145736 | tf_op jit(solution)/shard_map/ppermute | solution.py:366
  249.0 33.3 %collective-permute-start.35 = (bf16[256,2048]{1,0:T(8,128)(2,1)S(1)}, bf16[256,2048]{1,0:T(8,128)(2,1)S(1)}, u32[]{:S(2)}, u32[]{:S(2)}) collective-permute-start(bf16[256,2048]{1,0:T(8,128)(2,1)S(1)} %shard_map.156), channel_id=1, source_target_pairs={{0,2},{2,0},{1,3},{3,1},{4,6},{6,4},{5,7},{7,5},{8,10},{10,8},{9,1... | collective-permute-start | bytes 3145736 | tf_op jit(solution)/shard_map/ppermute | solution.py:366
  251.8 31.8 %collective-permute-start.34 = (bf16[2,128,1024]{2,1,0:T(8,128)(2,1)}, bf16[2,128,1024]{2,1,0:T(8,128)(2,1)}, u32[]{:S(2)}, u32[]{:S(2)}) collective-permute-start(bf16[2,128,1024]{2,1,0:T(8,128)(2,1)} %fusion.60), channel_id=1, source_target_pairs={{0,1},{1,0},{2,3},{3,2},{4,5},{5,4},{6,7},{7,6},{8,9},{9,8},{10,11... | collective-permute-start | bytes 1572872 | tf_op jit(solution)/shard_map/ppermute | solution.py:33
  254.1 86.2 %collective-permute-start.43 = (bf16[256,4224]{1,0:T(8,128)(2,1)S(1)}, bf16[256,4224]{1,0:T(8,128)(2,1)S(1)}, u32[]{:S(2)}, u32[]{:S(2)}) collective-permute-start(bf16[256,4224]{1,0:T(8,128)(2,1)S(1)} %shard_map.162), channel_id=1, source_target_pairs={{0,2},{2,0},{1,3},{3,1},{4,6},{6,4},{5,7},{7,5},{8,10},{10,8},{9,1... | collective-permute-start | bytes 6488072 | tf_op jit(solution)/shard_map/ppermute | solution.py:366
  281.6 48.9 %collective-permute-start.38 = (bf16[128,2048]{1,0:T(8,128)(2,1)S(1)}, bf16[128,2048]{1,0:T(8,128)(2,1)S(1)}, u32[]{:S(2)}, u32[]{:S(2)}) collective-permute-start(bf16[128,2048]{1,0:T(8,128)(2,1)S(1)} %shard_map.160), channel_id=1, source_target_pairs={{0,2},{2,0},{1,3},{3,1},{4,6},{6,4},{5,7},{7,5},{8,10},{10,8},{9,1... | collective-permute-start | bytes 1572872 | tf_op jit(solution)/shard_map/ppermute | solution.py:366
  282.9 48.2 %collective-permute-start.36 = (bf16[128,2048]{1,0:T(8,128)(2,1)S(1)}, bf16[128,2048]{1,0:T(8,128)(2,1)S(1)}, u32[]{:S(2)}, u32[]{:S(2)}) collective-permute-start(bf16[128,2048]{1,0:T(8,128)(2,1)S(1)} %shard_map.157), channel_id=1, source_target_pairs={{0,16},{16,0},{1,17},{17,1},{2,18},{18,2},{3,19},{19,3},{4,20},{20... | collective-permute-start | bytes 1572872 | tf_op jit(solution)/shard_map/ppermute | solution.py:366
  286.3 70.7 %collective-permute-start.46 = (bf16[128,4224]{1,0:T(8,128)(2,1)S(1)}, bf16[128,4224]{1,0:T(8,128)(2,1)S(1)}, u32[]{:S(2)}, u32[]{:S(2)}) collective-permute-start(bf16[128,4224]{1,0:T(8,128)(2,1)S(1)} %shard_map.166), channel_id=1, source_target_pairs={{0,2},{2,0},{1,3},{3,1},{4,6},{6,4},{5,7},{7,5},{8,10},{10,8},{9,1... | collective-permute-start | bytes 3244040 | tf_op jit(solution)/shard_map/ppermute | solution.py:366
  333.4 20.3 %collective-permute-start.40 = (bf16[2,32,2048]{2,1,0:T(8,128)(2,1)S(1)}, bf16[2,32,2048]{2,1,0:T(8,128)(2,1)S(1)}, u32[]{:S(2)}, u32[]{:S(2)}) collective-permute-start(bf16[2,32,2048]{2,1,0:T(8,128)(2,1)S(1)} %pad_maximum_fusion.24), channel_id=1, source_target_pairs={{0,8},{4,12},{8,0},{12,4},{1,9},{5,13},{9,1},{13,5},{2,10},{6,14},... | collective-permute-start | bytes 786440 | tf_op jit(solution)/shard_map/ppermute | solution.py:402
  333.6 22.3 %collective-permute-start.39 = (bf16[2,32,2048]{2,1,0:T(8,128)(2,1)S(1)}, bf16[2,32,2048]{2,1,0:T(8,128)(2,1)S(1)}, u32[]{:S(2)}, u32[]{:S(2)}) collective-permute-start(bf16[2,32,2048]{2,1,0:T(8,128)(2,1)S(1)} %pad_maximum_fusion.23), channel_id=1, source_target_pairs={{0,12},{4,0},{8,4},{12,8},{1,13},{5,1},{9,5},{13,9},{2,14},{6,2},{... | collective-permute-start | bytes 786440 | tf_op jit(solution)/shard_map/ppermute | solution.py:402
  341.1 21.9 %collective-permute-start.44 = (bf16[128,4224]{1,0:T(8,128)(2,1)S(1)}, bf16[128,4224]{1,0:T(8,128)(2,1)S(1)}, u32[]{:S(2)}, u32[]{:S(2)}) collective-permute-start(bf16[128,4224]{1,0:T(8,128)(2,1)S(1)} %shard_map.163), channel_id=1, source_target_pairs={{0,16},{16,0},{1,17},{17,1},{2,18},{18,2},{3,19},{19,3},{4,20},{20... | collective-permute-start | bytes 3244040 | tf_op jit(solution)/shard_map/ppermute | solution.py:366
  364.5 41.8 %collective-permute-start.48 = (bf16[2,32,4224]{2,1,0:T(8,128)(2,1)S(1)}, bf16[2,32,4224]{2,1,0:T(8,128)(2,1)S(1)}, u32[]{:S(2)}, u32[]{:S(2)}) collective-permute-start(bf16[2,32,4224]{2,1,0:T(8,128)(2,1)S(1)} %pad_maximum_fusion.15), channel_id=1, source_target_pairs={{0,8},{4,12},{8,0},{12,4},{1,9},{5,13},{9,1},{13,5},{2,10},{6,14},... | collective-permute-start | bytes 1622024 | tf_op jit(solution)/shard_map/ppermute | solution.py:402
  368.5 45.8 %collective-permute-start.47 = (bf16[2,32,4224]{2,1,0:T(8,128)(2,1)S(1)}, bf16[2,32,4224]{2,1,0:T(8,128)(2,1)S(1)}, u32[]{:S(2)}, u32[]{:S(2)}) collective-permute-start(bf16[2,32,4224]{2,1,0:T(8,128)(2,1)S(1)} %pad_maximum_fusion.14), channel_id=1, source_target_pairs={{0,12},{4,0},{8,4},{12,8},{1,13},{5,1},{9,5},{13,9},{2,14},{6,2},{... | collective-permute-start | bytes 1622024 | tf_op jit(solution)/shard_map/ppermute | solution.py:402
  (59 other events, 507.6 us)

commit v3 on v2

--- a/solution.py
+++ b/solution.py
@@ -27,6 +27,10 @@
 
 def matmul(left, right):
     return jnp.dot(left, right, preferred_element_type=F32)
+
+
+def tied(*values):
+    return lax.optimization_barrier(values)
 
 
 def swap(value):
@@ -303,21 +307,28 @@
     pieces = [piece]
     for _ in range(1, lax.axis_size(axis)):
         pieces.append(lax.ppermute(pieces[-1], axis, forward(axis)))
-    return jnp.concatenate(pieces, 0)
-
-
-def direct_gather(pair):
-    arrived = [pair] + [
+    return pieces
+
+
+def direct_sends(pair):
+    return [pair] + [
         lax.ppermute(pair, "outer", forward("outer", distance))
         for distance in range(1, lax.axis_size("outer"))
     ]
+
+
+def by_part(arrived):
     return [jnp.concatenate([piece[part] for piece in arrived], 0) for part in range(2)]
 
 
-def gather_rest(parts):
-    one = ring_gather("inner", ring_gather("dp", parts[0]))
-    two = ring_gather("dp", ring_gather("inner", parts[1]))
-    return jnp.concatenate([one, two], 0)
+def gather_near(parts):
+    both = tied(ring_gather("dp", parts[0]), ring_gather("inner", parts[1]))
+    return [jnp.concatenate(pieces, 0) for pieces in both]
+
+
+def gather_far(parts):
+    one, two = tied(ring_gather("inner", parts[0]), ring_gather("dp", parts[1]))
+    return jnp.concatenate(one + two, 0)
 
 
 def chunk_kernel(pairs, *refs):
@@ -360,10 +371,11 @@
     )(*lefts, *rights, *[array for array, _ in adds])
 
 
-def ring(axis, chunk):
+def ring(axis, chunk, first):
     arrived = None
     for step in range(1, lax.axis_size(axis)):
-        arrived = lax.ppermute(chunk(step, arrived), axis, forward(axis))
+        sent = first if step == 1 else chunk(step, arrived)
+        arrived = lax.ppermute(sent, axis, forward(axis))
     return arrived
 
 
@@ -371,38 +383,61 @@
     return [add for add in adds if add[0] is not None]
 
 
-def scatter_grads(lefts, rights, shard_rows):
-    inner, outer, dp = (lax.axis_size(name) for name in ("inner", "outer", "dp"))
-    rows = outer * shard_rows
-    half = inner * dp * rows
-    chunk = functools.partial(grad_chunk, lefts, rights)
-    a_one = ring(
-        "inner", lambda d, got: chunk(d * dp * rows, dp * rows, with_adds((got, 0)))
-    )
-    b_one = ring(
-        "dp",
-        lambda d, got: chunk(half + d * inner * rows, inner * rows, with_adds((got, 0))),
-    )
-    a_two = ring(
-        "dp", lambda d, got: chunk(d * rows, rows, with_adds((a_one, d), (got, 0)))
-    )
-    b_two = ring(
-        "inner", lambda d, got: chunk(half + d * rows, rows, with_adds((b_one, d), (got, 0)))
-    )
-    mine = [
-        chunk(0, rows, with_adds((a_one, 0), (a_two, 0))),
-        chunk(half, rows, with_adds((b_one, 0), (b_two, 0))),
-    ]
-
-    def part(distance):
-        cut = slice(distance * shard_rows, (distance + 1) * shard_rows)
-        return jnp.stack([piece[cut] for piece in mine])
-
-    arrived = [
-        lax.ppermute(part(distance), "outer", forward("outer", outer - distance))
-        for distance in range(1, outer)
-    ]
-    return sum([piece.astype(F32) for piece in arrived], part(0).astype(F32))
+class GradSum:
+    def __init__(self, lefts, rights, shard_rows):
+        self.inner, self.outer, self.dp = (
+            lax.axis_size(name) for name in ("inner", "outer", "dp")
+        )
+        self.shard_rows = shard_rows
+        self.rows = self.outer * shard_rows
+        self.half = self.inner * self.dp * self.rows
+        self.chunk = functools.partial(grad_chunk, lefts, rights)
+
+    def near_chunk(self, part, distance, arrived):
+        rows = (self.inner if part else self.dp) * self.rows
+        return self.chunk(part * self.half + distance * rows, rows, with_adds((arrived, 0)))
+
+    def near(self):
+        return [self.near_chunk(part, 1, None) for part in range(2)]
+
+    def send_near(self, firsts):
+        return tied(
+            *[
+                ring(axis, functools.partial(self.near_chunk, part), firsts[part])
+                for part, axis in enumerate(("inner", "dp"))
+            ]
+        )
+
+    def far_chunk(self, part, distance, arrived):
+        start = part * self.half + distance * self.rows
+        return self.chunk(
+            start, self.rows, with_adds((self.ones[part], distance), (arrived, 0))
+        )
+
+    def far(self, ones):
+        self.ones = ones
+        return [self.far_chunk(part, 1, None) for part in range(2)]
+
+    def send_far(self, firsts):
+        return tied(
+            *[
+                ring(axis, functools.partial(self.far_chunk, part), firsts[part])
+                for part, axis in enumerate(("dp", "inner"))
+            ]
+        )
+
+    def finish(self, twos):
+        mine = [self.far_chunk(part, 0, twos[part]) for part in range(2)]
+
+        def cut(distance):
+            span = slice(distance * self.shard_rows, (distance + 1) * self.shard_rows)
+            return jnp.stack([piece[span] for piece in mine])
+
+        arrived = [
+            lax.ppermute(cut(distance), "outer", forward("outer", self.outer - distance))
+            for distance in range(1, self.outer)
+        ]
+        return sum([piece.astype(F32) for piece in arrived], cut(0).astype(F32))
 
 
 def both_halves(total):
@@ -441,17 +476,18 @@
         return ordered(mine[None], other[None], 0)
 
     gains = jnp.pad(jnp.stack([norm_attn, norm_mlp], 1), ((0, 0), (0, LANES - 2)))
-    one = direct_gather(paired([halves(w_qkv, 3, side), ([gains], [gains])]))
-    pair_two = paired([halves(w_out, 1, side), halves(w_in, 2, padded)])
-    pair_three = paired([halves(w_down, 1, padded)])
-    pair_two, one = lax.optimization_barrier((pair_two, one))
-    two = direct_gather(pair_two)
-    first = gather_rest(one)
-    pair_three, two, first = lax.optimization_barrier((pair_three, two, first))
-    three = direct_gather(pair_three)
-    second = gather_rest(two)
-    three, second = lax.optimization_barrier((three, second))
-    down_half = gather_rest(three)
+    pair_one = paired([halves(w_qkv, 3, side), ([gains], [gains]), halves(w_out, 1, side)])
+    later_in, later_down, pair_one = tied(w_in, w_down, pair_one)
+    one = direct_sends(pair_one)
+    pair_two = paired([halves(later_in, 2, padded)])
+    pair_three = paired([halves(later_down, 1, padded)])
+    pair_two, one = tied(pair_two, one)
+    two = direct_sends(pair_two)
+    first = gather_far(gather_near(by_part(one)))
+    pair_three, two, first = tied(pair_three, two, first)
+    three = direct_sends(pair_three)
+    two = gather_near(by_part(two))
+    in_half = gather_far(two)
     order = arrival_order(width, shard_rows)
 
     def in_order(value):
@@ -491,21 +527,28 @@
     ids_padded = jnp.pad(doc_ids, ((0, 0), (HALF, HALF)), constant_values=-1)
     key_ids = lax.dynamic_slice_in_dim(ids_padded, start, length + 2 * HALF, 1)[:, None, :]
     query_ids = lax.dynamic_slice_in_dim(doc_ids, start, length, 1)[:, :, None]
+    low, high, two = tied(low, high, two)
     attended_half = attend(block, joined, low, high, query_ids, key_ids).reshape(rows, side)
+    three, in_half, attended_half = tied(three, in_half, attended_half)
+    three = gather_near(by_part(three))
     attended_low = ordered(attended_half, swap(attended_half), 1)
-    out_half = second[:, :side]
+    out_half = first[:, 3 * side + LANES :]
     full_out = ordered(out_half, swap(out_half), 1)
     full_out = matmul(order, in_order(full_out)).astype(BF16)
     hidden = values + matmul(attended_low, full_out)
+    three, hidden = tied(three, hidden)
+    down_half = gather_far(three)
     unit_mlp, scale_mlp = normalise(hidden)
     normed_mlp_low = (unit_mlp * gain_mlp).astype(BF16)
-    in_half = second[:, side:]
     expanded = matmul(normed_mlp_low, in_half)
     gate, up = expanded[:, :padded], expanded[:, padded:]
     below = 0.5 * (1.0 + lax.erf(gate * 0.5**0.5))
     active = gate * below
     mixed_low = (active * up).astype(BF16)
 
+    mixed_low, down_half = tied(mixed_low, down_half)
+    sum_down = GradSum([grad_output], [mixed_low], shard_rows)
+    down_ones = sum_down.send_near(sum_down.near())
     grad_mixed = matmul(grad_output, down_half)
     density = jnp.exp(-0.5 * gate * gate) * (2.0 * jnp.pi) ** -0.5
     grad_expanded_low = jnp.concatenate(
@@ -529,11 +572,15 @@
     output = own_rows(hidden)[0] + summed_rows(contract_cols(mixed_low, down_half))
     output = out_of_order(output.astype(BF16).reshape(-1, width)).reshape(tokens.shape)
 
-    mlp_total = scatter_grads(
-        [grad_output, normed_mlp_low], [mixed_low, grad_expanded_low], shard_rows
-    )
-
+    grad_expanded_low, down_ones = tied(grad_expanded_low, down_ones)
+    down_sent = sum_down.far(down_ones)
+    sum_in = GradSum([normed_mlp_low], [grad_expanded_low], shard_rows)
+    in_sent, down_sent, grad_expanded_low = tied(sum_in.near(), down_sent, grad_expanded_low)
+    down_twos = sum_down.send_far(down_sent)
+    in_ones = sum_in.send_near(in_sent)
     grad_normed_mlp = contract_cols(grad_expanded_low, in_half)
+    grad_normed_mlp, down_twos = tied(grad_normed_mlp, down_twos)
+    down_total = sum_down.finish(down_twos)
     grad_normed_mlp = grad_normed_mlp + swap(grad_normed_mlp.astype(BF16)).astype(F32)
     grad_hidden = grad_output.astype(F32) + norm_back(
         unit_mlp, scale_mlp, gain_mlp, grad_normed_mlp
@@ -548,12 +595,19 @@
     )
     from_lower = lax.ppermute(to_upper, ("outer", "inner"), onward)
     from_upper = lax.ppermute(to_lower, ("outer", "inner"), back)
+    from_lower, from_upper, in_ones = tied(from_lower, from_upper, in_ones)
+    in_sent = sum_in.far(in_ones)
+    from_lower, in_sent = tied(from_lower, in_sent)
+    in_twos = sum_in.send_far(in_sent)
     grad_joined = join_grads(grad_query, mid, from_lower, from_upper, cosine, sine)
     grad_joined = grad_joined.reshape(rows, 3 * side)
     hidden_side = lax.dynamic_slice_in_dim(out_of_order(grad_hidden_low), core * side, side, 1)
-    attn_total = scatter_grads(
+    sum_attn = GradSum(
         [normed_low, in_order(attended_low)], [grad_joined, hidden_side], shard_rows
     )
+    attn_sent, in_twos, grad_joined = tied(sum_attn.near(), in_twos, grad_joined)
+    in_total = sum_in.finish(in_twos)
+    attn_ones = sum_attn.send_near(attn_sent)
     grad_normed = summed_rows(contract_cols(grad_joined, first[:, : 3 * side]))
     unit_mine, scale_mine = normalise(own_rows(values)[0])
     grad_tokens = own_rows(grad_hidden)[0] + norm_back(
@@ -567,6 +621,9 @@
         preferred_element_type=F32,
     ).reshape(tokens.shape)
 
+    attn_twos = sum_attn.send_far(sum_attn.far(attn_ones))
+    attn_total = sum_attn.finish(attn_twos)
+
     def interleaved(pair, start, parts, stride, size):
         cuts = []
         for i in range(parts):
@@ -574,9 +631,8 @@
             cuts += [half[:, first_column : first_column + size] for half in pair]
         return jnp.concatenate(cuts, 1)
 
-    pair = both_halves(mlp_total)
-    grad_down = interleaved(pair, 0, 1, padded, units)
-    grad_in = interleaved(pair, padded, 2, padded, units)
+    grad_down = interleaved(both_halves(down_total), 0, 1, padded, units)
+    grad_in = interleaved(both_halves(in_total), 0, 2, padded, units)
     pair = both_halves(attn_total)
     grad_qkv = interleaved(pair, 0, 3, side, side)
     grad_out = interleaved(pair, 3 * side, 1, side, side)

time: 428 us -> 422 us (0.986)
  the two profiles are of different devices: /device:TPU:13 before, /device:TPU:0 now
where the time goes in v3:
time: 422 us; the launch traced here: 414 us
  waiting for transfers between devices  175 us (41%)
  starting transfers between devices  95.5 us (23%)
  other arithmetic  51.8 us (12%)
  matrix products  39.7 us (9%)
  Pallas kernels  39.6 us (9%)
  local copies, waits for them, and re-layouts  9.57 us (2%)
    ppermute x12, waiting for transfers between devices, ring(): arrived = lax.ppermute(sent, axis, forward(axis))  46 us
    ppermute x12, waiting for transfers between devices, ring_gather(): pieces.append(lax.ppermute(pieces[-1], axis, forward(axis)))  41.6 us
    ppermute x9, waiting for transfers between devices, finish(): lax.ppermute(cut(distance), 'outer', forward('outer', self.outer - distan...  35.5 us
    ppermute x9, starting transfers between devices, direct_sends(): lax.ppermute(pair, 'outer', forward('outer', distance))  33.2 us
    ppermute x1, waiting for transfers between devices, shards(): lax.ppermute(joined[:, length - HALF:, side:], ('outer', 'inner'), onward)  26.3 us
    ppermute x9, starting transfers between devices, finish(): lax.ppermute(cut(distance), 'outer', forward('outer', self.outer - distan...  25 us
    dot_general x7, matrix products, matmul(): return jnp.dot(left, right, preferred_element_type=F32)  23.5 us
    concatenate x3, other arithmetic, gather_far(): return jnp.concatenate(one + two, 0)  23.1 us
  transfers between devices with their start and end apart: 59, of which 33 were waited for; matrix products, arithmetic and copies ran while one was open for 18% of the time, Pallas kernels for 8%

profile of v3, /device:TPU:0, one launch (start us, length us, event | category | flops | bytes accessed | tf_op | source)
XLA Modules:
  0.0 413.6 jit_solution(11053796081927278393)
XLA Ops:
  22.2 11.7 %collective-permute-done.4 = bf16[2,32,2176]{2,1,0:T(8,128)(2,1)S(1)} collective-permute-done((bf16[2,32,2176]{2,1,0:T(8,128)(2,1)S(1)}, bf16[2,32,2176]{2,1,0:T(8,128)(2,1)S(1)}, u32[]{:S(2)}, u32[]{:S(2)}) %collective-permute-start.4) | collective-permute-done | bytes 278560 | tf_op jit(solution)/shard_map/ppermute | solution.py:315
  37.3 6.5 %collective-permute-start.6 = (bf16[2,32,2816]{2,1,0:T(8,128)(2,1)S(1)}, bf16[2,32,2816]{2,1,0:T(8,128)(2,1)S(1)}, u32[]{:S(2)}, u32[]{:S(2)}) collective-permute-start(bf16[2,32,2816]{2,1,0:T(8,128)(2,1)S(1)} %pad_maximum_fusion.15), channel_id=1, source_target_pairs={{0,4},{4,8},{8,12},{12,0},{1,5},{5,9},{9,13},{13,1},{2,6},{6,10},{... | collective-permute-start | bytes 1081352 | tf_op jit(solution)/shard_map/ppermute | solution.py:315
  54.2 7.5 %collective-permute-start.8 = (bf16[2,32,2816]{2,1,0:T(8,128)(2,1)S(1)}, bf16[2,32,2816]{2,1,0:T(8,128)(2,1)S(1)}, u32[]{:S(2)}, u32[]{:S(2)}) collective-permute-start(bf16[2,32,2816]{2,1,0:T(8,128)(2,1)S(1)} %pad_maximum_fusion.15), channel_id=1, source_target_pairs={{0,12},{4,0},{8,4},{12,8},{1,13},{5,1},{9,5},{13,9},{2,14},{6,2},{... | collective-permute-start | bytes 1081352 | tf_op jit(solution)/shard_map/ppermute | solution.py:315
  61.9 13.5 %collective-permute-done.11 = bf16[256,2176]{1,0:T(8,128)(2,1)S(1)} collective-permute-done((bf16[256,2176]{1,0:T(8,128)(2,1)S(1)}, bf16[256,2176]{1,0:T(8,128)(2,1)S(1)}, u32[]{:S(2)}, u32[]{:S(2)}) %collective-permute-start.11) | collective-permute-done | bytes 1114144 | tf_op jit(solution)/shard_map/ppermute | solution.py:309
  76.9 6.7 %pad_maximum_fusion.1.weight_ref = bf16[1024,2176]{1,0:T(8,128)(2,1)S(1)} fusion(bf16[256,2176]{1,0:T(8,128)(2,1)S(1)} %collective-permute-done.12, bf16[256,2176]{1,0:T(8,128)(2,1)S(1)} %constant_dynamic-update-slice_fusion.12, bf16[256,2176]{1,0:T(8,128)(2,1)S(1)} %collective-permute-done.11, bf16[256,2176]{1,0:T(8,128)(2,1)S(1)} %constant_dynamic-update-slice_fusion.10), kind=kLoop, calls=%fused_computation.1 | loop fusion | flops 17825792 | bytes 8912896 | tf_op jit(solution)/shard_map/concatenate | solution.py:331
  87.9 11.6 %collective-permute-done.16 = bf16[128,2816]{1,0:T(8,128)(2,1)S(1)} collective-permute-done((bf16[128,2816]{1,0:T(8,128)(2,1)S(1)}, bf16[128,2816]{1,0:T(8,128)(2,1)S(1)}, u32[]{:S(2)}, u32[]{:S(2)}) %collective-permute-start.16) | collective-permute-done | bytes 720928 | tf_op jit(solution)/shard_map/ppermute | solution.py:309
  103.7 4.4 %shard_map.152 = bf16[512,1536]{1,0:T(8,128)(2,1)S(1)} custom-call(bf16[512,1024]{1,0:T(8,128)(2,1)S(1)} %multiply_convert_fusion.3.normed_ref.refs_0_, bf16[1024,2176]{1,0:T(8,128)(2,1)S(1)} %pad_maximum_fusion.1.weight_ref, f32[512,256]{1,0:T(8,128)S(1)} %copy-done.4, f32[512,256]{1,0:T(8,128)S(1)} %get-tuple-element.298.sin_ref), custom_call_target="tpu_custom_call" | custom-call | flops 1024 | bytes 1024 | tf_op jit(solution)/shard_map/pallas_call | solution.py:80
  108.2 3.4 collective-permute-start.21
  113.8 26.3 %collective-permute-done.21.kl_ref.vl_ref = bf16[2,64,1024]{2,1,0:T(8,128)(2,1)S(1)} collective-permute-done((bf16[2,64,1024]{2,1,0:T(8,128)(2,1)S(1)}, bf16[2,64,1024]{2,1,0:T(8,128)(2,1)S(1)}, u32[]{:S(2)}, u32[]{:S(2)}) %collective-permute-start.21) | collective-permute-done | bytes 262176 | tf_op jit(solution)/shard_map/ppermute | solution.py:525
  140.0 6.7 %collective-permute-start.13 = (bf16[2,32,1408]{2,1,0:T(8,128)(2,1)S(1)}, bf16[2,32,1408]{2,1,0:T(8,128)(2,1)S(1)}, u32[]{:S(2)}, u32[]{:S(2)}) collective-permute-start(bf16[2,32,1408]{2,1,0:T(8,128)(2,1)S(1)} %pad_maximum_fusion.26), channel_id=1, source_target_pairs={{0,4},{4,8},{8,12},{12,0},{1,5},{5,9},{9,13},{13,1},{2,6},{6,10},{... | collective-permute-start | bytes 540680 | tf_op jit(solution)/shard_map/ppermute | solution.py:315
  147.6 8.8 %shard_map.153 = bf16[2,256,512]{2,1,0:T(8,128)(2,1)} custom-call(bf16[2,256,1536]{2,1,0:T(8,128)(2,1)S(1)} %bitcast.209, bf16[2,256,1536]{2,1,0:T(8,128)(2,1)S(1)} %bitcast.210, bf16[2,256,1536]{2,1,0:T(8,128)(2,1)S(1)} %bitcast.211, bf16[2,64,1024]{2,1,0:T(8,128)(2,1)S(1)} %collective-permute-done.21.kl_ref.vl_ref, ...), custom_call_target="tpu_custom_call" | custom-call | flops 1024 | bytes 1024 | tf_op jit(solution)/shard_map/pallas_call | solution.py:199
  156.4 3.4 collective-permute-start.15
  161.3 11.4 %pad_maximum_fusion = bf16[1024,2816]{1,0:T(8,128)(2,1)} fusion(bf16[256,2816]{1,0:T(8,128)(2,1)S(1)} %collective-permute-done.19, bf16[256,2816]{1,0:T(8,128)(2,1)S(1)} %constant_dynamic-update-slice_fusion.16, bf16[256,2816]{1,0:T(8,128)(2,1)S(1)} %collective-permute-done.18, bf16[256,2816]{1,0:T(8,128)(2,1)S(1)} %constant_dynamic-update-slice_fusion.14), kind=kLoop, calls=%fused_computation | loop fusion | flops 23068672 | bytes 11534336 | tf_op jit(solution)/shard_map/concatenate | solution.py:331
  176.4 7.4 %fusion.30 = bf16[1024,1024]{1,0:T(8,128)(2,1)} fusion(s32[1024]{0:T(1024)} %copy-done.29, bf16[1024,512]{1,0:T(8,128)(2,1)} %get-tuple-element.197, bf16[1024,512]{1,0:T(8,128)(2,1)} %get-tuple-element.196), kind=kOutput, calls=%fused_computation.49 | convolution fusion | flops 4303355904 | bytes 4198400 | tf_op jit(solution)/shard_map/dot_general | solution.py:29
  200.3 5.9 %fusion.111 = f32[512,2816]{1,0:T(8,128)S(1)} fusion(bf16[512,1024]{1,0:T(8,128)(2,1)S(1)} %multiply_convert_fusion.2.refs_0_, bf16[1024,2816]{1,0:T(8,128)(2,1)} %pad_maximum_fusion), kind=kOutput, calls=%fused_computation.323 | convolution fusion | flops 2952790016 | bytes 12582912 | tf_op jit(solution)/shard_map/dot_general | solution.py:29
  208.3 8.4 %collective-permute-done.27 = bf16[256,1408]{1,0:T(8,128)(2,1)S(1)} collective-permute-done((bf16[256,1408]{1,0:T(8,128)(2,1)}, bf16[256,1408]{1,0:T(8,128)(2,1)S(1)}, u32[]{:S(2)}, u32[]{:S(2)}) %collective-permute-start.27) | collective-permute-done | bytes 720928 | tf_op jit(solution)/shard_map/ppermute | solution.py:309
  217.9 5.1 %pad_maximum_fusion.2 = bf16[1024,1408]{1,0:T(8,128)(2,1)S(1)} fusion(bf16[256,1408]{1,0:T(8,128)(2,1)S(1)} %collective-permute-done.28, bf16[256,1408]{1,0:T(8,128)(2,1)S(1)} %copy-done.11, bf16[256,1408]{1,0:T(8,128)(2,1)S(1)} %collective-permute-done.27, bf16[256,1408]{1,0:T(8,128)(2,1)S(1)} %copy-done.10), kind=kLoop, calls=%fused_computation.21 | loop fusion | flops 11534336 | bytes 5767168 | tf_op jit(solution)/shard_map/concatenate | solution.py:331
  230.5 14.3 %collective-permute-done.31.refs_2_ = bf16[256,1408]{1,0:T(8,128)(2,1)S(1)} collective-permute-done((bf16[256,1408]{1,0:T(8,128)(2,1)S(1)}, bf16[256,1408]{1,0:T(8,128)(2,1)S(1)}, u32[]{:S(2)}, u32[]{:S(2)}) %collective-permute-start.31) | collective-permute-done | bytes 720928 | tf_op jit(solution)/shard_map/ppermute | solution.py:378
  249.9 5.2 %fusion.113 = f32[512,1024]{1,0:T(8,128)S(1)} fusion(bf16[512,2816]{1,0:T(8,128)(2,1)S(1)} %pad_maximum_fusion.3.refs_1_, bf16[1024,2816]{1,0:T(8,128)(2,1)} %pad_maximum_fusion), kind=kOutput, calls=%fused_computation.325 | convolution fusion | flops 2952790016 | bytes 10747904 | tf_op jit(solution)/shard_map/dot_general | solution.py:21
  270.8 5.3 %collective-permute-done.56 = bf16[2,32,1408]{2,1,0:T(8,128)(2,1)S(1)} collective-permute-done((bf16[2,32,1408]{2,1,0:T(8,128)(2,1)S(1)}, bf16[2,32,1408]{2,1,0:T(8,128)(2,1)S(1)}, u32[]{:S(2)}, u32[]{:S(2)}) %collective-permute-start.56) | collective-permute-done | bytes 180256 | tf_op jit(solution)/shard_map/ppermute | solution.py:437
  279.6 14.8 %shard_map.160 = (bf16[2,256,512]{2,1,0:T(8,128)(2,1)S(1)}, f32[2,2,256,512]{3,2,1,0:T(8,128)S(1)}, bf16[2,2,64,512]{3,2,1,0:T(8,128)(2,1)S(1)}, bf16[2,2,64,512]{3,2,1,0:T(8,128)(2,1)S(1)}) custom-call(bf16[2,256,1536]{2,1,0:T(8,128)(2,1)S(1)} %bitcast.212, bf16[2,256,1536]{2,1,0:T(8,128)(2,1)S(1)} %bitcast.213, bf16[2,256,1536]{2,1,0:T(8,128)(2,1)S(1)} %bitcast.214, ...), custom_call_target="tpu_custom_call" | custom-call | flops 1024 | bytes 1024 | tf_op jit(solution)/shard_map/pallas_call | solution.py:220
  304.0 6.3 %collective-permute-done.37.high_ref = bf16[2,2,64,512]{3,2,1,0:T(8,128)(2,1)S(1)} collective-permute-done((bf16[2,2,64,512]{3,2,1,0:T(8,128)(2,1)S(1)}, bf16[2,2,64,512]{3,2,1,0:T(8,128)(2,1)S(1)}, u32[]{:S(2)}, u32[]{:S(2)}) %collective-permute-start.37) | collective-permute-done | bytes 262176 | tf_op jit(solution)/shard_map/ppermute | solution.py:597
  320.4 9.1 %collective-permute-done.40.refs_3_ = bf16[128,2816]{1,0:T(8,128)(2,1)S(1)} collective-permute-done((bf16[128,2816]{1,0:T(8,128)(2,1)S(1)}, bf16[128,2816]{1,0:T(8,128)(2,1)S(1)}, u32[]{:S(2)}, u32[]{:S(2)}) %collective-permute-start.40) | collective-permute-done | bytes 720928 | tf_op jit(solution)/shard_map/ppermute | solution.py:378
  332.7 5.0 %collective-permute-start.53 = (bf16[2,32,2816]{2,1,0:T(8,128)(2,1)S(1)}, bf16[2,32,2816]{2,1,0:T(8,128)(2,1)S(1)}, u32[]{:S(2)}, u32[]{:S(2)}) collective-permute-start(bf16[2,32,2816]{2,1,0:T(8,128)(2,1)S(1)} %pad_maximum_fusion.20), channel_id=1, source_target_pairs={{0,4},{4,8},{8,12},{12,0},{1,5},{5,9},{9,13},{13,1},{2,6},{6,10},{... | collective-permute-start | bytes 1081352 | tf_op jit(solution)/shard_map/ppermute | solution.py:437
  343.1 3.9 collective-permute-done.53
  347.5 13.1 %collective-permute-done.52 = bf16[2,32,2816]{2,1,0:T(8,128)(2,1)S(1)} collective-permute-done((bf16[2,32,2816]{2,1,0:T(8,128)(2,1)S(1)}, bf16[2,32,2816]{2,1,0:T(8,128)(2,1)S(1)}, u32[]{:S(2)}, u32[]{:S(2)}) %collective-permute-start.52) | collective-permute-done | bytes 360480 | tf_op jit(solution)/shard_map/ppermute | solution.py:437
  361.4 3.5 fusion.8
  364.9 3.4 collective-permute-done.43.refs_4_
  371.8 10.6 %collective-permute-done.45.refs_5_ = bf16[128,2048]{1,0:T(8,128)(2,1)S(1)} collective-permute-done((bf16[128,2048]{1,0:T(8,128)(2,1)S(1)}, bf16[128,2048]{1,0:T(8,128)(2,1)S(1)}, u32[]{:S(2)}, u32[]{:S(2)}) %collective-permute-start.45) | collective-permute-done | bytes 524320 | tf_op jit(solution)/shard_map/ppermute | solution.py:378
  384.3 5.7 %collective-permute-start.49 = (bf16[2,32,2048]{2,1,0:T(8,128)(2,1)S(1)}, bf16[2,32,2048]{2,1,0:T(8,128)(2,1)S(1)}, u32[]{:S(2)}, u32[]{:S(2)}) collective-permute-start(bf16[2,32,2048]{2,1,0:T(8,128)(2,1)S(1)} %pad_maximum_fusion.25), channel_id=1, source_target_pairs={{0,4},{4,8},{8,12},{12,0},{1,5},{5,9},{9,13},{13,1},{2,6},{6,10},{... | collective-permute-start | bytes 786440 | tf_op jit(solution)/shard_map/ppermute | solution.py:437
  390.0 4.3 %collective-permute-start.48 = (bf16[2,32,2048]{2,1,0:T(8,128)(2,1)S(1)}, bf16[2,32,2048]{2,1,0:T(8,128)(2,1)S(1)}, u32[]{:S(2)}, u32[]{:S(2)}) collective-permute-start(bf16[2,32,2048]{2,1,0:T(8,128)(2,1)S(1)} %pad_maximum_fusion.24), channel_id=1, source_target_pairs={{0,8},{4,12},{8,0},{12,4},{1,9},{5,13},{9,1},{13,5},{2,10},{6,14},... | collective-permute-start | bytes 786440 | tf_op jit(solution)/shard_map/ppermute | solution.py:437
  399.3 9.7 %collective-permute-done.48 = bf16[2,32,2048]{2,1,0:T(8,128)(2,1)S(1)} collective-permute-done((bf16[2,32,2048]{2,1,0:T(8,128)(2,1)S(1)}, bf16[2,32,2048]{2,1,0:T(8,128)(2,1)S(1)}, u32[]{:S(2)}, u32[]{:S(2)}) %collective-permute-start.48) | collective-permute-done | bytes 262176 | tf_op jit(solution)/shard_map/ppermute | solution.py:437
  (335 shorter events, 148.6 us)
Async XLA Ops:
  6.4 37.4 %collective-permute-start.20 = (bf16[2,128,1024]{2,1,0:T(8,128)(2,1)}, bf16[2,128,1024]{2,1,0:T(8,128)(2,1)S(1)}, u32[]{:S(2)}, u32[]{:S(2)}) collective-permute-start(bf16[2,128,1024]{2,1,0:T(8,128)(2,1)} %param.9), channel_id=1, source_target_pairs={{0,1},{1,0},{2,3},{3,2},{4,5},{5,4},{6,7},{7,6},{8,9},{9,8},{10,11... | collective-permute-start | bytes 1572872 | tf_op jit(solution)/shard_map/ppermute | solution.py:37
  6.5 47.7 %collective-permute-start.30 = (bf16[2,128,1024]{2,1,0:T(8,128)(2,1)}, bf16[2,128,1024]{2,1,0:T(8,128)(2,1)S(1)}, u32[]{:S(2)}, u32[]{:S(2)}) collective-permute-start(bf16[2,128,1024]{2,1,0:T(8,128)(2,1)} %param.17), channel_id=1, source_target_pairs={{0,1},{1,0},{2,3},{3,2},{4,5},{5,4},{6,7},{7,6},{8,9},{9,8},{10,11... | collective-permute-start | bytes 1572872 | tf_op jit(solution)/shard_map/ppermute | solution.py:37
  12.6 21.3 %collective-permute-start.4 = (bf16[2,32,2176]{2,1,0:T(8,128)(2,1)S(1)}, bf16[2,32,2176]{2,1,0:T(8,128)(2,1)S(1)}, u32[]{:S(2)}, u32[]{:S(2)}) collective-permute-start(bf16[2,32,2176]{2,1,0:T(8,128)(2,1)S(1)} %pad_maximum_fusion.22), channel_id=1, source_target_pairs={{0,8},{4,12},{8,0},{12,4},{1,9},{5,13},{9,1},{13,5},{2,10},{6,14},... | collective-permute-start | bytes 835592 | tf_op jit(solution)/shard_map/ppermute | solution.py:315
  37.3 46.2 %collective-permute-start.6 = (bf16[2,32,2816]{2,1,0:T(8,128)(2,1)S(1)}, bf16[2,32,2816]{2,1,0:T(8,128)(2,1)S(1)}, u32[]{:S(2)}, u32[]{:S(2)}) collective-permute-start(bf16[2,32,2816]{2,1,0:T(8,128)(2,1)S(1)} %pad_maximum_fusion.15), channel_id=1, source_target_pairs={{0,4},{4,8},{8,12},{12,0},{1,5},{5,9},{9,13},{13,1},{2,6},{6,10},{... | collective-permute-start | bytes 1081352 | tf_op jit(solution)/shard_map/ppermute | solution.py:315
  43.8 39.7 %collective-permute-start.7 = (bf16[2,32,2816]{2,1,0:T(8,128)(2,1)S(1)}, bf16[2,32,2816]{2,1,0:T(8,128)(2,1)S(1)}, u32[]{:S(2)}, u32[]{:S(2)}) collective-permute-start(bf16[2,32,2816]{2,1,0:T(8,128)(2,1)S(1)} %pad_maximum_fusion.15), channel_id=1, source_target_pairs={{0,8},{4,12},{8,0},{12,4},{1,9},{5,13},{9,1},{13,5},{2,10},{6,14},... | collective-permute-start | bytes 1081352 | tf_op jit(solution)/shard_map/ppermute | solution.py:315
  50.1 25.3 %collective-permute-start.11 = (bf16[256,2176]{1,0:T(8,128)(2,1)S(1)}, bf16[256,2176]{1,0:T(8,128)(2,1)S(1)}, u32[]{:S(2)}, u32[]{:S(2)}) collective-permute-start(bf16[256,2176]{1,0:T(8,128)(2,1)S(1)} %constant_dynamic-update-slice_fusion.10), channel_id=1, source_target_pairs={{0,2},{2,0},{1,3},{3,1},{4,6},{6,4},{5,7},{7,5},{8,10},{10,8},{9,1... | collective-permute-start | bytes 3342344 | tf_op jit(solution)/shard_map/ppermute | solution.py:309
  51.8 25.1 %collective-permute-start.12 = (bf16[256,2176]{1,0:T(8,128)(2,1)S(1)}, bf16[256,2176]{1,0:T(8,128)(2,1)S(1)}, u32[]{:S(2)}, u32[]{:S(2)}) collective-permute-start(bf16[256,2176]{1,0:T(8,128)(2,1)S(1)} %constant_dynamic-update-slice_fusion.12), channel_id=1, source_target_pairs={{0,16},{16,0},{1,17},{17,1},{2,18},{18,2},{3,19},{19,3},{4,20},{20... | collective-permute-start | bytes 3342344 | tf_op jit(solution)/shard_map/ppermute | solution.py:309
  54.2 29.3 %collective-permute-start.8 = (bf16[2,32,2816]{2,1,0:T(8,128)(2,1)S(1)}, bf16[2,32,2816]{2,1,0:T(8,128)(2,1)S(1)}, u32[]{:S(2)}, u32[]{:S(2)}) collective-permute-start(bf16[2,32,2816]{2,1,0:T(8,128)(2,1)S(1)} %pad_maximum_fusion.15), channel_id=1, source_target_pairs={{0,12},{4,0},{8,4},{12,8},{1,13},{5,1},{9,5},{13,9},{2,14},{6,2},{... | collective-permute-start | bytes 1081352 | tf_op jit(solution)/shard_map/ppermute | solution.py:315
  87.8 68.6 %collective-permute-start.26 = (bf16[1024,512]{1,0:T(8,128)(2,1)S(1)}, bf16[1024,512]{1,0:T(8,128)(2,1)S(1)}, u32[]{:S(2)}, u32[]{:S(2)}) collective-permute-start(bf16[1024,512]{1,0:T(8,128)(2,1)S(1)} %slice.295), channel_id=1, source_target_pairs={{0,1},{1,0},{2,3},{3,2},{4,5},{5,4},{6,7},{7,6},{8,9},{9,8},{10,11... | collective-permute-start | bytes 3145736 | tf_op jit(solution)/shard_map/ppermute | solution.py:37
  100.7 60.6 %collective-permute-start.18 = (bf16[256,2816]{1,0:T(8,128)(2,1)S(1)}, bf16[256,2816]{1,0:T(8,128)(2,1)S(1)}, u32[]{:S(2)}, u32[]{:S(2)}) collective-permute-start(bf16[256,2816]{1,0:T(8,128)(2,1)S(1)} %constant_dynamic-update-slice_fusion.14), channel_id=1, source_target_pairs={{0,2},{2,0},{1,3},{3,1},{4,6},{6,4},{5,7},{7,5},{8,10},{10,8},{9,1... | collective-permute-start | bytes 4325384 | tf_op jit(solution)/shard_map/ppermute | solution.py:309
  101.4 59.8 %collective-permute-start.19 = (bf16[256,2816]{1,0:T(8,128)(2,1)S(1)}, bf16[256,2816]{1,0:T(8,128)(2,1)S(1)}, u32[]{:S(2)}, u32[]{:S(2)}) collective-permute-start(bf16[256,2816]{1,0:T(8,128)(2,1)S(1)} %constant_dynamic-update-slice_fusion.16), channel_id=1, source_target_pairs={{0,16},{16,0},{1,17},{17,1},{2,18},{18,2},{3,19},{19,3},{4,20},{20... | collective-permute-start | bytes 4325384 | tf_op jit(solution)/shard_map/ppermute | solution.py:309
  108.2 31.8 %collective-permute-start.21 = (bf16[2,64,1024]{2,1,0:T(8,128)(2,1)S(1)}, bf16[2,64,1024]{2,1,0:T(8,128)(2,1)S(1)}, u32[]{:S(2)}, u32[]{:S(2)}) collective-permute-start(bf16[2,64,1024]{2,1,0:T(8,128)(2,1)S(1)} %get-tuple-element.199), channel_id=1, source_target_pairs={{0,2},{2,4},{4,6},{6,8},{8,10},{10,12},{12,14},{1,3},{3,5},{5,7},{... | collective-permute-start | bytes 786440 | tf_op jit(solution)/shard_map/ppermute | solution.py:525
  111.6 35.1 %collective-permute-start.22 = (bf16[2,64,1024]{2,1,0:T(8,128)(2,1)S(1)}, bf16[2,64,1024]{2,1,0:T(8,128)(2,1)S(1)}, u32[]{:S(2)}, u32[]{:S(2)}) collective-permute-start(bf16[2,64,1024]{2,1,0:T(8,128)(2,1)S(1)} %get-tuple-element.198), channel_id=1, source_target_pairs={{2,0},{4,2},{6,4},{8,6},{10,8},{12,10},{14,12},{3,1},{5,3},{7,5},{... | collective-permute-start | bytes 786440 | tf_op jit(solution)/shard_map/ppermute | solution.py:526
  140.0 32.6 %collective-permute-start.13 = (bf16[2,32,1408]{2,1,0:T(8,128)(2,1)S(1)}, bf16[2,32,1408]{2,1,0:T(8,128)(2,1)S(1)}, u32[]{:S(2)}, u32[]{:S(2)}) collective-permute-start(bf16[2,32,1408]{2,1,0:T(8,128)(2,1)S(1)} %pad_maximum_fusion.26), channel_id=1, source_target_pairs={{0,4},{4,8},{8,12},{12,0},{1,5},{5,9},{9,13},{13,1},{2,6},{6,10},{... | collective-permute-start | bytes 540680 | tf_op jit(solution)/shard_map/ppermute | solution.py:315
  146.7 25.9 %collective-permute-start.14 = (bf16[2,32,1408]{2,1,0:T(8,128)(2,1)S(1)}, bf16[2,32,1408]{2,1,0:T(8,128)(2,1)S(1)}, u32[]{:S(2)}, u32[]{:S(2)}) collective-permute-start(bf16[2,32,1408]{2,1,0:T(8,128)(2,1)S(1)} %pad_maximum_fusion.26), channel_id=1, source_target_pairs={{0,8},{4,12},{8,0},{12,4},{1,9},{5,13},{9,1},{13,5},{2,10},{6,14},... | collective-permute-start | bytes 540680 | tf_op jit(solution)/shard_map/ppermute | solution.py:315
  156.4 16.2 %collective-permute-start.15 = (bf16[2,32,1408]{2,1,0:T(8,128)(2,1)S(1)}, bf16[2,32,1408]{2,1,0:T(8,128)(2,1)S(1)}, u32[]{:S(2)}, u32[]{:S(2)}) collective-permute-start(bf16[2,32,1408]{2,1,0:T(8,128)(2,1)S(1)} %pad_maximum_fusion.26), channel_id=1, source_target_pairs={{0,12},{4,0},{8,4},{12,8},{1,13},{5,1},{9,5},{13,9},{2,14},{6,2},{... | collective-permute-start | bytes 540680 | tf_op jit(solution)/shard_map/ppermute | solution.py:315
  197.9 18.8 %collective-permute-start.27 = (bf16[256,1408]{1,0:T(8,128)(2,1)}, bf16[256,1408]{1,0:T(8,128)(2,1)S(1)}, u32[]{:S(2)}, u32[]{:S(2)}) collective-permute-start(bf16[256,1408]{1,0:T(8,128)(2,1)} %pad_maximum_fusion.9), channel_id=1, source_target_pairs={{0,2},{2,0},{1,3},{3,1},{4,6},{6,4},{5,7},{7,5},{8,10},{10,8},{9,1... | collective-permute-start | bytes 2162696 | tf_op jit(solution)/shard_map/ppermute | solution.py:309
  199.4 18.5 %collective-permute-start.28 = (bf16[256,1408]{1,0:T(8,128)(2,1)}, bf16[256,1408]{1,0:T(8,128)(2,1)S(1)}, u32[]{:S(2)}, u32[]{:S(2)}) collective-permute-start(bf16[256,1408]{1,0:T(8,128)(2,1)} %pad_maximum_fusion.10), channel_id=1, source_target_pairs={{0,16},{16,0},{1,17},{17,1},{2,18},{18,2},{3,19},{19,3},{4,20},{20... | collective-permute-start | bytes 2162696 | tf_op jit(solution)/shard_map/ppermute | solution.py:309
  226.2 18.6 %collective-permute-start.31 = (bf16[256,1408]{1,0:T(8,128)(2,1)S(1)}, bf16[256,1408]{1,0:T(8,128)(2,1)S(1)}, u32[]{:S(2)}, u32[]{:S(2)}) collective-permute-start(bf16[256,1408]{1,0:T(8,128)(2,1)S(1)} %shard_map.154), channel_id=1, source_target_pairs={{0,2},{2,0},{1,3},{3,1},{4,6},{6,4},{5,7},{7,5},{8,10},{10,8},{9,1... | collective-permute-start | bytes 2162696 | tf_op jit(solution)/shard_map/ppermute | solution.py:378
  226.9 18.2 %collective-permute-start.32 = (bf16[256,1408]{1,0:T(8,128)(2,1)S(1)}, bf16[256,1408]{1,0:T(8,128)(2,1)S(1)}, u32[]{:S(2)}, u32[]{:S(2)}) collective-permute-start(bf16[256,1408]{1,0:T(8,128)(2,1)S(1)} %shard_map.155), channel_id=1, source_target_pairs={{0,16},{16,0},{1,17},{17,1},{2,18},{18,2},{3,19},{19,3},{4,20},{20... | collective-permute-start | bytes 2162696 | tf_op jit(solution)/shard_map/ppermute | solution.py:378
  259.0 17.4 %collective-permute-start.35 = (bf16[512,1024]{1,0:T(8,128)(2,1)}, bf16[512,1024]{1,0:T(8,128)(2,1)S(1)}, u32[]{:S(2)}, u32[]{:S(2)}) collective-permute-start(bf16[512,1024]{1,0:T(8,128)(2,1)} %convert_element_type.186), channel_id=1, source_target_pairs={{0,1},{1,0},{2,3},{3,2},{4,5},{5,4},{6,7},{7,6},{8,9},{9,8},{10,11... | collective-permute-start | bytes 3145736 | tf_op jit(solution)/shard_map/ppermute | solution.py:37
  266.0 33.4 %collective-permute-start.38 = (bf16[256,2816]{1,0:T(8,128)(2,1)S(1)}, bf16[256,2816]{1,0:T(8,128)(2,1)S(1)}, u32[]{:S(2)}, u32[]{:S(2)}) collective-permute-start(bf16[256,2816]{1,0:T(8,128)(2,1)S(1)} %shard_map.156), channel_id=1, source_target_pairs={{0,2},{2,0},{1,3},{3,1},{4,6},{6,4},{5,7},{7,5},{8,10},{10,8},{9,1... | collective-permute-start | bytes 4325384 | tf_op jit(solution)/shard_map/ppermute | solution.py:378
  269.3 32.8 %collective-permute-start.39 = (bf16[256,2816]{1,0:T(8,128)(2,1)S(1)}, bf16[256,2816]{1,0:T(8,128)(2,1)S(1)}, u32[]{:S(2)}, u32[]{:S(2)}) collective-permute-start(bf16[256,2816]{1,0:T(8,128)(2,1)S(1)} %shard_map.157), channel_id=1, source_target_pairs={{0,16},{16,0},{1,17},{17,1},{2,18},{18,2},{3,19},{19,3},{4,20},{20... | collective-permute-start | bytes 4325384 | tf_op jit(solution)/shard_map/ppermute | solution.py:378
  276.3 22.7 %collective-permute-start.58 = (f32[32,1408]{1,0:T(8,128)S(1)}, f32[32,1408]{1,0:T(8,128)S(1)}, u32[]{:S(2)}, u32[]{:S(2)}) collective-permute-start(f32[32,1408]{1,0:T(8,128)S(1)} %get-tuple-element.233), channel_id=1, source_target_pairs={{0,1},{1,0},{2,3},{3,2},{4,5},{5,4},{6,7},{7,6},{8,9},{9,8},{10,11... | collective-permute-start | bytes 540680 | tf_op jit(solution)/shard_map/ppermute | solution.py:37
  311.6 17.8 %collective-permute-start.40 = (bf16[128,2816]{1,0:T(8,128)(2,1)S(1)}, bf16[128,2816]{1,0:T(8,128)(2,1)S(1)}, u32[]{:S(2)}, u32[]{:S(2)}) collective-permute-start(bf16[128,2816]{1,0:T(8,128)(2,1)S(1)} %shard_map.161), channel_id=1, source_target_pairs={{0,16},{16,0},{1,17},{17,1},{2,18},{18,2},{3,19},{19,3},{4,20},{20... | collective-permute-start | bytes 2162696 | tf_op jit(solution)/shard_map/ppermute | solution.py:378
  313.2 18.0 %collective-permute-start.41 = (bf16[128,2816]{1,0:T(8,128)(2,1)S(1)}, bf16[128,2816]{1,0:T(8,128)(2,1)S(1)}, u32[]{:S(2)}, u32[]{:S(2)}) collective-permute-start(bf16[128,2816]{1,0:T(8,128)(2,1)S(1)} %shard_map.162), channel_id=1, source_target_pairs={{0,2},{2,0},{1,3},{3,1},{4,6},{6,4},{5,7},{7,5},{8,10},{10,8},{9,1... | collective-permute-start | bytes 2162696 | tf_op jit(solution)/shard_map/ppermute | solution.py:378
  337.7 22.8 %collective-permute-start.52 = (bf16[2,32,2816]{2,1,0:T(8,128)(2,1)S(1)}, bf16[2,32,2816]{2,1,0:T(8,128)(2,1)S(1)}, u32[]{:S(2)}, u32[]{:S(2)}) collective-permute-start(bf16[2,32,2816]{2,1,0:T(8,128)(2,1)S(1)} %pad_maximum_fusion.19), channel_id=1, source_target_pairs={{0,8},{4,12},{8,0},{12,4},{1,9},{5,13},{9,1},{13,5},{2,10},{6,14},... | collective-permute-start | bytes 1081352 | tf_op jit(solution)/shard_map/ppermute | solution.py:437
  338.2 22.3 %collective-permute-start.51 = (bf16[2,32,2816]{2,1,0:T(8,128)(2,1)S(1)}, bf16[2,32,2816]{2,1,0:T(8,128)(2,1)S(1)}, u32[]{:S(2)}, u32[]{:S(2)}) collective-permute-start(bf16[2,32,2816]{2,1,0:T(8,128)(2,1)S(1)} %pad_maximum_fusion.18), channel_id=1, source_target_pairs={{0,12},{4,0},{8,4},{12,8},{1,13},{5,1},{9,5},{13,9},{2,14},{6,2},{... | collective-permute-start | bytes 1081352 | tf_op jit(solution)/shard_map/ppermute | solution.py:437
  342.6 18.2 %collective-permute-start.42 = (bf16[2,128,1024]{2,1,0:T(8,128)(2,1)S(1)}, bf16[2,128,1024]{2,1,0:T(8,128)(2,1)S(1)}, u32[]{:S(2)}, u32[]{:S(2)}) collective-permute-start(bf16[2,128,1024]{2,1,0:T(8,128)(2,1)S(1)} %fusion.55), channel_id=1, source_target_pairs={{0,1},{1,0},{2,3},{3,2},{4,5},{5,4},{6,7},{7,6},{8,9},{9,8},{10,11... | collective-permute-start | bytes 1572872 | tf_op jit(solution)/shard_map/ppermute | solution.py:37
  342.7 25.6 %collective-permute-start.43 = (bf16[256,2048]{1,0:T(8,128)(2,1)S(1)}, bf16[256,2048]{1,0:T(8,128)(2,1)S(1)}, u32[]{:S(2)}, u32[]{:S(2)}) collective-permute-start(bf16[256,2048]{1,0:T(8,128)(2,1)S(1)} %shard_map.164), channel_id=1, source_target_pairs={{0,2},{2,0},{1,3},{3,1},{4,6},{6,4},{5,7},{7,5},{8,10},{10,8},{9,1... | collective-permute-start | bytes 3145736 | tf_op jit(solution)/shard_map/ppermute | solution.py:378
  346.9 21.4 %collective-permute-start.44 = (bf16[256,2048]{1,0:T(8,128)(2,1)S(1)}, bf16[256,2048]{1,0:T(8,128)(2,1)S(1)}, u32[]{:S(2)}, u32[]{:S(2)}) collective-permute-start(bf16[256,2048]{1,0:T(8,128)(2,1)S(1)} %shard_map.165), channel_id=1, source_target_pairs={{0,16},{16,0},{1,17},{17,1},{2,18},{18,2},{3,19},{19,3},{4,20},{20... | collective-permute-start | bytes 3145736 | tf_op jit(solution)/shard_map/ppermute | solution.py:378
  390.0 19.0 %collective-permute-start.48 = (bf16[2,32,2048]{2,1,0:T(8,128)(2,1)S(1)}, bf16[2,32,2048]{2,1,0:T(8,128)(2,1)S(1)}, u32[]{:S(2)}, u32[]{:S(2)}) collective-permute-start(bf16[2,32,2048]{2,1,0:T(8,128)(2,1)S(1)} %pad_maximum_fusion.24), channel_id=1, source_target_pairs={{0,8},{4,12},{8,0},{12,4},{1,9},{5,13},{9,1},{13,5},{2,10},{6,14},... | collective-permute-start | bytes 786440 | tf_op jit(solution)/shard_map/ppermute | solution.py:437
  (63 other events, 773.1 us)

commit v4 on v2

v4 whole, which is shorter than its diff:
```python
import functools

import jax
import jax.numpy as jnp
import numpy as np
from jax import lax
from jax.experimental import pallas as pl
from jax.experimental.pallas import tpu as pltpu
from jax.sharding import Mesh, PartitionSpec as P

HD = 64
HALF = 64
LANES = 128
NORM_EPSILON = 1e-05
ROPE_BASE = 10000.0
F32 = jnp.float32
BF16 = jnp.bfloat16


def contract_cols(left, right):
    return lax.dot_general(left, right, (((1,), (1,)), ((), ())), preferred_element_type=F32)


def contract_rows(left, right):
    return lax.dot_general(left, right, (((0,), (0,)), ((), ())), preferred_element_type=F32)


def matmul(left, right):
    return jnp.dot(left, right, preferred_element_type=F32)


def tied(*values):
    return lax.optimization_barrier(values)


def call(kernel, grid, ins, outs, scratch=(), limit=40):
    out = pl.pallas_call(
        kernel,
        grid=grid,
        in_specs=[pl.BlockSpec(block, index) for _, block, index in ins],
        out_specs=[pl.BlockSpec(block, index) for _, _, block, index in outs],
        out_shape=[jax.ShapeDtypeStruct(shape, kind) for shape, kind, _, _ in outs],
        scratch_shapes=list(scratch),
        compiler_params=pltpu.CompilerParams(vmem_limit_bytes=limit * 2**20),
        cost_estimate=pl.CostEstimate(flops=1024, bytes_accessed=1024, transcendentals=0),
    )(*[array for array, _, _ in ins])
    return out


def whole(array):
    return (array, array.shape, lambda *_: (0,) * array.ndim)


def swap(value):
    return lax.ppermute(value, "core", [(0, 1), (1, 0)])


def ordered(mine, other, axis):
    first = lax.axis_index("core") == 0
    return jnp.concatenate(
        [jnp.where(first, mine, other), jnp.where(first, other, mine)], axis=axis
    )


def forward(axis, distance=1):
    count = lax.axis_size(axis)
    return [(i, (i + distance) % count) for i in range(count)]


def ring_gather(axis, piece):
    pieces = [piece]
    for _ in range(1, lax.axis_size(axis)):
        pieces.append(lax.ppermute(pieces[-1], axis, forward(axis)))
    return pieces[1:]


def direct_sends(rows):
    return [rows] + [
        lax.ppermute(rows, "outer", forward("outer", distance))
        for distance in range(1, lax.axis_size("outer"))
    ]


def joined_rows(pieces):
    return jnp.concatenate(pieces, 0) if len(pieces) > 1 else pieces[0]


def gather_near(arrived):
    own = joined_rows(arrived)
    return (own,) + tied(ring_gather("inner", own), ring_gather("dp", own))


def gather_far(own, along_x, along_y):
    half = own.shape[0] // 2
    one = ring_gather("inner", joined_rows([piece[:half] for piece in along_y]))
    two = ring_gather("dp", joined_rows([piece[half:] for piece in along_x]))
    return tied(one, two)


def in_pieces(own, along_x, along_y, one, two):
    pieces = [own, *along_x, *along_y, *one, *two]
    if any(piece.shape[0] % LANES for piece in pieces):
        pieces = [joined_rows(pieces)]
    return pieces


def arrival_order(width, shard_rows):
    inner, outer, dp = (lax.axis_size(name) for name in ("inner", "outer", "dp"))
    x, z, y = (lax.axis_index(name) for name in ("inner", "outer", "dp"))
    half = outer * shard_rows
    blocks = [(0, 0, 0, 2)]
    blocks += [(d, 0, 0, 2) for d in range(1, inner)] + [(0, d, 0, 2) for d in range(1, dp)]
    blocks += [(d, e, 0, 1) for d in range(1, inner) for e in range(1, dp)]
    blocks += [(d, e, 1, 2) for e in range(1, dp) for d in range(1, inner)]
    place = np.concatenate([np.arange(low * half, high * half) for _, _, low, high in blocks])
    sizes = [(high - low) * half for _, _, low, high in blocks]
    along_x = np.repeat([block[0] for block in blocks], sizes)
    along_y = np.repeat([block[1] for block in blocks], sizes)
    along_z, row = place // (2 * shard_rows), place % (2 * shard_rows)
    at_x = (x - jnp.asarray(along_x, jnp.int32) + inner) % inner
    at_y = (y - jnp.asarray(along_y, jnp.int32) + dp) % dp
    at_z = (z - jnp.asarray(along_z, jnp.int32) + outer) % outer
    source = ((at_y * outer + at_z) * inner + at_x) * 2 * shard_rows + row
    return (jnp.arange(width, dtype=jnp.int32)[:, None] == source[None, :]).astype(BF16)


def rows_kernel(pairs, places, *refs):
    lefts, rights, rest = refs[:pairs], refs[pairs : 2 * pairs], refs[2 * pairs :]
    adds, out_ref = rest[:-1], rest[-1]
    start = 0
    for left, right in zip(lefts, rights):
        columns = slice(start, start + right.shape[1])
        total = contract_rows(left[...], right[...])
        full = [add for add in adds if add.shape[0] == total.shape[0]]
        for add in full:
            total = total + add[:, columns].astype(F32)
        out_ref[:, columns] = total.astype(BF16)
        for add, at in zip(adds, places):
            if add.shape[0] != total.shape[0]:
                span = slice(at, at + add.shape[0])
                part = total[span] + add[:, columns].astype(F32)
                out_ref[span, columns] = part.astype(BF16)
        start = columns.stop


class GradSum:
    def __init__(self, lefts, rights, shard_rows):
        self.lefts, self.rights = lefts, rights
        self.inner, self.outer, self.dp = (
            lax.axis_size(name) for name in ("inner", "outer", "dp")
        )
        self.shard = 2 * shard_rows
        self.half = self.outer * shard_rows
        self.at_x = 2 * self.half
        self.at_y = self.at_x + (self.inner - 1) * 2 * self.half
        self.at_one = self.at_y + (self.dp - 1) * 2 * self.half
        self.at_two = self.at_one + (self.inner - 1) * (self.dp - 1) * self.half

    def rows(self, start, count, adds):
        adds = [(rows, place) for rows, place in adds if rows is not None]
        lefts, index = self.lefts, start // max(count, 1)
        if count % LANES or start % count:
            lefts, index = [left[:, start : start + count] for left in lefts], 0
        depth = lefts[0].shape[0]
        columns = sum(right.shape[1] for right in self.rights)
        return call(
            functools.partial(rows_kernel, len(lefts), [place for _, place in adds]),
            (1,),
            [(left, (depth, count), lambda i: (0, index)) for left in lefts]
            + [whole(right) for right in self.rights]
            + [whole(rows) for rows, _ in adds],
            [((count, columns), BF16, (count, columns), lambda i: (0, 0))],
        )[0]

    def ring(self, axis, chunk, first):
        arrived = None
        for step in range(1, lax.axis_size(axis)):
            sent = first if step == 1 else chunk(step, arrived)
            arrived = lax.ppermute(sent, axis, forward(axis))
        return arrived

    def one(self, distance, arrived):
        count = (self.dp - 1) * self.half
        return self.rows(self.at_one + (distance - 1) * count, count, [(arrived, 0)])

    def two(self, distance, arrived):
        count = (self.inner - 1) * self.half
        return self.rows(self.at_two + (distance - 1) * count, count, [(arrived, 0)])

    def far(self):
        if self.dp == 1 or self.inner == 1:
            return (None, None)
        return self.one(1, None), self.two(1, None)

    def send_far(self, firsts):
        if firsts[0] is None:
            return firsts
        return tied(
            self.ring("inner", self.one, firsts[0]), self.ring("dp", self.two, firsts[1])
        )

    def along(self, start, distance, arrived, extra, place):
        count = 2 * self.half
        if extra is not None:
            extra = extra[(distance - 1) * self.half : distance * self.half]
        at = start + (distance - 1) * count
        return self.rows(at, count, [(arrived, 0), (extra, place)])

    def along_x(self, distance, arrived):
        return self.along(self.at_x, distance, arrived, self.sums[1], self.half)

    def along_y(self, distance, arrived):
        return self.along(self.at_y, distance, arrived, self.sums[0], 0)

    def near(self, sums):
        self.sums = sums
        return (
            self.along_x(1, None) if self.inner > 1 else None,
            self.along_y(1, None) if self.dp > 1 else None,
        )

    def send_near(self, firsts):
        return tied(
            self.ring("inner", self.along_x, firsts[0]),
            self.ring("dp", self.along_y, firsts[1]),
        )

    def own(self, nears):
        return self.rows(0, 2 * self.half, [(near, 0) for near in nears])

    def finish(self, own):
        def cut(distance):
            return own[distance * self.shard : (distance + 1) * self.shard]

        arrived = [
            lax.ppermute(cut(distance), "outer", forward("outer", self.outer - distance))
            for distance in range(1, self.outer)
        ]
        total = sum([piece.astype(F32) for piece in arrived], cut(0).astype(F32))
        return total.reshape(2, self.shard // 2, -1)


def both_halves(total):
    core = lax.axis_index("core")
    mine = lax.dynamic_index_in_dim(total, core, 0, keepdims=False)
    other = swap(lax.dynamic_index_in_dim(total, 1 - core, 0, keepdims=False))
    return (
        jnp.where(core == 0, mine, other),
        jnp.where(core == 0, other, mine),
    )


def normalise(values):
    centred = values - jnp.mean(values, -1, keepdims=True)
    scale = lax.rsqrt(jnp.mean(centred * centred, -1, keepdims=True) + NORM_EPSILON)
    return centred * scale, scale


def norm_back(unit, scale, gain, incoming):
    grad = incoming * gain
    return scale * (
        grad
        - jnp.mean(grad, -1, keepdims=True)
        - unit * jnp.mean(grad * unit, -1, keepdims=True)
    )


def piece_matmul(left, pieces):
    total, start = None, 0
    for piece in pieces:
        part = matmul(left[:, start : start + piece.shape[0]], piece[...])
        total = part if total is None else total + part
        start += piece.shape[0]
    return total


def back_kernel(starts, count, *refs):
    grads, pieces, out_refs = refs[: len(starts)], refs[len(starts) : count], refs[count:]
    at = 0
    for piece in pieces:
        total = None
        for grad, start in zip(grads, starts):
            part = contract_cols(grad[...], piece[:, start : start + grad.shape[1]])
            total = part if total is None else total + part
        for out_ref in out_refs:
            out_ref[:, at : at + piece.shape[0]] = total.astype(out_ref.dtype)
        at += piece.shape[0]


def back_project(grads, pieces, kinds):
    rows = grads[0].shape[0]
    block = rows // 2
    starts, end = [], 0
    for grad in grads:
        starts.append(end)
        end += grad.shape[1]
    width = sum(piece.shape[0] for piece in pieces)
    return call(
        functools.partial(back_kernel, starts, len(grads) + len(pieces)),
        (2,),
        [(grad, (block, grad.shape[1]), lambda i: (i, 0)) for grad in grads]
        + [(piece, (piece.shape[0], end), lambda i: (0, 0)) for piece in pieces],
        [((rows, width), kind, (block, width), lambda i: (i, 0)) for kind in kinds],
    )


def turned(values):
    width = values.shape[-1]
    lane = lax.broadcasted_iota(jnp.int32, values.shape, values.ndim - 1)
    ahead = pltpu.roll(values, width - HD // 2, values.ndim - 1)
    behind = pltpu.roll(values, HD // 2, values.ndim - 1)
    return jnp.where(lane % HD < HD // 2, ahead, behind)


def project_kernel(count, x_ref, cos_ref, sin_ref, *refs):
    gains, weights = refs[:count], refs[count : 2 * count]
    out_ref, norm_ref, gain_ref = refs[2 * count :]

    @pl.when(pl.program_id(0) == 0)
    def _():
        pick = lax.broadcasted_iota(jnp.int32, (8, LANES), 0) == lax.broadcasted_iota(
            jnp.int32, (8, LANES), 1
        )
        pick = pick.astype(F32).astype(BF16)
        start = 0
        for piece in gains:
            gain_ref[:, start : start + piece.shape[0]] = contract_cols(pick, piece[...])
            start += piece.shape[0]
        unit, _ = normalise(x_ref[...].astype(F32))
        norm_ref[...] = (unit * gain_ref[0:1, :]).astype(BF16)

    values = piece_matmul(norm_ref, weights)
    keep = pl.program_id(0) == 2
    length = cos_ref.shape[0]
    for top in range(0, values.shape[0], length):
        for left in range(0, values.shape[1], LANES):
            part = values[top : top + length, left : left + LANES]
            rotated = part * cos_ref[...] + turned(part) * sin_ref[...]
            out_ref[top : top + length, left : left + LANES] = jnp.where(
                keep, part, rotated
            ).astype(BF16)


def project(tokens, pieces, cosine, sine, side):
    rows, width = tokens.shape
    gain_block = 3 * side // LANES
    return call(
        functools.partial(project_kernel, len(pieces)),
        (3,),
        [whole(tokens), whole(cosine), whole(sine)]
        + [(piece, (piece.shape[0], LANES), lambda j: (0, gain_block)) for piece in pieces]
        + [(piece, (piece.shape[0], side), lambda j: (0, j)) for piece in pieces],
        [
            ((rows, 3 * side), BF16, (rows, side), lambda j: (0, j)),
            ((rows, width), BF16, (rows, width), lambda j: (0, 0)),
            ((8, width), F32, (8, width), lambda j: (0, 0)),
        ],
    )


def head_masks():
    lane = lax.broadcasted_iota(jnp.int32, (1, LANES), 1)
    return [(lane // HD == head).astype(F32).astype(BF16) for head in range(LANES // HD)]


def block_mask(query_ids, key_ids):
    rows, width = query_ids.shape[0], key_ids.shape[1]
    offset = lax.broadcasted_iota(jnp.int32, (rows, width), 1) - lax.broadcasted_iota(
        jnp.int32, (rows, width), 0
    )
    return (offset >= 0) & (offset <= 2 * HALF) & (query_ids == key_ids)


def block_probs(query, keys, allowed):
    scores = jnp.where(allowed, contract_cols(query, keys) * HD**-0.5, -1e30)
    grown = jnp.exp(scores - jnp.max(scores, -1, keepdims=True))
    return grown / jnp.sum(grown, -1, keepdims=True)


def attend_kernel(block, q_ref, k_ref, v_ref, qid_ref, kid_ref, out_ref):
    masks = head_masks()
    for start in range(0, out_ref.shape[1], block):
        span = slice(start, start + block + 2 * HALF)
        allowed = block_mask(qid_ref[0, start : start + block], kid_ref[0, :, span])
        query = q_ref[0, HALF + start : HALF + start + block]
        total = None
        for mask in masks:
            probs = block_probs(query * mask, k_ref[0, span], allowed)
            part = matmul(probs.astype(BF16), v_ref[0, span]) * mask.astype(F32)
            total = part if total is None else total + part
        out_ref[0, start : start + block] = total.astype(BF16)


def attend_back_kernel(
    block, q_ref, k_ref, v_ref, qid_ref, kid_ref, grad_ref, cos_ref, sin_ref,
    dq_ref, mid_ref, low_ref, high_ref,
):
    masks = head_masks()
    length = dq_ref.shape[1]
    grad_keys = grad_values = jnp.zeros((length + 2 * HALF, LANES), F32)
    for start in range(0, length, block):
        span = slice(start, start + block + 2 * HALF)
        mid = slice(HALF + start, HALF + start + block)
        rows = slice(start, start + block)
        allowed = block_mask(qid_ref[0, rows], kid_ref[0, :, span])
        query_all, grad_all = q_ref[0, mid], grad_ref[0, rows]
        keys, values = k_ref[0, span], v_ref[0, span]
        grad_query, part_keys, part_values = 0.0, 0.0, 0.0
        for mask in masks:
            query, grad = query_all * mask, grad_all * mask
            probs = block_probs(query, keys, allowed)
            grad_probs = contract_cols(grad, values)
            delta = jnp.sum(probs * grad_probs, -1, keepdims=True)
            grad_scores = (probs * (grad_probs - delta)).astype(BF16)
            grad_query += matmul(grad_scores, keys) * mask.astype(F32)
            part_keys += contract_rows(grad_scores, query)
            part_values += contract_rows(probs.astype(BF16), grad)
        grad_query = grad_query * HD**-0.5
        dq_ref[0, rows] = (
            grad_query * cos_ref[mid] - turned(grad_query) * sin_ref[mid]
        ).astype(BF16)
        before, after = start, length - start - block

        def placed(part):
            pieces = [part]
            if before:
                pieces.insert(0, jnp.zeros((before, LANES), F32))
            if after:
                pieces.append(jnp.zeros((after, LANES), F32))
            return jnp.concatenate(pieces, 0)

        grad_keys += placed(part_keys)
        grad_values += placed(part_values)
    for index, total in enumerate((grad_keys * HD**-0.5, grad_values)):
        low_ref[0, index] = total[:HALF].astype(BF16)
        mid_ref[0, index] = total[HALF : HALF + length]
        high_ref[0, index] = total[HALF + length :].astype(BF16)


def attention_inputs(joined, query_ids, key_ids):
    window, groups = joined.shape[1], joined.shape[2] // 3 // LANES
    inputs = [
        (joined, (1, window, LANES), lambda s, h, shift=shift: (s, 0, h + shift))
        for shift in (0, groups, 2 * groups)
    ]
    inputs += [
        (ids, (1,) + ids.shape[1:], lambda s, h: (s, 0, 0)) for ids in (query_ids, key_ids)
    ]
    return inputs


def attend(block, joined, query_ids, key_ids):
    streams, window, columns = joined.shape
    length, side = window - 2 * HALF, columns // 3
    return call(
        functools.partial(attend_kernel, block),
        (streams, side // LANES),
        attention_inputs(joined, query_ids, key_ids),
        [((streams, length, side), BF16, (1, length, LANES), lambda s, h: (s, 0, h))],
        limit=24,
    )[0]


def attend_back(block, joined, query_ids, key_ids, grad, cosine, sine):
    streams, length, side = grad.shape

    def pair(rows, kind):
        return (
            (streams, 2, rows, side), kind, (1, 2, rows, LANES), lambda s, h: (s, 0, 0, h)
        )

    return call(
        functools.partial(attend_back_kernel, block),
        (streams, side // LANES),
        attention_inputs(joined, query_ids, key_ids)
        + [(grad, (1, length, LANES), lambda s, h: (s, 0, h)), whole(cosine), whole(sine)],
        [
            ((streams, length, side), BF16, (1, length, LANES), lambda s, h: (s, 0, h)),
            pair(length, F32),
            pair(HALF, BF16),
            pair(HALF, BF16),
        ],
        limit=24,
    )


def join_kernel(dq_ref, mid_ref, low_ref, high_ref, cos_ref, sin_ref, out_ref):
    length, width = dq_ref.shape[1:]
    out_ref[0, :, :width] = dq_ref[0]
    cosine, sine = cos_ref[HALF : HALF + length], sin_ref[HALF : HALF + length]
    for index in range(2):
        for start in range(0, width, LANES):
            lanes = slice(start, start + LANES)
            total = mid_ref[0, index, :, lanes]
            total = total + jnp.concatenate(
                [
                    low_ref[0, index, :, lanes].astype(F32),
                    jnp.zeros((length - 2 * HALF, LANES), F32),
                    high_ref[0, index, :, lanes].astype(F32),
                ],
                0,
            )
            if index == 0:
                total = total * cosine - turned(total) * sine
            to = (1 + index) * width + start
            out_ref[0, :, to : to + LANES] = total.astype(BF16)


def join_grads(grad_query, mid, from_lower, from_upper, cosine, sine):
    streams, length, width = grad_query.shape

    def of_stream(array):
        block = (1,) + array.shape[1:]
        return (array, block, lambda s: (s,) + (0,) * (array.ndim - 1))

    return call(
        join_kernel,
        (streams,),
        [of_stream(array) for array in (grad_query, mid, from_lower, from_upper)]
        + [whole(cosine), whole(sine)],
        [((streams, length, 3 * width), BF16, (1, length, 3 * width), lambda s: (s, 0, 0))],
        limit=24,
    )[0]


def by_rows(array, block):
    return (array, (block, array.shape[1]), lambda i: (i, 0))


def out_kernel(att_ref, weight_ref, x_ref, gain_ref, hidden_ref, norm_ref):
    hidden = x_ref[...].astype(F32) + matmul(att_ref[...], weight_ref[...])
    hidden_ref[...] = hidden
    norm_ref[...] = (normalise(hidden)[0] * gain_ref[1:2, :]).astype(BF16)


def out_project(attended, weight, tokens, gains):
    rows, width = tokens.shape
    block = rows // 4
    return call(
        out_kernel,
        (4,),
        [by_rows(attended, block), whole(weight), by_rows(tokens, block), whole(gains)],
        [
            ((rows, width), kind, (block, width), lambda i: (i, 0)) for kind in (F32, BF16)
        ],
        limit=24,
    )


def hidden_back_kernel(
    part_ref, other_ref, hidden_ref, g_ref, gain_ref, weight_ref, grad_ref, low_ref, att_ref
):
    unit, scale = normalise(hidden_ref[...])
    incoming = part_ref[...] + other_ref[...].astype(F32)
    grad = g_ref[...].astype(F32) + norm_back(unit, scale, gain_ref[1:2, :], incoming)
    low = grad.astype(BF16)
    grad_ref[...] = grad
    low_ref[...] = low
    att_ref[...] = contract_cols(low, weight_ref[...]).astype(BF16)


def hidden_back(part, other, hidden, grad_output, gains, weight):
    rows, width = hidden.shape
    block, side = rows // 4, weight.shape[0]
    return call(
        hidden_back_kernel,
        (4,),
        [by_rows(array, block) for array in (part, other, hidden, grad_output)]
        + [whole(gains), whole(weight)],
        [
            ((rows, size), kind, (block, size), lambda i: (i, 0))
            for size, kind in ((width, F32), (width, BF16), (side, BF16))
        ],
        limit=24,
    )


def feed_kernel(count, norm_ref, *refs):
    gates, ups = refs[:count], refs[count : 2 * count]
    mixed_ref, factor_ref, active_ref = refs[2 * count :]
    gate, up = piece_matmul(norm_ref, gates), piece_matmul(norm_ref, ups)
    below = 0.5 * (1.0 + lax.erf(gate * 0.5**0.5))
    active = gate * below
    mixed_ref[...] = (active * up).astype(BF16)
    active_ref[...] = active
    density = jnp.exp(-0.5 * gate * gate) * (2.0 * np.pi) ** -0.5
    factor_ref[...] = up * (below + gate * density)


def feed(normed, pieces, units):
    rows = normed.shape[0]
    tiles = units // LANES
    return call(
        functools.partial(feed_kernel, len(pieces)),
        (tiles,),
        [whole(normed)]
        + [(piece, (piece.shape[0], LANES), lambda j: (0, j)) for piece in pieces]
        + [(piece, (piece.shape[0], LANES), lambda j: (0, j + tiles)) for piece in pieces],
        [
            ((rows, units), kind, (rows, LANES), lambda j: (0, j))
            for kind in (BF16, F32, F32)
        ],
        limit=24,
    )


def feed_back_kernel(count, g_ref, factor_ref, active_ref, *refs):
    grad = piece_matmul(g_ref, refs[:count])
    gate_ref, up_ref = refs[count:]
    gate_ref[...] = (grad * factor_ref[...]).astype(BF16)
    up_ref[...] = (grad * active_ref[...]).astype(BF16)


def feed_back(grad_output, factor, active, pieces):
    rows, units = factor.shape

    def tile(array):
        return (array, (array.shape[0], LANES), lambda j: (0, j))

    return call(
        functools.partial(feed_back_kernel, len(pieces)),
        (units // LANES,),
        [whole(grad_output), tile(factor), tile(active)] + [tile(piece) for piece in pieces],
        [((rows, units), BF16, (rows, LANES), lambda j: (0, j)) for _ in range(2)],
        limit=24,
    )


def shards(tokens, doc_ids, norm_attn, norm_mlp, w_qkv, w_out, w_in, w_down, cotangent):
    streams, block, width = tokens.shape
    shard_rows = w_qkv.shape[0]
    inner, outer = lax.axis_size("inner"), lax.axis_size("outer")
    core = lax.axis_index("core")
    length = 2 * block
    window = length + 2 * HALF
    rows = streams * length
    side = width // 2
    units = w_down.shape[1] // 2
    padded = -(-units // LANES) * LANES
    chips = outer * inner
    onward = [(i, i + 1) for i in range(chips - 1)]
    back = [(i + 1, i) for i in range(chips - 1)]

    def halves(weight, parts, pad):
        size = weight.shape[1] // (2 * parts)
        cut = [weight[:, i * size : (i + 1) * size] for i in range(2 * parts)]
        if pad != size:
            cut = [jnp.pad(piece, ((0, 0), (0, pad - size))) for piece in cut]
        return cut[0::2], cut[1::2]

    def paired(pieces):
        low = jnp.concatenate([piece for one, _ in pieces for piece in one], 1)
        high = jnp.concatenate([piece for _, two in pieces for piece in two], 1)
        mine = jnp.where(core == 0, low, high)
        return ordered(mine, swap(jnp.where(core == 0, high, low)), 0)

    pair_tokens = ordered(tokens, swap(tokens), 1)

    gains = jnp.pad(jnp.stack([norm_attn, norm_mlp], 1), ((0, 0), (0, LANES - 2)))
    pair_one = paired([halves(w_qkv, 3, side), ([gains], [gains]), halves(w_out, 1, side)])
    later_in, later_down, pair_one, pair_tokens = tied(w_in, w_down, pair_one, pair_tokens)
    low = lax.ppermute(pair_tokens[:, length - HALF :], ("outer", "inner"), onward)
    high = lax.ppermute(pair_tokens[:, :HALF], ("outer", "inner"), back)
    one = direct_sends(pair_one)
    pair_two = paired([halves(later_in, 2, padded)])
    pair_three = paired([halves(later_down, 1, padded)])
    pair_two, one, low, high, pair_tokens = tied(pair_two, one, low, high, pair_tokens)
    two = direct_sends(pair_two)
    near = gather_near(one)
    far = gather_far(*near)
    pair_three, two, near, far = tied(pair_three, two, near, far)
    three = direct_sends(pair_three)
    first = in_pieces(*near, *far)
    two_near = gather_near(two)

    order = arrival_order(width, shard_rows)

    def in_order(value):
        return matmul(value, order).astype(BF16)

    def out_of_order(value):
        return contract_cols(value, order).astype(BF16)

    window_tokens = jnp.concatenate([low, pair_tokens, high], 1).reshape(-1, width)
    window_tokens = in_order(window_tokens)
    own_tokens = window_tokens.reshape(streams, window, width)[:, HALF : HALF + length]
    own_tokens = own_tokens.reshape(rows, width)
    grad_output = in_order(ordered(cotangent, swap(cotangent), 1).reshape(rows, width))

    start = lax.axis_index(("outer", "inner")) * length
    positions = (start - HALF + jnp.arange(window, dtype=jnp.int32)).astype(F32)
    frequency = ROPE_BASE ** (-(jnp.arange(HD // 2, dtype=F32) * 2.0 / HD))
    angles = positions[:, None] * frequency[None, :]
    cosine, sine = jnp.cos(angles), jnp.sin(angles)
    cosine = jnp.tile(cosine, (1, LANES // (HD // 2)))
    sine = jnp.tile(jnp.concatenate([-sine, sine], 1), (1, LANES // HD))
    ids_padded = jnp.pad(doc_ids, ((0, 0), (HALF, HALF)), constant_values=-1)
    key_ids = lax.dynamic_slice_in_dim(ids_padded, start, window, 1)[:, None, :]
    query_ids = lax.dynamic_slice_in_dim(doc_ids, start, length, 1)[:, :, None]

    joined, window_norm, gain_rows = project(window_tokens, first, cosine, sine, side)
    joined, two_near = tied(joined, two_near)
    two_far = gather_far(*two_near)
    joined = joined.reshape(streams, window, 3 * side)
    attended_half = attend(block, joined, query_ids, key_ids).reshape(rows, side)
    out_half = joined_rows([piece[:, 3 * side + LANES :] for piece in first])
    full_out = ordered(out_half, swap(out_half), 1)
    full_out = matmul(order, in_order(full_out)).astype(BF16)
    attended_half, full_out, two_near, two_far, three = tied(
        attended_half, full_out, two_near, two_far, three
    )
    in_half = in_pieces(*two_near, *two_far)
    three_near = gather_near(three)
    attended_low = ordered(attended_half, swap(attended_half), 1)
    hidden, normed_mlp_low = out_project(attended_low, full_out, own_tokens, gain_rows)
    hidden, normed_mlp_low, three_near = tied(hidden, normed_mlp_low, three_near)
    three_far = gather_far(*three_near)
    mixed_low, factor, active = feed(normed_mlp_low, in_half, padded)
    mixed_low, factor, active, three_near, three_far = tied(
        mixed_low, factor, active, three_near, three_far
    )
    down_half = in_pieces(*three_near, *three_far)

    sum_down = GradSum([grad_output], [mixed_low], shard_rows)
    down_far = sum_down.send_far(sum_down.far())
    grad_gate, grad_up = feed_back(grad_output, factor, active, down_half)
    grad_gate, grad_up, down_far = tied(grad_gate, grad_up, down_far)
    sum_in = GradSum([normed_mlp_low], [jnp.concatenate([grad_gate, grad_up], 1)], shard_rows)
    sent_down, sent_in = sum_down.near(down_far), sum_in.far()
    grad_gate, grad_up, sent_down, sent_in = tied(grad_gate, grad_up, sent_down, sent_in)
    down_near = sum_down.send_near(sent_down)
    in_far = sum_in.send_far(sent_in)
    part, part_low = back_project([grad_gate, grad_up], in_half, [F32, BF16])
    out_rows = lax.dynamic_slice_in_dim(full_out, core * side, side, 0)
    grad_hidden, grad_hidden_low, grad_attended = hidden_back(
        part, swap(part_low), hidden, grad_output, gain_rows, out_rows
    )
    grad_attended, down_near, in_far = tied(grad_attended, down_near, in_far)
    down_total = sum_down.finish(sum_down.own(down_near))

    grad_query, mid, to_lower, to_upper = attend_back(
        block, joined, query_ids, key_ids, grad_attended.reshape(streams, length, side),
        cosine, sine,
    )
    sent_in = sum_in.near(in_far)
    to_lower, to_upper, sent_in = tied(to_lower, to_upper, sent_in)
    from_lower = lax.ppermute(to_upper, ("outer", "inner"), onward)
    from_upper = lax.ppermute(to_lower, ("outer", "inner"), back)
    in_near = sum_in.send_near(sent_in)
    grad_joined = join_grads(grad_query, mid, from_lower, from_upper, cosine, sine)
    grad_joined = grad_joined.reshape(rows, 3 * side)
    hidden_side = lax.dynamic_slice_in_dim(out_of_order(grad_hidden_low), core * side, side, 1)
    normed_low = window_norm.reshape(streams, window, width)[:, HALF : HALF + length]
    sum_attn = GradSum(
        [normed_low.reshape(rows, width), in_order(attended_low)],
        [grad_joined, hidden_side],
        shard_rows,
    )
    sent_attn = sum_attn.far()
    sent_attn, in_near, grad_joined = tied(sent_attn, in_near, grad_joined)
    in_own = sum_in.own(in_near)
    attn_far = sum_attn.send_far(sent_attn)
    in_total = sum_in.finish(in_own)

    def own_rows(value):
        value = value.reshape(streams, 2, block, width)
        mine = lax.dynamic_index_in_dim(value, core, 1, keepdims=False)
        other = lax.dynamic_index_in_dim(value, 1 - core, 1, keepdims=False)
        return mine, other

    def summed_rows(partial):
        mine, other = own_rows(partial)
        return mine + swap(other.astype(BF16)).astype(F32)

    (out_part,) = back_project([mixed_low], down_half, [F32])
    output = own_rows(hidden)[0] + summed_rows(out_part)
    output = out_of_order(output.astype(BF16).reshape(-1, width)).reshape(tokens.shape)

    (norm_part,) = back_project([grad_joined], first, [F32])
    grad_normed = summed_rows(norm_part)
    unit, scale = normalise(own_rows(own_tokens)[0].astype(F32))
    grad_tokens = own_rows(grad_hidden)[0] + norm_back(unit, scale, gain_rows[0], grad_normed)
    grad_tokens = lax.dot_general(
        grad_tokens.reshape(-1, width),
        order.astype(F32),
        (((1,), (1,)), ((), ())),
        precision=lax.Precision.HIGHEST,
        preferred_element_type=F32,
    ).reshape(tokens.shape)

    attn_near = sum_attn.send_near(sum_attn.near(attn_far))
    attn_total = sum_attn.finish(sum_attn.own(attn_near))

    def interleaved(pair, start, parts, stride, size):
        cuts = []
        for i in range(parts):
            first_column = start + i * stride
            cuts += [half[:, first_column : first_column + size] for half in pair]
        return jnp.concatenate(cuts, 1)

    grad_down = interleaved(both_halves(down_total), 0, 1, padded, units)
    grad_in = interleaved(both_halves(in_total), 0, 2, padded, units)
    pair = both_halves(attn_total)
    grad_qkv = interleaved(pair, 0, 3, side, side)
    grad_out = interleaved(pair, 3 * side, 1, side, side)

    def gain_grad(weight, grad, gain):
        return jnp.sum(weight.astype(F32) * grad, -1) / gain.astype(F32)

    return (
        output,
        grad_tokens,
        gain_grad(w_qkv, grad_qkv, norm_attn),
        gain_grad(w_in, grad_in, norm_mlp),
        grad_qkv,
        grad_out,
        grad_in,
        grad_down,
    )


def solution(mesh):
    dp, seq = mesh.shape["dp"], mesh.shape["seq"]
    chips = seq // 2
    outer = 4 if chips % 4 == 0 else 1
    fine = Mesh(
        mesh.devices.reshape(dp, outer, chips // outer, 2), ("dp", "outer", "inner", "core")
    )
    line = ("outer", "inner", "core")
    every = ("dp",) + line
    token = P("dp", line, None)
    vector = P(every)
    matrix = P(every, None)
    return jax.shard_map(
        shards,
        mesh=fine,
        in_specs=(token, P("dp", None), vector, vector, matrix, matrix, matrix, matrix, token),
        out_specs=(token, token, vector, vector, matrix, matrix, matrix, matrix),
        check_vma=False,
    )
```

time: 428 us -> 461 us (1.077)
  the two profiles are of different devices: /device:TPU:13 before, /device:TPU:0 now
where the time goes in v4:
time: 461 us; the launch traced here: 456 us
  waiting for transfers between devices  208 us (45%)
  Pallas kernels  92.8 us (20%)
  starting transfers between devices  69.8 us (15%)
  local copies, waits for them, and re-layouts  48 us (10%)
  matrix products  18.7 us (4%)
  other arithmetic  16.7 us (4%)
    pallas_call x26, Pallas kernels, call(): pl.pallas_call(kernel, grid=grid, in_specs=[pl.BlockSpec(block, index) fo...  92.8 us
    ppermute x12, waiting for transfers between devices, ring(): arrived = lax.ppermute(sent, axis, forward(axis))  73.3 us
    ppermute x9, waiting for transfers between devices, finish(): lax.ppermute(cut(distance), 'outer', forward('outer', self.outer - distan...  44.4 us
    ppermute x12, waiting for transfers between devices, ring_gather(): pieces.append(lax.ppermute(pieces[-1], axis, forward(axis)))  42.8 us
    unnamed x195, local copies, waits for them, and re-layouts  32.6 us
    ppermute x9, waiting for transfers between devices, direct_sends(): lax.ppermute(rows, 'outer', forward('outer', distance))  30.7 us
    ppermute x9, starting transfers between devices, direct_sends(): lax.ppermute(rows, 'outer', forward('outer', distance))  16.4 us
    ppermute x12, starting transfers between devices, ring_gather(): pieces.append(lax.ppermute(pieces[-1], axis, forward(axis)))  15.6 us
  transfers between devices with their start and end apart: 59, of which 29 were waited for; matrix products, arithmetic and copies ran while one was open for 11% of the time, Pallas kernels for 19%

profile of v4, /device:TPU:0, one launch (start us, length us, event | category | flops | bytes accessed | tf_op | source)
XLA Modules:
  0.0 456.4 jit_solution(3851784713074921581)
XLA Ops:
  8.2 4.8 %collective-permute-start.5 = (bf16[64,2176]{1,0:T(8,128)(2,1)S(1)}, bf16[64,2176]{1,0:T(8,128)(2,1)S(1)}, u32[]{:S(2)}, u32[]{:S(2)}) collective-permute-start(bf16[64,2176]{1,0:T(8,128)(2,1)S(1)} %pad_maximum_fusion.6), channel_id=1, source_target_pairs={{0,12},{4,0},{8,4},{12,8},{1,13},{5,1},{9,5},{13,9},{2,14},{6,2},{... | collective-permute-start | bytes 835592 | tf_op jit(solution)/shard_map/ppermute | solution.py:79
  17.9 4.6 collective-permute-start.6
  23.3 3.7 collective-permute-done.7
  27.1 4.0 collective-permute-done.6
  31.1 6.8 %collective-permute-done.4 = bf16[64,2176]{1,0:T(8,128)(2,1)S(1)} collective-permute-done((bf16[64,2176]{1,0:T(8,128)(2,1)S(1)}, bf16[64,2176]{1,0:T(8,128)(2,1)S(1)}, u32[]{:S(2)}, u32[]{:S(2)}) %collective-permute-start.4) | collective-permute-done | bytes 278560 | tf_op jit(solution)/shard_map/ppermute | solution.py:79
  42.6 20.9 %collective-permute-done.13.refs_2_.refs_7_.refs_3_ = bf16[256,2176]{1,0:T(8,128)(2,1)S(1)} collective-permute-done((bf16[256,2176]{1,0:T(8,128)(2,1)S(1)}, bf16[256,2176]{1,0:T(8,128)(2,1)S(1)}, u32[]{:S(2)}, u32[]{:S(2)}) %collective-permute-start.13) | collective-permute-done | bytes 1114144 | tf_op jit(solution)/shard_map/ppermute | solution.py:73
  63.5 3.1 collective-permute-done.12.refs_1_.refs_6_.refs_2_
  70.7 4.5 collective-permute-start.10
  81.1 23.9 %collective-permute-done.10 = bf16[64,2816]{1,0:T(8,128)(2,1)S(1)} collective-permute-done((bf16[64,2816]{1,0:T(8,128)(2,1)S(1)}, bf16[64,2816]{1,0:T(8,128)(2,1)S(1)}, u32[]{:S(2)}, u32[]{:S(2)}) %collective-permute-start.10) | collective-permute-done | bytes 360480 | tf_op jit(solution)/shard_map/ppermute | solution.py:79
  121.2 7.7 %shard_map.188 = (bf16[768,1536]{1,0:T(8,128)(2,1)S(1)}, bf16[768,1024]{1,0:T(8,128)(2,1)S(1)}, f32[8,1024]{1,0:T(8,128)S(1)}) custom-call(bf16[768,1024]{1,0:T(8,128)(2,1)S(1)} %fusion.25.x_ref, f32[384,128]{1,0:T(8,128)S(1)} %copy-done.42, f32[384,128]{1,0:T(8,128)S(1)} %copy-done.40, bf16[256,2176]{1,0:T(8,128)(2,1)S(1)} %copy-done.11, ...), custom_call_target="tpu_custom_call" | custom-call | flops 1024 | bytes 1024 | tf_op jit(solution)/shard_map/pallas_call | solution.py:37
  131.1 3.0 broadcast_select_fusion.1
  134.2 5.2 %collective-permute-done.17.refs_2_.refs_7_.refs_4_ = bf16[256,2816]{1,0:T(8,128)(2,1)} collective-permute-done((bf16[256,2816]{1,0:T(8,128)(2,1)}, bf16[256,2816]{1,0:T(8,128)(2,1)}, u32[]{:S(2)}, u32[]{:S(2)}) %collective-permute-start.17) | collective-permute-done | bytes 1441824 | tf_op jit(solution)/shard_map/ppermute | solution.py:73
  146.3 7.5 %fusion.22.weight_ref = bf16[1024,1024]{1,0:T(8,128)(2,1)} fusion(s32[1024]{0:T(1024)S(1)} %fusion.72, bf16[1024,512]{1,0:T(8,128)(2,1)} %get-tuple-element.245, bf16[1024,512]{1,0:T(8,128)(2,1)} %get-tuple-element.244), kind=kOutput, calls=%fused_computation.22 | convolution fusion | flops 4303355904 | bytes 4198400 | tf_op jit(solution)/shard_map/dot_general | solution.py:29
  153.9 8.0 %shard_map.189 = bf16[2,256,512]{2,1,0:T(8,128)(2,1)S(1)} custom-call(bf16[2,384,1536]{2,1,0:T(8,128)(2,1)S(1)} %bitcast.103, bf16[2,384,1536]{2,1,0:T(8,128)(2,1)S(1)} %bitcast.104, bf16[2,384,1536]{2,1,0:T(8,128)(2,1)S(1)} %bitcast.105, s32[2,256,1]{2,1,0:T(8,128)S(1)} %copy-done.48, s32[2,1,384]{2,1,0:T(1,128)S(1)} %broadcast_in_dim.5.kid_ref), custom_call_target="tpu_custom_call" | custom-call | flops 1024 | bytes 1024 | tf_op jit(solution)/shard_map/pallas_call | solution.py:37
  173.2 11.3 %collective-permute-done.26.refs_3_.refs_2_ = bf16[256,1408]{1,0:T(8,128)(2,1)S(1)} collective-permute-done((bf16[256,1408]{1,0:T(8,128)(2,1)S(1)}, bf16[256,1408]{1,0:T(8,128)(2,1)S(1)}, u32[]{:S(2)}, u32[]{:S(2)}) %collective-permute-start.26) | collective-permute-done | bytes 720928 | tf_op jit(solution)/shard_map/ppermute | solution.py:73
  190.4 10.8 %shard_map.191 = (bf16[512,1408]{1,0:T(8,128)(2,1)S(1)}, f32[512,1408]{1,0:T(8,128)S(1)}, f32[512,1408]{1,0:T(8,128)S(1)}) custom-call(bf16[512,1024]{1,0:T(8,128)(2,1)S(1)} %get-tuple-element.172.norm_ref.refs_0_, bf16[256,2816]{1,0:T(8,128)(2,1)} %constant_dynamic-update-slice_fusion.14.refs_0_.refs_5_.refs_2_, ...), custom_call_target="tpu_custom_call" | custom-call | flops 1024 | bytes 1024 | tf_op jit(solution)/shard_map/pallas_call | solution.py:37
  220.1 6.5 %shard_map.193 = (bf16[512,1408]{1,0:T(8,128)(2,1)S(1)}, bf16[512,1408]{1,0:T(8,128)(2,1)S(1)}) custom-call(bf16[512,1024]{1,0:T(8,128)(2,1)S(1)} %fusion.26.g_ref.refs_0_, f32[512,1408]{1,0:T(8,128)S(1)} %copy-done.45, f32[512,1408]{1,0:T(8,128)S(1)} %copy-done.47, bf16[256,1408]{1,0:T(8,128)(2,1)S(1)} %copy-done.39, bf16[256,1408]{1,0:T(8,128)(2,1)S(1)} %copy-done.35, ...), custom_call_target="tpu_custom_call" | custom-call | flops 1024 | bytes 1024 | tf_op jit(solution)/shard_map/pallas_call | solution.py:37
  237.5 16.0 %shard_map.200 = (f32[512,1024]{1,0:T(8,128)S(1)}, bf16[512,1024]{1,0:T(8,128)(2,1)}) custom-call(bf16[512,1408]{1,0:T(8,128)(2,1)S(1)} %copy-done.25, bf16[512,1408]{1,0:T(8,128)(2,1)S(1)} %copy-done.27, bf16[256,2816]{1,0:T(8,128)(2,1)} %constant_dynamic-update-slice_fusion.14.refs_0_.refs_5_.refs_2_, ...), custom_call_target="tpu_custom_call" | custom-call | flops 1024 | bytes 1024 | tf_op jit(solution)/shard_map/pallas_call | solution.py:37
  264.2 10.6 %collective-permute-done.34.refs_2_ = bf16[256,1408]{1,0:T(8,128)(2,1)S(1)} collective-permute-done((bf16[256,1408]{1,0:T(8,128)(2,1)}, bf16[256,1408]{1,0:T(8,128)(2,1)S(1)}, u32[]{:S(2)}, u32[]{:S(2)}) %collective-permute-start.34) | collective-permute-done | bytes 720928 | tf_op jit(solution)/shard_map/ppermute | solution.py:179
  275.6 13.8 %collective-permute-done.36.refs_2_ = bf16[128,2816]{1,0:T(8,128)(2,1)S(1)} collective-permute-done((bf16[128,2816]{1,0:T(8,128)(2,1)}, bf16[128,2816]{1,0:T(8,128)(2,1)S(1)}, u32[]{:S(2)}, u32[]{:S(2)}) %collective-permute-start.36) | collective-permute-done | bytes 720928 | tf_op jit(solution)/shard_map/ppermute | solution.py:179
  289.8 3.1 shard_map.201
  301.9 14.6 %shard_map.202 = (bf16[2,256,512]{2,1,0:T(8,128)(2,1)S(1)}, f32[2,2,256,512]{3,2,1,0:T(8,128)S(1)}, bf16[2,2,64,512]{3,2,1,0:T(8,128)(2,1)S(1)}, bf16[2,2,64,512]{3,2,1,0:T(8,128)(2,1)S(1)}) custom-call(bf16[2,384,1536]{2,1,0:T(8,128)(2,1)S(1)} %bitcast.106, bf16[2,384,1536]{2,1,0:T(8,128)(2,1)S(1)} %bitcast.107, bf16[2,384,1536]{2,1,0:T(8,128)(2,1)S(1)} %bitcast.108, ...), custom_call_target="tpu_custom_call" | custom-call | flops 1024 | bytes 1024 | tf_op jit(solution)/shard_map/pallas_call | solution.py:37
  318.5 3.3 collective-permute-start.38
  328.5 5.3 %collective-permute-done.38.low_ref = bf16[2,2,64,512]{3,2,1,0:T(8,128)(2,1)S(1)} collective-permute-done((bf16[2,2,64,512]{3,2,1,0:T(8,128)(2,1)S(1)}, bf16[2,2,64,512]{3,2,1,0:T(8,128)(2,1)S(1)}, u32[]{:S(2)}, u32[]{:S(2)}) %collective-permute-start.38) | collective-permute-done | bytes 262176 | tf_op jit(solution)/shard_map/ppermute | solution.py:747
  335.6 26.6 %collective-permute-done.40.refs_2_ = bf16[256,2816]{1,0:T(8,128)(2,1)S(1)} collective-permute-done((bf16[256,2816]{1,0:T(8,128)(2,1)S(1)}, bf16[256,2816]{1,0:T(8,128)(2,1)S(1)}, u32[]{:S(2)}, u32[]{:S(2)}) %collective-permute-start.40) | collective-permute-done | bytes 1441824 | tf_op jit(solution)/shard_map/ppermute | solution.py:179
  363.4 3.1 collective-permute-start.51
  376.4 8.3 %collective-permute-done.53 = bf16[64,2816]{1,0:T(8,128)(2,1)S(1)} collective-permute-done((bf16[64,2816]{1,0:T(8,128)(2,1)S(1)}, bf16[64,2816]{1,0:T(8,128)(2,1)S(1)}, u32[]{:S(2)}, u32[]{:S(2)}) %collective-permute-start.53) | collective-permute-done | bytes 360480 | tf_op jit(solution)/shard_map/ppermute | solution.py:236
  384.6 14.2 %collective-permute-done.52 = bf16[64,2816]{1,0:T(8,128)(2,1)S(1)} collective-permute-done((bf16[64,2816]{1,0:T(8,128)(2,1)S(1)}, bf16[64,2816]{1,0:T(8,128)(2,1)S(1)}, u32[]{:S(2)}, u32[]{:S(2)}) %collective-permute-start.52) | collective-permute-done | bytes 360480 | tf_op jit(solution)/shard_map/ppermute | solution.py:236
  402.5 3.6 fusion.8
  406.1 20.1 %collective-permute-done.46.refs_5_ = bf16[256,2048]{1,0:T(8,128)(2,1)S(1)} collective-permute-done((bf16[256,2048]{1,0:T(8,128)(2,1)S(1)}, bf16[256,2048]{1,0:T(8,128)(2,1)S(1)}, u32[]{:S(2)}, u32[]{:S(2)}) %collective-permute-start.46) | collective-permute-done | bytes 1048608 | tf_op jit(solution)/shard_map/ppermute | solution.py:179
  432.5 12.7 %collective-permute-done.47 = bf16[64,2048]{1,0:T(8,128)(2,1)S(1)} collective-permute-done((bf16[64,2048]{1,0:T(8,128)(2,1)}, bf16[64,2048]{1,0:T(8,128)(2,1)S(1)}, u32[]{:S(2)}, u32[]{:S(2)}) %collective-permute-start.47) | collective-permute-done | bytes 262176 | tf_op jit(solution)/shard_map/ppermute | solution.py:236
  445.2 6.6 %collective-permute-done.48 = bf16[64,2048]{1,0:T(8,128)(2,1)} collective-permute-done((bf16[64,2048]{1,0:T(8,128)(2,1)S(1)}, bf16[64,2048]{1,0:T(8,128)(2,1)}, u32[]{:S(2)}, u32[]{:S(2)}) %collective-permute-start.48) | collective-permute-done | bytes 262176 | tf_op jit(solution)/shard_map/ppermute | solution.py:236
  (397 shorter events, 155.8 us)
Async XLA Ops:
  8.2 22.9 %collective-permute-start.5 = (bf16[64,2176]{1,0:T(8,128)(2,1)S(1)}, bf16[64,2176]{1,0:T(8,128)(2,1)S(1)}, u32[]{:S(2)}, u32[]{:S(2)}) collective-permute-start(bf16[64,2176]{1,0:T(8,128)(2,1)S(1)} %pad_maximum_fusion.6), channel_id=1, source_target_pairs={{0,12},{4,0},{8,4},{12,8},{1,13},{5,1},{9,5},{13,9},{2,14},{6,2},{... | collective-permute-start | bytes 835592 | tf_op jit(solution)/shard_map/ppermute | solution.py:79
  13.1 24.8 %collective-permute-start.4 = (bf16[64,2176]{1,0:T(8,128)(2,1)S(1)}, bf16[64,2176]{1,0:T(8,128)(2,1)S(1)}, u32[]{:S(2)}, u32[]{:S(2)}) collective-permute-start(bf16[64,2176]{1,0:T(8,128)(2,1)S(1)} %pad_maximum_fusion.6), channel_id=1, source_target_pairs={{0,8},{4,12},{8,0},{12,4},{1,9},{5,13},{9,1},{13,5},{2,10},{6,14},... | collective-permute-start | bytes 835592 | tf_op jit(solution)/shard_map/ppermute | solution.py:79
  13.1 24.8 %collective-permute-start.3 = (bf16[64,2176]{1,0:T(8,128)(2,1)S(1)}, bf16[64,2176]{1,0:T(8,128)(2,1)S(1)}, u32[]{:S(2)}, u32[]{:S(2)}) collective-permute-start(bf16[64,2176]{1,0:T(8,128)(2,1)S(1)} %pad_maximum_fusion.6), channel_id=1, source_target_pairs={{0,4},{4,8},{8,12},{12,0},{1,5},{5,9},{9,13},{13,1},{2,6},{6,10},{... | collective-permute-start | bytes 835592 | tf_op jit(solution)/shard_map/ppermute | solution.py:79
  38.0 25.4 %collective-permute-start.13 = (bf16[256,2176]{1,0:T(8,128)(2,1)S(1)}, bf16[256,2176]{1,0:T(8,128)(2,1)S(1)}, u32[]{:S(2)}, u32[]{:S(2)}) collective-permute-start(bf16[256,2176]{1,0:T(8,128)(2,1)S(1)} %constant_dynamic-update-slice_fusion.10.refs_0_.refs_5_.refs_1_), channel_id=1, source_target_pairs={{0,16},{16,0},{1,17},{17,1},{2,18},{18,2},{3,19},{19,3},{4,20},{20... | collective-permute-start | bytes 3342344 | tf_op jit(solution)/shard_map/ppermute | solution.py:73
  39.6 26.9 %collective-permute-start.12 = (bf16[256,2176]{1,0:T(8,128)(2,1)S(1)}, bf16[256,2176]{1,0:T(8,128)(2,1)S(1)}, u32[]{:S(2)}, u32[]{:S(2)}) collective-permute-start(bf16[256,2176]{1,0:T(8,128)(2,1)S(1)} %constant_dynamic-update-slice_fusion.10.refs_0_.refs_5_.refs_1_), channel_id=1, source_target_pairs={{0,2},{2,0},{1,3},{3,1},{4,6},{6,4},{5,7},{7,5},{8,10},{10,8},{9,1... | collective-permute-start | bytes 3342344 | tf_op jit(solution)/shard_map/ppermute | solution.py:73
  70.7 34.2 %collective-permute-start.10 = (bf16[64,2816]{1,0:T(8,128)(2,1)S(1)}, bf16[64,2816]{1,0:T(8,128)(2,1)S(1)}, u32[]{:S(2)}, u32[]{:S(2)}) collective-permute-start(bf16[64,2816]{1,0:T(8,128)(2,1)S(1)} %copy-done.69), channel_id=1, source_target_pairs={{0,8},{4,12},{8,0},{12,4},{1,9},{5,13},{9,1},{13,5},{2,10},{6,14},... | collective-permute-start | bytes 1081352 | tf_op jit(solution)/shard_map/ppermute | solution.py:79
  75.2 29.7 %collective-permute-start.9 = (bf16[64,2816]{1,0:T(8,128)(2,1)S(1)}, bf16[64,2816]{1,0:T(8,128)(2,1)S(1)}, u32[]{:S(2)}, u32[]{:S(2)}) collective-permute-start(bf16[64,2816]{1,0:T(8,128)(2,1)S(1)} %copy-done.69), channel_id=1, source_target_pairs={{0,4},{4,8},{8,12},{12,0},{1,5},{5,9},{9,13},{13,1},{2,6},{6,10},{... | collective-permute-start | bytes 1081352 | tf_op jit(solution)/shard_map/ppermute | solution.py:79
  108.1 31.3 %collective-permute-start.17 = (bf16[256,2816]{1,0:T(8,128)(2,1)}, bf16[256,2816]{1,0:T(8,128)(2,1)}, u32[]{:S(2)}, u32[]{:S(2)}) collective-permute-start(bf16[256,2816]{1,0:T(8,128)(2,1)} %constant_dynamic-update-slice_fusion.14.refs_0_.refs_5_.refs_2_), channel_id=1, source_target_pairs={{0,16},{16,0},{1,17},{17,1},{2,18},{18,2},{3,19},{19,3},{4,20},{20... | collective-permute-start | bytes 4325384 | tf_op jit(solution)/shard_map/ppermute | solution.py:73
  109.2 30.6 %collective-permute-start.16 = (bf16[256,2816]{1,0:T(8,128)(2,1)}, bf16[256,2816]{1,0:T(8,128)(2,1)}, u32[]{:S(2)}, u32[]{:S(2)}) collective-permute-start(bf16[256,2816]{1,0:T(8,128)(2,1)} %constant_dynamic-update-slice_fusion.14.refs_0_.refs_5_.refs_2_), channel_id=1, source_target_pairs={{0,2},{2,0},{1,3},{3,1},{4,6},{6,4},{5,7},{7,5},{8,10},{10,8},{9,1... | collective-permute-start | bytes 4325384 | tf_op jit(solution)/shard_map/ppermute | solution.py:73
  121.0 41.0 %collective-permute-start.23 = (bf16[64,1408]{1,0:T(8,128)(2,1)}, bf16[64,1408]{1,0:T(8,128)(2,1)}, u32[]{:S(2)}, u32[]{:S(2)}) collective-permute-start(bf16[64,1408]{1,0:T(8,128)(2,1)} %pad_maximum_fusion.7), channel_id=1, source_target_pairs={{0,12},{4,0},{8,4},{12,8},{1,13},{5,1},{9,5},{13,9},{2,14},{6,2},{... | collective-permute-start | bytes 540680 | tf_op jit(solution)/shard_map/ppermute | solution.py:79
  121.1 41.0 %collective-permute-start.22 = (bf16[64,1408]{1,0:T(8,128)(2,1)}, bf16[64,1408]{1,0:T(8,128)(2,1)}, u32[]{:S(2)}, u32[]{:S(2)}) collective-permute-start(bf16[64,1408]{1,0:T(8,128)(2,1)} %pad_maximum_fusion.7), channel_id=1, source_target_pairs={{0,8},{4,12},{8,0},{12,4},{1,9},{5,13},{9,1},{13,5},{2,10},{6,14},... | collective-permute-start | bytes 540680 | tf_op jit(solution)/shard_map/ppermute | solution.py:79
  128.9 33.1 %collective-permute-start.21 = (bf16[64,1408]{1,0:T(8,128)(2,1)}, bf16[64,1408]{1,0:T(8,128)(2,1)}, u32[]{:S(2)}, u32[]{:S(2)}) collective-permute-start(bf16[64,1408]{1,0:T(8,128)(2,1)} %pad_maximum_fusion.7), channel_id=1, source_target_pairs={{0,4},{4,8},{8,12},{12,0},{1,5},{5,9},{9,13},{13,1},{2,6},{6,10},{... | collective-permute-start | bytes 540680 | tf_op jit(solution)/shard_map/ppermute | solution.py:79
  207.1 19.6 %collective-permute-start.31 = (bf16[128,1408]{1,0:T(8,128)(2,1)}, bf16[128,1408]{1,0:T(8,128)(2,1)}, u32[]{:S(2)}, u32[]{:S(2)}) collective-permute-start(bf16[128,1408]{1,0:T(8,128)(2,1)} %shard_map.194), channel_id=1, source_target_pairs={{0,2},{2,0},{1,3},{3,1},{4,6},{6,4},{5,7},{7,5},{8,10},{10,8},{9,1... | collective-permute-start | bytes 1081352 | tf_op jit(solution)/shard_map/ppermute | solution.py:179
  220.1 38.8 %collective-permute-start.29 = (bf16[2,128,1024]{2,1,0:T(8,128)(2,1)}, bf16[2,128,1024]{2,1,0:T(8,128)(2,1)}, u32[]{:S(2)}, u32[]{:S(2)}) collective-permute-start(bf16[2,128,1024]{2,1,0:T(8,128)(2,1)} %fusion.50), channel_id=1, source_target_pairs={{0,1},{1,0},{2,3},{3,2},{4,5},{5,4},{6,7},{7,6},{8,9},{9,8},{10,11... | collective-permute-start | bytes 1572872 | tf_op jit(solution)/shard_map/ppermute | solution.py:55
  254.8 35.0 %collective-permute-start.33 = (bf16[512,1024]{1,0:T(8,128)(2,1)}, bf16[512,1024]{1,0:T(8,128)(2,1)S(1)}, u32[]{:S(2)}, u32[]{:S(2)}) collective-permute-start(bf16[512,1024]{1,0:T(8,128)(2,1)} %get-tuple-element.205), channel_id=1, source_target_pairs={{0,1},{1,0},{2,3},{3,2},{4,5},{5,4},{6,7},{7,6},{8,9},{9,8},{10,11... | collective-permute-start | bytes 3145736 | tf_op jit(solution)/shard_map/ppermute | solution.py:55
  255.6 19.3 %collective-permute-start.34 = (bf16[256,1408]{1,0:T(8,128)(2,1)}, bf16[256,1408]{1,0:T(8,128)(2,1)S(1)}, u32[]{:S(2)}, u32[]{:S(2)}) collective-permute-start(bf16[256,1408]{1,0:T(8,128)(2,1)} %shard_map.196), channel_id=1, source_target_pairs={{0,2},{2,0},{1,3},{3,1},{4,6},{6,4},{5,7},{7,5},{8,10},{10,8},{9,1... | collective-permute-start | bytes 2162696 | tf_op jit(solution)/shard_map/ppermute | solution.py:179
  256.3 19.3 %collective-permute-start.35 = (bf16[256,1408]{1,0:T(8,128)(2,1)}, bf16[256,1408]{1,0:T(8,128)(2,1)S(1)}, u32[]{:S(2)}, u32[]{:S(2)}) collective-permute-start(bf16[256,1408]{1,0:T(8,128)(2,1)} %shard_map.197), channel_id=1, source_target_pairs={{0,16},{16,0},{1,17},{17,1},{2,18},{18,2},{3,19},{19,3},{4,20},{20... | collective-permute-start | bytes 2162696 | tf_op jit(solution)/shard_map/ppermute | solution.py:179
  257.7 31.7 %collective-permute-start.36 = (bf16[128,2816]{1,0:T(8,128)(2,1)}, bf16[128,2816]{1,0:T(8,128)(2,1)S(1)}, u32[]{:S(2)}, u32[]{:S(2)}) collective-permute-start(bf16[128,2816]{1,0:T(8,128)(2,1)} %shard_map.198), channel_id=1, source_target_pairs={{0,2},{2,0},{1,3},{3,1},{4,6},{6,4},{5,7},{7,5},{8,10},{10,8},{9,1... | collective-permute-start | bytes 2162696 | tf_op jit(solution)/shard_map/ppermute | solution.py:179
  258.9 30.9 %collective-permute-start.37 = (bf16[128,2816]{1,0:T(8,128)(2,1)}, bf16[128,2816]{1,0:T(8,128)(2,1)S(1)}, u32[]{:S(2)}, u32[]{:S(2)}) collective-permute-start(bf16[128,2816]{1,0:T(8,128)(2,1)} %shard_map.199), channel_id=1, source_target_pairs={{0,16},{16,0},{1,17},{17,1},{2,18},{18,2},{3,19},{19,3},{4,20},{20... | collective-permute-start | bytes 2162696 | tf_op jit(solution)/shard_map/ppermute | solution.py:179
  295.9 27.2 %collective-permute-start.55 = (bf16[64,1408]{1,0:T(8,128)(2,1)S(1)}, bf16[64,1408]{1,0:T(8,128)(2,1)S(1)}, u32[]{:S(2)}, u32[]{:S(2)}) collective-permute-start(bf16[64,1408]{1,0:T(8,128)(2,1)S(1)} %get-tuple-element.264), channel_id=1, source_target_pairs={{0,12},{4,0},{8,4},{12,8},{1,13},{5,1},{9,5},{13,9},{2,14},{6,2},{... | collective-permute-start | bytes 540680 | tf_op jit(solution)/shard_map/ppermute | solution.py:236
  296.0 29.9 %collective-permute-start.57 = (bf16[64,1408]{1,0:T(8,128)(2,1)S(1)}, bf16[64,1408]{1,0:T(8,128)(2,1)S(1)}, u32[]{:S(2)}, u32[]{:S(2)}) collective-permute-start(bf16[64,1408]{1,0:T(8,128)(2,1)S(1)} %get-tuple-element.265), channel_id=1, source_target_pairs={{0,4},{4,8},{8,12},{12,0},{1,5},{5,9},{9,13},{13,1},{2,6},{6,10},{... | collective-permute-start | bytes 540680 | tf_op jit(solution)/shard_map/ppermute | solution.py:236
  298.0 28.9 %collective-permute-start.56 = (bf16[64,1408]{1,0:T(8,128)(2,1)S(1)}, bf16[64,1408]{1,0:T(8,128)(2,1)S(1)}, u32[]{:S(2)}, u32[]{:S(2)}) collective-permute-start(bf16[64,1408]{1,0:T(8,128)(2,1)S(1)} %get-tuple-element.266), channel_id=1, source_target_pairs={{0,8},{4,12},{8,0},{12,4},{1,9},{5,13},{9,1},{13,5},{2,10},{6,14},... | collective-permute-start | bytes 540680 | tf_op jit(solution)/shard_map/ppermute | solution.py:236
  323.1 39.1 %collective-permute-start.40 = (bf16[256,2816]{1,0:T(8,128)(2,1)S(1)}, bf16[256,2816]{1,0:T(8,128)(2,1)S(1)}, u32[]{:S(2)}, u32[]{:S(2)}) collective-permute-start(bf16[256,2816]{1,0:T(8,128)(2,1)S(1)} %shard_map.203), channel_id=1, source_target_pairs={{0,2},{2,0},{1,3},{3,1},{4,6},{6,4},{5,7},{7,5},{8,10},{10,8},{9,1... | collective-permute-start | bytes 4325384 | tf_op jit(solution)/shard_map/ppermute | solution.py:179
  325.8 36.4 %collective-permute-start.41 = (bf16[256,2816]{1,0:T(8,128)(2,1)S(1)}, bf16[256,2816]{1,0:T(8,128)(2,1)S(1)}, u32[]{:S(2)}, u32[]{:S(2)}) collective-permute-start(bf16[256,2816]{1,0:T(8,128)(2,1)S(1)} %shard_map.204), channel_id=1, source_target_pairs={{0,16},{16,0},{1,17},{17,1},{2,18},{18,2},{3,19},{19,3},{4,20},{20... | collective-permute-start | bytes 4325384 | tf_op jit(solution)/shard_map/ppermute | solution.py:179
  366.5 18.1 %collective-permute-start.53 = (bf16[64,2816]{1,0:T(8,128)(2,1)S(1)}, bf16[64,2816]{1,0:T(8,128)(2,1)S(1)}, u32[]{:S(2)}, u32[]{:S(2)}) collective-permute-start(bf16[64,2816]{1,0:T(8,128)(2,1)S(1)} %get-tuple-element.247), channel_id=1, source_target_pairs={{0,4},{4,8},{8,12},{12,0},{1,5},{5,9},{9,13},{13,1},{2,6},{6,10},{... | collective-permute-start | bytes 1081352 | tf_op jit(solution)/shard_map/ppermute | solution.py:236
  366.5 32.3 %collective-permute-start.52 = (bf16[64,2816]{1,0:T(8,128)(2,1)S(1)}, bf16[64,2816]{1,0:T(8,128)(2,1)S(1)}, u32[]{:S(2)}, u32[]{:S(2)}) collective-permute-start(bf16[64,2816]{1,0:T(8,128)(2,1)S(1)} %get-tuple-element.248), channel_id=1, source_target_pairs={{0,8},{4,12},{8,0},{12,4},{1,9},{5,13},{9,1},{13,5},{2,10},{6,14},... | collective-permute-start | bytes 1081352 | tf_op jit(solution)/shard_map/ppermute | solution.py:236
  372.0 30.1 %collective-permute-start.42 = (bf16[2,128,1024]{2,1,0:T(8,128)(2,1)S(1)}, bf16[2,128,1024]{2,1,0:T(8,128)(2,1)S(1)}, u32[]{:S(2)}, u32[]{:S(2)}) collective-permute-start(bf16[2,128,1024]{2,1,0:T(8,128)(2,1)S(1)} %fusion.51), channel_id=1, source_target_pairs={{0,1},{1,0},{2,3},{3,2},{4,5},{5,4},{6,7},{7,6},{8,9},{9,8},{10,11... | collective-permute-start | bytes 1572872 | tf_op jit(solution)/shard_map/ppermute | solution.py:55
  372.1 27.1 %collective-permute-start.43 = (bf16[128,2048]{1,0:T(8,128)(2,1)S(1)}, bf16[128,2048]{1,0:T(8,128)(2,1)S(1)}, u32[]{:S(2)}, u32[]{:S(2)}) collective-permute-start(bf16[128,2048]{1,0:T(8,128)(2,1)S(1)} %shard_map.206), channel_id=1, source_target_pairs={{0,2},{2,0},{1,3},{3,1},{4,6},{6,4},{5,7},{7,5},{8,10},{10,8},{9,1... | collective-permute-start | bytes 1572872 | tf_op jit(solution)/shard_map/ppermute | solution.py:179
  375.3 23.8 %collective-permute-start.44 = (bf16[128,2048]{1,0:T(8,128)(2,1)S(1)}, bf16[128,2048]{1,0:T(8,128)(2,1)S(1)}, u32[]{:S(2)}, u32[]{:S(2)}) collective-permute-start(bf16[128,2048]{1,0:T(8,128)(2,1)S(1)} %shard_map.207), channel_id=1, source_target_pairs={{0,16},{16,0},{1,17},{17,1},{2,18},{18,2},{3,19},{19,3},{4,20},{20... | collective-permute-start | bytes 1572872 | tf_op jit(solution)/shard_map/ppermute | solution.py:179
  400.6 25.6 %collective-permute-start.46 = (bf16[256,2048]{1,0:T(8,128)(2,1)S(1)}, bf16[256,2048]{1,0:T(8,128)(2,1)S(1)}, u32[]{:S(2)}, u32[]{:S(2)}) collective-permute-start(bf16[256,2048]{1,0:T(8,128)(2,1)S(1)} %shard_map.210), channel_id=1, source_target_pairs={{0,16},{16,0},{1,17},{17,1},{2,18},{18,2},{3,19},{19,3},{4,20},{20... | collective-permute-start | bytes 3145736 | tf_op jit(solution)/shard_map/ppermute | solution.py:179
  402.1 25.3 %collective-permute-start.45 = (bf16[256,2048]{1,0:T(8,128)(2,1)S(1)}, bf16[256,2048]{1,0:T(8,128)(2,1)S(1)}, u32[]{:S(2)}, u32[]{:S(2)}) collective-permute-start(bf16[256,2048]{1,0:T(8,128)(2,1)S(1)} %shard_map.209), channel_id=1, source_target_pairs={{0,2},{2,0},{1,3},{3,1},{4,6},{6,4},{5,7},{7,5},{8,10},{10,8},{9,1... | collective-permute-start | bytes 3145736 | tf_op jit(solution)/shard_map/ppermute | solution.py:179
  431.6 20.2 %collective-permute-start.48 = (bf16[64,2048]{1,0:T(8,128)(2,1)S(1)}, bf16[64,2048]{1,0:T(8,128)(2,1)}, u32[]{:S(2)}, u32[]{:S(2)}) collective-permute-start(bf16[64,2048]{1,0:T(8,128)(2,1)S(1)} %get-tuple-element.253), channel_id=1, source_target_pairs={{0,8},{4,12},{8,0},{12,4},{1,9},{5,13},{9,1},{13,5},{2,10},{6,14},... | collective-permute-start | bytes 786440 | tf_op jit(solution)/shard_map/ppermute | solution.py:236
  (113 other events, 1000.4 us)

commit v5 on v4

--- a/solution.py
+++ b/solution.py
@@ -87,14 +87,14 @@
 
 def gather_near(arrived):
     own = joined_rows(arrived)
-    return (own,) + tied(ring_gather("inner", own), ring_gather("dp", own))
+    return own, ring_gather("inner", own), ring_gather("dp", own)
 
 
 def gather_far(own, along_x, along_y):
     half = own.shape[0] // 2
     one = ring_gather("inner", joined_rows([piece[:half] for piece in along_y]))
     two = ring_gather("dp", joined_rows([piece[half:] for piece in along_x]))
-    return tied(one, two)
+    return one, two
 
 
 def in_pieces(own, along_x, along_y, one, two):
@@ -124,23 +124,26 @@
     return (jnp.arange(width, dtype=jnp.int32)[:, None] == source[None, :]).astype(BF16)
 
 
-def rows_kernel(pairs, places, *refs):
-    lefts, rights, rest = refs[:pairs], refs[pairs : 2 * pairs], refs[2 * pairs :]
-    adds, out_ref = rest[:-1], rest[-1]
-    start = 0
-    for left, right in zip(lefts, rights):
-        columns = slice(start, start + right.shape[1])
-        total = contract_rows(left[...], right[...])
-        full = [add for add in adds if add.shape[0] == total.shape[0]]
-        for add in full:
-            total = total + add[:, columns].astype(F32)
-        out_ref[:, columns] = total.astype(BF16)
-        for add, at in zip(adds, places):
-            if add.shape[0] != total.shape[0]:
-                span = slice(at, at + add.shape[0])
-                part = total[span] + add[:, columns].astype(F32)
-                out_ref[span, columns] = part.astype(BF16)
-        start = columns.stop
+def rows_kernel(pairs, layout, *refs):
+    rights, refs = refs[:pairs], refs[pairs:]
+    inputs, outs = refs[: -len(layout)], refs[-len(layout) :]
+    for places, out_ref in zip(layout, outs):
+        lefts, adds = inputs[:pairs], inputs[pairs : pairs + len(places)]
+        inputs = inputs[pairs + len(places) :]
+        start = 0
+        for left, right in zip(lefts, rights):
+            columns = slice(start, start + right.shape[1])
+            start = columns.stop
+            total = contract_rows(left[...], right[...])
+            for add in adds:
+                if add.shape[0] == total.shape[0]:
+                    total = total + add[:, columns].astype(F32)
+            out_ref[:, columns] = total.astype(BF16)
+            for add, at in zip(adds, places):
+                if add.shape[0] != total.shape[0]:
+                    span = slice(at, at + add.shape[0])
+                    part = total[span] + add[:, columns].astype(F32)
+                    out_ref[span, columns] = part.astype(BF16)
 
 
 class GradSum:
@@ -156,55 +159,52 @@
         self.at_one = self.at_y + (self.dp - 1) * 2 * self.half
         self.at_two = self.at_one + (self.inner - 1) * (self.dp - 1) * self.half
 
-    def rows(self, start, count, adds):
-        adds = [(rows, place) for rows, place in adds if rows is not None]
-        lefts, index = self.lefts, start // max(count, 1)
-        if count % LANES or start % count:
-            lefts, index = [left[:, start : start + count] for left in lefts], 0
-        depth = lefts[0].shape[0]
+    def rows(self, *parts):
+        depth = self.lefts[0].shape[0]
         columns = sum(right.shape[1] for right in self.rights)
+        ins, outs, layout = [whole(right) for right in self.rights], [], []
+        for start, count, adds in parts:
+            adds = [(rows, place) for rows, place in adds if rows is not None]
+            lefts, index = self.lefts, start // count
+            if count % LANES or start % count:
+                lefts, index = [left[:, start : start + count] for left in lefts], 0
+            ins += [
+                (left, (depth, count), lambda i, index=index: (0, index)) for left in lefts
+            ]
+            ins += [whole(rows) for rows, _ in adds]
+            outs.append(((count, columns), BF16, (count, columns), lambda i: (0, 0)))
+            layout.append([place for _, place in adds])
         return call(
-            functools.partial(rows_kernel, len(lefts), [place for _, place in adds]),
-            (1,),
-            [(left, (depth, count), lambda i: (0, index)) for left in lefts]
-            + [whole(right) for right in self.rights]
-            + [whole(rows) for rows, _ in adds],
-            [((count, columns), BF16, (count, columns), lambda i: (0, 0))],
-        )[0]
-
-    def ring(self, axis, chunk, first):
+            functools.partial(rows_kernel, len(self.rights), layout), (1,), ins, outs
+        )
+
+    def ring(self, axis, part, first):
         arrived = None
         for step in range(1, lax.axis_size(axis)):
-            sent = first if step == 1 else chunk(step, arrived)
+            sent = first if step == 1 else self.rows(part(step, arrived))[0]
             arrived = lax.ppermute(sent, axis, forward(axis))
         return arrived
 
     def one(self, distance, arrived):
         count = (self.dp - 1) * self.half
-        return self.rows(self.at_one + (distance - 1) * count, count, [(arrived, 0)])
+        return (self.at_one + (distance - 1) * count, count, [(arrived, 0)])
 
     def two(self, distance, arrived):
         count = (self.inner - 1) * self.half
-        return self.rows(self.at_two + (distance - 1) * count, count, [(arrived, 0)])
+        return (self.at_two + (distance - 1) * count, count, [(arrived, 0)])
 
     def far(self):
-        if self.dp == 1 or self.inner == 1:
-            return (None, None)
-        return self.one(1, None), self.two(1, None)
+        return self.rows(self.one(1, None), self.two(1, None))
 
     def send_far(self, firsts):
-        if firsts[0] is None:
-            return firsts
-        return tied(
+        return (
             self.ring("inner", self.one, firsts[0]), self.ring("dp", self.two, firsts[1])
         )
 
     def along(self, start, distance, arrived, extra, place):
         count = 2 * self.half
-        if extra is not None:
-            extra = extra[(distance - 1) * self.half : distance * self.half]
-        at = start + (distance - 1) * count
-        return self.rows(at, count, [(arrived, 0), (extra, place)])
+        extra = extra[(distance - 1) * self.half : distance * self.half]
+        return (start + (distance - 1) * count, count, [(arrived, 0), (extra, place)])
 
     def along_x(self, distance, arrived):
         return self.along(self.at_x, distance, arrived, self.sums[1], self.half)
@@ -214,29 +214,30 @@
 
     def near(self, sums):
         self.sums = sums
+        return self.rows(self.along_x(1, None), self.along_y(1, None))
+
+    def send_near(self, firsts):
         return (
-            self.along_x(1, None) if self.inner > 1 else None,
-            self.along_y(1, None) if self.dp > 1 else None,
-        )
-
-    def send_near(self, firsts):
-        return tied(
             self.ring("inner", self.along_x, firsts[0]),
             self.ring("dp", self.along_y, firsts[1]),
         )
 
     def own(self, nears):
-        return self.rows(0, 2 * self.half, [(near, 0) for near in nears])
-
-    def finish(self, own):
-        def cut(distance):
-            return own[distance * self.shard : (distance + 1) * self.shard]
-
-        arrived = [
-            lax.ppermute(cut(distance), "outer", forward("outer", self.outer - distance))
+        return self.rows((0, 2 * self.half, [(near, 0) for near in nears]))[0]
+
+    def cut(self, own, distance):
+        return own[distance * self.shard : (distance + 1) * self.shard]
+
+    def send_direct(self, own):
+        return [
+            lax.ppermute(
+                self.cut(own, distance), "outer", forward("outer", self.outer - distance)
+            )
             for distance in range(1, self.outer)
         ]
-        total = sum([piece.astype(F32) for piece in arrived], cut(0).astype(F32))
+
+    def total(self, own, arrived):
+        total = sum([piece.astype(F32) for piece in arrived], self.cut(own, 0).astype(F32))
         return total.reshape(2, self.shard // 2, -1)
 
 
@@ -527,102 +528,151 @@
     return (array, (block, array.shape[1]), lambda i: (i, 0))
 
 
-def out_kernel(att_ref, weight_ref, x_ref, gain_ref, hidden_ref, norm_ref):
-    hidden = x_ref[...].astype(F32) + matmul(att_ref[...], weight_ref[...])
+def weight_kernel(count, other_ref, own_order_ref, other_order_ref, *refs):
+    start = 0
+    out_ref = refs[count]
+    for piece in refs[:count]:
+        span = slice(start, start + piece.shape[0])
+        total = matmul(piece[...], own_order_ref[...])
+        total = total + matmul(other_ref[span, :], other_order_ref[...])
+        out_ref[span, :] = total.astype(BF16)
+        start = span.stop
+
+
+def out_weight(pieces, own, other, own_order, other_order):
+    side, width = own_order.shape
+    if len(pieces) == 1:
+        own_pieces = [(own, own.shape, lambda i: (0, 0))]
+    else:
+        own_pieces, start = [], 0
+        for piece in pieces:
+            count = piece.shape[0]
+            own_pieces.append(
+                (own, (count, side), lambda i, index=start // count: (index, 0))
+            )
+            start += count
+    return call(
+        functools.partial(weight_kernel, len(own_pieces)),
+        (1,),
+        [whole(other), whole(own_order), whole(other_order)] + own_pieces,
+        [((width, width), BF16, (width, width), lambda i: (0, 0))],
+    )[0]
+
+
+def out_kernel(
+    own_ref, other_ref, own_order_ref, other_order_ref, weight_ref, x_ref, gain_ref,
+    att_ref, hidden_ref, norm_ref,
+):
+    attended = matmul(own_ref[...], own_order_ref[...])
+    attended = (attended + matmul(other_ref[...], other_order_ref[...])).astype(BF16)
+    att_ref[...] = attended
+    hidden = x_ref[...].astype(F32) + matmul(attended, weight_ref[...])
     hidden_ref[...] = hidden
     norm_ref[...] = (normalise(hidden)[0] * gain_ref[1:2, :]).astype(BF16)
 
 
-def out_project(attended, weight, tokens, gains):
+def out_project(own, other, own_order, other_order, weight, tokens, gains):
     rows, width = tokens.shape
-    block = rows // 4
+    block = rows // 2
     return call(
         out_kernel,
-        (4,),
-        [by_rows(attended, block), whole(weight), by_rows(tokens, block), whole(gains)],
+        (2,),
+        [by_rows(own, block), by_rows(other, block), whole(own_order), whole(other_order)]
+        + [whole(weight), by_rows(tokens, block), whole(gains)],
         [
-            ((rows, width), kind, (block, width), lambda i: (i, 0)) for kind in (F32, BF16)
+            ((rows, width), kind, (block, width), lambda i: (i, 0))
+            for kind in (BF16, F32, BF16)
         ],
-        limit=24,
     )
 
 
 def hidden_back_kernel(
-    part_ref, other_ref, hidden_ref, g_ref, gain_ref, weight_ref, grad_ref, low_ref, att_ref
+    part_ref, other_ref, hidden_ref, g_ref, gain_ref, weight_ref, order_ref,
+    grad_ref, side_ref, att_ref,
 ):
     unit, scale = normalise(hidden_ref[...])
     incoming = part_ref[...] + other_ref[...].astype(F32)
     grad = g_ref[...].astype(F32) + norm_back(unit, scale, gain_ref[1:2, :], incoming)
     low = grad.astype(BF16)
     grad_ref[...] = grad
-    low_ref[...] = low
-    att_ref[...] = contract_cols(low, weight_ref[...]).astype(BF16)
-
-
-def hidden_back(part, other, hidden, grad_output, gains, weight):
+    side_ref[...] = contract_cols(low, order_ref[...]).astype(BF16)
+    attended = contract_cols(low, weight_ref[...]).astype(BF16)
+    att_ref[...] = contract_cols(attended, order_ref[...]).astype(BF16)
+
+
+def hidden_back(part, other, hidden, grad_output, gains, weight, own_order):
     rows, width = hidden.shape
-    block, side = rows // 4, weight.shape[0]
+    block, side = rows // 2, own_order.shape[0]
     return call(
         hidden_back_kernel,
-        (4,),
+        (2,),
         [by_rows(array, block) for array in (part, other, hidden, grad_output)]
-        + [whole(gains), whole(weight)],
+        + [whole(gains), whole(weight), whole(own_order)],
         [
             ((rows, size), kind, (block, size), lambda i: (i, 0))
-            for size, kind in ((width, F32), (width, BF16), (side, BF16))
+            for size, kind in ((width, F32), (side, BF16), (side, BF16))
         ],
-        limit=24,
-    )
-
-
-def feed_kernel(count, norm_ref, *refs):
-    gates, ups = refs[:count], refs[count : 2 * count]
-    mixed_ref, factor_ref, active_ref = refs[2 * count :]
-    gate, up = piece_matmul(norm_ref, gates), piece_matmul(norm_ref, ups)
-    below = 0.5 * (1.0 + lax.erf(gate * 0.5**0.5))
-    active = gate * below
-    mixed_ref[...] = (active * up).astype(BF16)
-    active_ref[...] = active
-    density = jnp.exp(-0.5 * gate * gate) * (2.0 * np.pi) ** -0.5
-    factor_ref[...] = up * (below + gate * density)
+    )
+
+
+def column_spans(width):
+    return [slice(at, min(at + 2 * LANES, width)) for at in range(0, width, 2 * LANES)]
+
+
+def tile_matmul(left, pieces, columns):
+    total, start = None, 0
+    for piece in pieces:
+        part = matmul(left[:, start : start + piece.shape[0]], piece[:, columns])
+        total = part if total is None else total + part
+        start += piece.shape[0]
+    return total
+
+
+def feed_kernel(norm_ref, *refs):
+    pieces, (mixed_ref, factor_ref, active_ref) = refs[:-3], refs[-3:]
+    units = mixed_ref.shape[1]
+    for span in column_spans(units):
+        gate = tile_matmul(norm_ref, pieces, span)
+        up = tile_matmul(norm_ref, pieces, slice(units + span.start, units + span.stop))
+        below = 0.5 * (1.0 + lax.erf(gate * 0.5**0.5))
+        active = gate * below
+        mixed_ref[:, span] = (active * up).astype(BF16)
+        active_ref[:, span] = active
+        density = jnp.exp(-0.5 * gate * gate) * (2.0 * np.pi) ** -0.5
+        factor_ref[:, span] = up * (below + gate * density)
 
 
 def feed(normed, pieces, units):
     rows = normed.shape[0]
-    tiles = units // LANES
+    block = rows // 2
     return call(
-        functools.partial(feed_kernel, len(pieces)),
-        (tiles,),
-        [whole(normed)]
-        + [(piece, (piece.shape[0], LANES), lambda j: (0, j)) for piece in pieces]
-        + [(piece, (piece.shape[0], LANES), lambda j: (0, j + tiles)) for piece in pieces],
+        feed_kernel,
+        (2,),
+        [by_rows(normed, block)] + [whole(piece) for piece in pieces],
         [
-            ((rows, units), kind, (rows, LANES), lambda j: (0, j))
+            ((rows, units), kind, (block, units), lambda i: (i, 0))
             for kind in (BF16, F32, F32)
         ],
-        limit=24,
-    )
-
-
-def feed_back_kernel(count, g_ref, factor_ref, active_ref, *refs):
-    grad = piece_matmul(g_ref, refs[:count])
-    gate_ref, up_ref = refs[count:]
-    gate_ref[...] = (grad * factor_ref[...]).astype(BF16)
-    up_ref[...] = (grad * active_ref[...]).astype(BF16)
+    )
+
+
+def feed_back_kernel(g_ref, factor_ref, active_ref, *refs):
+    pieces, (gate_ref, up_ref) = refs[:-2], refs[-2:]
+    for span in column_spans(factor_ref.shape[1]):
+        grad = tile_matmul(g_ref, pieces, span)
+        gate_ref[:, span] = (grad * factor_ref[:, span]).astype(BF16)
+        up_ref[:, span] = (grad * active_ref[:, span]).astype(BF16)
 
 
 def feed_back(grad_output, factor, active, pieces):
     rows, units = factor.shape
-
-    def tile(array):
-        return (array, (array.shape[0], LANES), lambda j: (0, j))
-
+    block = rows // 2
     return call(
-        functools.partial(feed_back_kernel, len(pieces)),
-        (units // LANES,),
-        [whole(grad_output), tile(factor), tile(active)] + [tile(piece) for piece in pieces],
-        [((rows, units), BF16, (rows, LANES), lambda j: (0, j)) for _ in range(2)],
-        limit=24,
+        feed_back_kernel,
+        (2,),
+        [by_rows(array, block) for array in (grad_output, factor, active)]
+        + [whole(piece) for piece in pieces],
+        [((rows, units), BF16, (block, units), lambda i: (i, 0)) for _ in range(2)],
     )
 
 
@@ -667,19 +717,10 @@
     pair_two, one, low, high, pair_tokens = tied(pair_two, one, low, high, pair_tokens)
     two = direct_sends(pair_two)
     near = gather_near(one)
-    far = gather_far(*near)
-    pair_three, two, near, far = tied(pair_three, two, near, far)
-    three = direct_sends(pair_three)
-    first = in_pieces(*near, *far)
-    two_near = gather_near(two)
-
     order = arrival_order(width, shard_rows)
 
     def in_order(value):
         return matmul(value, order).astype(BF16)
-
-    def out_of_order(value):
-        return contract_cols(value, order).astype(BF16)
 
     window_tokens = jnp.concatenate([low, pair_tokens, high], 1).reshape(-1, width)
     window_tokens = in_order(window_tokens)
@@ -698,22 +739,38 @@
     key_ids = lax.dynamic_slice_in_dim(ids_padded, start, window, 1)[:, None, :]
     query_ids = lax.dynamic_slice_in_dim(doc_ids, start, length, 1)[:, :, None]
 
+    own_order = lax.dynamic_slice_in_dim(order, core * side, side, 0)
+    other_order = lax.dynamic_slice_in_dim(order, (1 - core) * side, side, 0)
+    prepared = (window_tokens, own_tokens, grad_output, order, own_order, other_order)
+    prepared += (cosine, sine, key_ids, query_ids, pair_three)
+    prepared, two, near = tied(prepared, two, near)
+    window_tokens, own_tokens, grad_output, order, own_order, other_order = prepared[:6]
+    cosine, sine, key_ids, query_ids, pair_three = prepared[6:]
+
+    far = gather_far(*near)
+    two_near = gather_near(two)
+    three = direct_sends(pair_three)
+    first = in_pieces(*near, *far)
     joined, window_norm, gain_rows = project(window_tokens, first, cosine, sine, side)
-    joined, two_near = tied(joined, two_near)
+    out_half = joined_rows([piece[:, 3 * side + LANES :] for piece in first])
+    weight = out_weight(first, out_half, swap(out_half), own_order, other_order)
+    joined, weight, first, two_near, three = tied(joined, weight, first, two_near, three)
+
     two_far = gather_far(*two_near)
     joined = joined.reshape(streams, window, 3 * side)
-    attended_half = attend(block, joined, query_ids, key_ids).reshape(rows, side)
-    out_half = joined_rows([piece[:, 3 * side + LANES :] for piece in first])
-    full_out = ordered(out_half, swap(out_half), 1)
-    full_out = matmul(order, in_order(full_out)).astype(BF16)
-    attended_half, full_out, two_near, two_far, three = tied(
-        attended_half, full_out, two_near, two_far, three
+    attended = attend(block, joined, query_ids, key_ids).reshape(rows, side)
+    attended_other = swap(attended)
+    attended, attended_other, two_near, two_far = tied(
+        attended, attended_other, two_near, two_far
     )
     in_half = in_pieces(*two_near, *two_far)
+
     three_near = gather_near(three)
-    attended_low = ordered(attended_half, swap(attended_half), 1)
-    hidden, normed_mlp_low = out_project(attended_low, full_out, own_tokens, gain_rows)
+    attended_low, hidden, normed_mlp_low = out_project(
+        attended, attended_other, own_order, other_order, weight, own_tokens, gain_rows
+    )
     hidden, normed_mlp_low, three_near = tied(hidden, normed_mlp_low, three_near)
+
     three_far = gather_far(*three_near)
     mixed_low, factor, active = feed(normed_mlp_low, in_half, padded)
     mixed_low, factor, active, three_near, three_far = tied(
@@ -725,42 +782,45 @@
     down_far = sum_down.send_far(sum_down.far())
     grad_gate, grad_up = feed_back(grad_output, factor, active, down_half)
     grad_gate, grad_up, down_far = tied(grad_gate, grad_up, down_far)
-    sum_in = GradSum([normed_mlp_low], [jnp.concatenate([grad_gate, grad_up], 1)], shard_rows)
-    sent_down, sent_in = sum_down.near(down_far), sum_in.far()
-    grad_gate, grad_up, sent_down, sent_in = tied(grad_gate, grad_up, sent_down, sent_in)
-    down_near = sum_down.send_near(sent_down)
+
+    sum_in = GradSum([normed_mlp_low] * 2, [grad_gate, grad_up], shard_rows)
+    down_near = sum_down.send_near(sum_down.near(down_far))
+    sent_in = sum_in.far()
+    part, part_low = back_project([grad_gate, grad_up], in_half, [F32, BF16])
+    part, part_low, down_near, sent_in = tied(part, part_low, down_near, sent_in)
+
     in_far = sum_in.send_far(sent_in)
-    part, part_low = back_project([grad_gate, grad_up], in_half, [F32, BF16])
-    out_rows = lax.dynamic_slice_in_dim(full_out, core * side, side, 0)
-    grad_hidden, grad_hidden_low, grad_attended = hidden_back(
-        part, swap(part_low), hidden, grad_output, gain_rows, out_rows
-    )
-    grad_attended, down_near, in_far = tied(grad_attended, down_near, in_far)
-    down_total = sum_down.finish(sum_down.own(down_near))
-
+    down_own = sum_down.own(down_near)
+    down_arrived = sum_down.send_direct(down_own)
+    grad_hidden, hidden_side, grad_attended = hidden_back(
+        part, swap(part_low), hidden, grad_output, gain_rows, weight, own_order
+    )
+    grad_attended, in_far, down_arrived = tied(grad_attended, in_far, down_arrived)
+
+    in_near = sum_in.send_near(sum_in.near(in_far))
     grad_query, mid, to_lower, to_upper = attend_back(
         block, joined, query_ids, key_ids, grad_attended.reshape(streams, length, side),
         cosine, sine,
     )
-    sent_in = sum_in.near(in_far)
-    to_lower, to_upper, sent_in = tied(to_lower, to_upper, sent_in)
     from_lower = lax.ppermute(to_upper, ("outer", "inner"), onward)
     from_upper = lax.ppermute(to_lower, ("outer", "inner"), back)
-    in_near = sum_in.send_near(sent_in)
+    from_lower, from_upper, in_near = tied(from_lower, from_upper, in_near)
+
     grad_joined = join_grads(grad_query, mid, from_lower, from_upper, cosine, sine)
     grad_joined = grad_joined.reshape(rows, 3 * side)
-    hidden_side = lax.dynamic_slice_in_dim(out_of_order(grad_hidden_low), core * side, side, 1)
     normed_low = window_norm.reshape(streams, window, width)[:, HALF : HALF + length]
     sum_attn = GradSum(
-        [normed_low.reshape(rows, width), in_order(attended_low)],
-        [grad_joined, hidden_side],
-        shard_rows,
-    )
-    sent_attn = sum_attn.far()
-    sent_attn, in_near, grad_joined = tied(sent_attn, in_near, grad_joined)
-    in_own = sum_in.own(in_near)
+        [normed_low.reshape(rows, width), attended_low], [grad_joined, hidden_side], shard_rows
+    )
+    sent_attn, in_own = sum_attn.far(), sum_in.own(in_near)
+    sent_attn, in_own, grad_joined = tied(sent_attn, in_own, grad_joined)
+
     attn_far = sum_attn.send_far(sent_attn)
-    in_total = sum_in.finish(in_own)
+    attn_far, grad_joined, mixed_low, grad_hidden, hidden = tied(
+        attn_far, grad_joined, mixed_low, grad_hidden, hidden
+    )
+    in_arrived = sum_in.send_direct(in_own)
+    attn_near = sum_attn.send_near(sum_attn.near(attn_far))
 
     def own_rows(value):
         value = value.reshape(streams, 2, block, width)
@@ -774,7 +834,8 @@
 
     (out_part,) = back_project([mixed_low], down_half, [F32])
     output = own_rows(hidden)[0] + summed_rows(out_part)
-    output = out_of_order(output.astype(BF16).reshape(-1, width)).reshape(tokens.shape)
+    output = contract_cols(output.astype(BF16).reshape(-1, width), order)
+    output = output.astype(BF16).reshape(tokens.shape)
 
     (norm_part,) = back_project([grad_joined], first, [F32])
     grad_normed = summed_rows(norm_part)
@@ -788,8 +849,11 @@
         preferred_element_type=F32,
     ).reshape(tokens.shape)
 
-    attn_near = sum_attn.send_near(sum_attn.near(attn_far))
-    attn_total = sum_attn.finish(sum_attn.own(attn_near))
+    attn_near, in_arrived = tied(attn_near, in_arrived)
+    attn_own = sum_attn.own(attn_near)
+    attn_total = sum_attn.total(attn_own, sum_attn.send_direct(attn_own))
+    down_total = sum_down.total(down_own, down_arrived)
+    in_total = sum_in.total(in_own, in_arrived)
 
     def interleaved(pair, start, parts, stride, size):
         cuts = []

time: 461 us -> 411 us (0.89)
  waiting for transfers between devices: 208 us -> 176 us
  Pallas kernels: 92.8 us -> 80.8 us
  matrix products: 18.7 us -> 8.83 us
    ppermute x12, waiting for transfers between devices: 73.3 us -> 23.7 us  [ring(): arrived = lax.ppermute(sent, axis, forward(axis))]
    pallas_call x26 -> x21, Pallas kernels: 92.8 us -> 80.8 us  [call(): pl.pallas_call(kernel, grid=grid, in_specs=[pl.BlockSpec(block, index) fo...]
    ppermute x1, waiting for transfers between devices: 5.33 us -> 13.8 us  [shards(): from_lower = lax.ppermute(to_upper, ('outer', 'inner'), onward)]
    ppermute x12, waiting for transfers between devices: 42.8 us -> 51 us  [ring_gather(): pieces.append(lax.ppermute(pieces[-1], axis, forward(axis)))]
    dot_general x4 -> x2, matrix products: 12 us -> 4.15 us  [matmul(): return jnp.dot(left, right, preferred_element_type=F32)]
    ppermute x9, starting transfers between devices: 12.1 us -> 17.2 us  [send_direct(): lax.ppermute(self.cut(own, distance), 'outer', forward('outer', self.oute...]
    unnamed x195 -> x196, local copies, waits for them, and re-layouts: 32.6 us -> 33.3 us
  transfers between devices with their start and end apart: 59 -> 59, of which waited for: 29 -> 28; matrix products, arithmetic and copies ran while one was open for 11% -> 8% of each run, Pallas kernels for 19% -> 17%
where the time goes in v5:
time: 411 us; the launch traced here: 403 us
  waiting for transfers between devices  176 us (43%)
  Pallas kernels  80.8 us (20%)
  starting transfers between devices  71.7 us (17%)
  local copies, waits for them, and re-layouts  48.7 us (12%)
  other arithmetic  14.8 us (4%)
  matrix products  8.83 us (2%)
    pallas_call x21, Pallas kernels, call(): pl.pallas_call(kernel, grid=grid, in_specs=[pl.BlockSpec(block, index) fo...  80.8 us
    ppermute x12, waiting for transfers between devices, ring_gather(): pieces.append(lax.ppermute(pieces[-1], axis, forward(axis)))  51 us
    ppermute x9, waiting for transfers between devices, send_direct(): lax.ppermute(self.cut(own, distance), 'outer', forward('outer', self.oute...  41.1 us
    unnamed x196, local copies, waits for them, and re-layouts  33.3 us
    ppermute x9, waiting for transfers between devices, direct_sends(): lax.ppermute(rows, 'outer', forward('outer', distance))  32.3 us
    ppermute x12, waiting for transfers between devices, ring(): arrived = lax.ppermute(sent, axis, forward(axis))  23.7 us
    ppermute x9, starting transfers between devices, send_direct(): lax.ppermute(self.cut(own, distance), 'outer', forward('outer', self.oute...  17.2 us
    ppermute x9, starting transfers between devices, direct_sends(): lax.ppermute(rows, 'outer', forward('outer', distance))  15.9 us
  transfers between devices with their start and end apart: 59, of which 28 were waited for; matrix products, arithmetic and copies ran while one was open for 8% of the time, Pallas kernels for 17%

profile of v5, /device:TPU:0, one launch (start us, length us, event | category | flops | bytes accessed | tf_op | source)
XLA Modules:
  0.0 403.0 jit_solution(17590982777586763954)
XLA Ops:
  12.5 4.7 %collective-permute-start.5 = (bf16[64,2176]{1,0:T(8,128)(2,1)S(1)}, bf16[64,2176]{1,0:T(8,128)(2,1)S(1)}, u32[]{:S(2)}, u32[]{:S(2)}) collective-permute-start(bf16[64,2176]{1,0:T(8,128)(2,1)S(1)} %pad_maximum_fusion.5), channel_id=1, source_target_pairs={{0,12},{4,0},{8,4},{12,8},{1,13},{5,1},{9,5},{13,9},{2,14},{6,2},{... | collective-permute-start | bytes 835592 | tf_op jit(solution)/shard_map/ppermute | solution.py:79
  22.6 4.6 %collective-permute-start.6 = (bf16[2,64,1024]{2,1,0:T(8,128)(2,1)S(1)}, bf16[2,64,1024]{2,1,0:T(8,128)(2,1)S(1)}, u32[]{:S(2)}, u32[]{:S(2)}) collective-permute-start(bf16[2,64,1024]{2,1,0:T(8,128)(2,1)S(1)} %get-tuple-element.285), channel_id=1, source_target_pairs={{0,2},{2,4},{4,6},{6,8},{8,10},{10,12},{12,14},{1,3},{3,5},{5,7},{... | collective-permute-start | bytes 786440 | tf_op jit(solution)/shard_map/ppermute | solution.py:712
  30.0 5.4 %collective-permute-done.6 = bf16[2,64,1024]{2,1,0:T(8,128)(2,1)S(1)} collective-permute-done((bf16[2,64,1024]{2,1,0:T(8,128)(2,1)S(1)}, bf16[2,64,1024]{2,1,0:T(8,128)(2,1)S(1)}, u32[]{:S(2)}, u32[]{:S(2)}) %collective-permute-start.6) | collective-permute-done | bytes 262176 | tf_op jit(solution)/shard_map/ppermute | solution.py:712
  35.4 6.6 %collective-permute-done.4 = bf16[64,2176]{1,0:T(8,128)(2,1)S(1)} collective-permute-done((bf16[64,2176]{1,0:T(8,128)(2,1)S(1)}, bf16[64,2176]{1,0:T(8,128)(2,1)S(1)}, u32[]{:S(2)}, u32[]{:S(2)}) %collective-permute-start.4) | collective-permute-done | bytes 278560 | tf_op jit(solution)/shard_map/ppermute | solution.py:79
  50.5 5.3 %collective-permute-start.11 = (bf16[64,2816]{1,0:T(8,128)(2,1)S(1)}, bf16[64,2816]{1,0:T(8,128)(2,1)S(1)}, u32[]{:S(2)}, u32[]{:S(2)}) collective-permute-start(bf16[64,2816]{1,0:T(8,128)(2,1)S(1)} %pad_maximum_fusion.3), channel_id=1, source_target_pairs={{0,8},{4,12},{8,0},{12,4},{1,9},{5,13},{9,1},{13,5},{2,10},{6,14},... | collective-permute-start | bytes 1081352 | tf_op jit(solution)/shard_map/ppermute | solution.py:79
  61.8 24.7 %collective-permute-done.11 = bf16[64,2816]{1,0:T(8,128)(2,1)S(1)} collective-permute-done((bf16[64,2816]{1,0:T(8,128)(2,1)S(1)}, bf16[64,2816]{1,0:T(8,128)(2,1)S(1)}, u32[]{:S(2)}, u32[]{:S(2)}) %collective-permute-start.11) | collective-permute-done | bytes 360480 | tf_op jit(solution)/shard_map/ppermute | solution.py:79
  94.1 39.9 %collective-permute-done.15.refs_3_.refs_8_.refs_4_ = bf16[128,2176]{1,0:T(8,128)(2,1)S(1)} collective-permute-done((bf16[128,2176]{1,0:T(8,128)(2,1)S(1)}, bf16[128,2176]{1,0:T(8,128)(2,1)S(1)}, u32[]{:S(2)}, u32[]{:S(2)}) %collective-permute-start.15) | collective-permute-done | bytes 557088 | tf_op jit(solution)/shard_map/ppermute | solution.py:73
  150.3 7.6 %shard_map.188 = (bf16[768,1536]{1,0:T(8,128)(2,1)S(1)}, bf16[768,1024]{1,0:T(8,128)(2,1)S(1)}, f32[8,1024]{1,0:T(8,128)S(1)}) custom-call(bf16[768,1024]{1,0:T(8,128)(2,1)S(1)} %copy-done.38, f32[384,128]{1,0:T(8,128)S(1)} %copy-done.39, f32[384,128]{1,0:T(8,128)S(1)} %copy-done.42, bf16[256,2176]{1,0:T(8,128)(2,1)S(1)} %copy-done.23, ...), custom_call_target="tpu_custom_call" | custom-call | flops 1024 | bytes 1024 | tf_op jit(solution)/shard_map/pallas_call | solution.py:37
  175.4 8.0 %shard_map.190 = bf16[2,256,512]{2,1,0:T(8,128)(2,1)S(1)} custom-call(bf16[2,384,1536]{2,1,0:T(8,128)(2,1)S(1)} %bitcast.111, bf16[2,384,1536]{2,1,0:T(8,128)(2,1)S(1)} %bitcast.112, bf16[2,384,1536]{2,1,0:T(8,128)(2,1)S(1)} %bitcast.113, s32[2,256,1]{2,1,0:T(8,128)S(1)} %copy.41.qid_ref, s32[2,1,384]{2,1,0:T(1,128)S(1)} %broadcast_in_dim.4.kid_ref), custom_call_target="tpu_custom_call" | custom-call | flops 1024 | bytes 1024 | tf_op jit(solution)/shard_map/pallas_call | solution.py:37
  187.2 3.0 shard_map.191
  191.3 10.2 %collective-permute-done.27.refs_2_.refs_3_ = bf16[256,1408]{1,0:T(8,128)(2,1)} collective-permute-done((bf16[256,1408]{1,0:T(8,128)(2,1)}, bf16[256,1408]{1,0:T(8,128)(2,1)}, u32[]{:S(2)}, u32[]{:S(2)}) %collective-permute-start.27) | collective-permute-done | bytes 720928 | tf_op jit(solution)/shard_map/ppermute | solution.py:73
  205.6 7.5 %shard_map.192 = (bf16[512,1408]{1,0:T(8,128)(2,1)S(1)}, f32[512,1408]{1,0:T(8,128)S(1)}, f32[512,1408]{1,0:T(8,128)S(1)}) custom-call(bf16[512,1024]{1,0:T(8,128)(2,1)S(1)} %get-tuple-element.183.norm_ref.refs_2_.refs_3_.refs_4_.refs_5_.refs_6_, bf16[256,2816]{1,0:T(8,128)(2,1)} %constant_dynamic-update-slice_fusion.14.refs_0_.refs_2_, ...), custom_call_target="tpu_custom_call" | custom-call | flops 1024 | bytes 1024 | tf_op jit(solution)/shard_map/pallas_call | solution.py:37
  217.7 4.1 %shard_map.193 = (bf16[512,1408]{1,0:T(8,128)(2,1)S(1)}, bf16[512,1408]{1,0:T(8,128)(2,1)S(1)}) custom-call(bf16[512,1024]{1,0:T(8,128)(2,1)S(1)} %copy-done, f32[512,1408]{1,0:T(8,128)S(1)} %get-tuple-element.195.factor_ref, f32[512,1408]{1,0:T(8,128)S(1)} %get-tuple-element.196.active_ref, ...), custom_call_target="tpu_custom_call" | custom-call | flops 1024 | bytes 1024 | tf_op jit(solution)/shard_map/pallas_call | solution.py:37
  228.4 7.5 %shard_map.195 = (f32[512,1024]{1,0:T(8,128)S(1)}, bf16[512,1024]{1,0:T(8,128)(2,1)}) custom-call(bf16[512,1408]{1,0:T(8,128)(2,1)S(1)} %get-tuple-element.207.refs_0_, bf16[512,1408]{1,0:T(8,128)(2,1)S(1)} %get-tuple-element.208.refs_1_, bf16[256,2816]{1,0:T(8,128)(2,1)} %constant_dynamic-update-slice_fusion.14.refs_0_.refs_2_, ...), custom_call_target="tpu_custom_call" | custom-call | flops 1024 | bytes 1024 | tf_op jit(solution)/shard_map/pallas_call | solution.py:37
  237.8 4.7 %collective-permute-done.32.refs_2_ = bf16[256,1408]{1,0:T(8,128)(2,1)S(1)} collective-permute-done((bf16[256,1408]{1,0:T(8,128)(2,1)}, bf16[256,1408]{1,0:T(8,128)(2,1)S(1)}, u32[]{:S(2)}, u32[]{:S(2)}) %collective-permute-start.32) | collective-permute-done | bytes 720928 | tf_op jit(solution)/shard_map/ppermute | solution.py:185
  247.8 3.3 collective-permute-start.38
  251.4 3.8 shard_map.198
  256.9 6.7 %collective-permute-done.38 = bf16[64,1408]{1,0:T(8,128)(2,1)S(1)} collective-permute-done((bf16[64,1408]{1,0:T(8,128)(2,1)S(1)}, bf16[64,1408]{1,0:T(8,128)(2,1)S(1)}, u32[]{:S(2)}, u32[]{:S(2)}) %collective-permute-start.38) | collective-permute-done | bytes 180256 | tf_op jit(solution)/shard_map/ppermute | solution.py:233
  263.7 3.0 shard_map.201
  275.9 14.6 %shard_map.200 = (bf16[2,256,512]{2,1,0:T(8,128)(2,1)S(1)}, f32[2,2,256,512]{3,2,1,0:T(8,128)S(1)}, bf16[2,2,64,512]{3,2,1,0:T(8,128)(2,1)S(1)}, bf16[2,2,64,512]{3,2,1,0:T(8,128)(2,1)S(1)}) custom-call(bf16[2,384,1536]{2,1,0:T(8,128)(2,1)S(1)} %bitcast.114, bf16[2,384,1536]{2,1,0:T(8,128)(2,1)S(1)} %bitcast.115, bf16[2,384,1536]{2,1,0:T(8,128)(2,1)S(1)} %bitcast.116, ...), custom_call_target="tpu_custom_call" | custom-call | flops 1024 | bytes 1024 | tf_op jit(solution)/shard_map/pallas_call | solution.py:37
  296.0 13.8 %collective-permute-done.40.low_ref = bf16[2,2,64,512]{3,2,1,0:T(8,128)(2,1)S(1)} collective-permute-done((bf16[2,2,64,512]{3,2,1,0:T(8,128)(2,1)S(1)}, bf16[2,2,64,512]{3,2,1,0:T(8,128)(2,1)S(1)}, u32[]{:S(2)}, u32[]{:S(2)}) %collective-permute-start.40) | collective-permute-done | bytes 262176 | tf_op jit(solution)/shard_map/ppermute | solution.py:805
  309.8 2.9 shard_map.204
  319.7 8.4 %collective-permute-done.44.refs_7_ = bf16[128,2048]{1,0:T(8,128)(2,1)S(1)} collective-permute-done((bf16[128,2048]{1,0:T(8,128)(2,1)S(1)}, bf16[128,2048]{1,0:T(8,128)(2,1)S(1)}, u32[]{:S(2)}, u32[]{:S(2)}) %collective-permute-start.44) | collective-permute-done | bytes 524320 | tf_op jit(solution)/shard_map/ppermute | solution.py:185
  329.6 4.1 %shard_map.205 = f32[512,1024]{1,0:T(8,128)S(1)} custom-call(bf16[512,1408]{1,0:T(8,128)(2,1)S(1)} %copy-done.8, bf16[256,1408]{1,0:T(8,128)(2,1)} %constant_dynamic-update-slice_fusion.18.refs_0_.refs_1_, bf16[256,1408]{1,0:T(8,128)(2,1)} %collective-permute-done.26.refs_1_.refs_2_, bf16[256,1408]{1,0:T(8,128)(2,1)} %collective-permute-done.27.refs_2_.refs_3_, ...), custom_call_target="tpu_custom_call" | custom-call | flops 1024 | bytes 1024 | tf_op jit(solution)/shard_map/pallas_call | solution.py:37
  337.3 4.8 %collective-permute-start.52 = (bf16[64,2816]{1,0:T(8,128)(2,1)S(1)}, bf16[64,2816]{1,0:T(8,128)(2,1)S(1)}, u32[]{:S(2)}, u32[]{:S(2)}) collective-permute-start(bf16[64,2816]{1,0:T(8,128)(2,1)S(1)} %get-tuple-element.274), channel_id=1, source_target_pairs={{0,4},{4,8},{8,12},{12,0},{1,5},{5,9},{9,13},{13,1},{2,6},{6,10},{... | collective-permute-start | bytes 1081352 | tf_op jit(solution)/shard_map/ppermute | solution.py:233
  350.3 3.1 fusion.3
  353.4 11.7 %collective-permute-done.51 = bf16[64,2816]{1,0:T(8,128)(2,1)S(1)} collective-permute-done((bf16[64,2816]{1,0:T(8,128)(2,1)S(1)}, bf16[64,2816]{1,0:T(8,128)(2,1)S(1)}, u32[]{:S(2)}, u32[]{:S(2)}) %collective-permute-start.51) | collective-permute-done | bytes 360480 | tf_op jit(solution)/shard_map/ppermute | solution.py:233
  365.5 5.0 %collective-permute-done.48.refs_4_ = bf16[256,2048]{1,0:T(8,128)(2,1)S(1)} collective-permute-done((bf16[256,2048]{1,0:T(8,128)(2,1)S(1)}, bf16[256,2048]{1,0:T(8,128)(2,1)S(1)}, u32[]{:S(2)}, u32[]{:S(2)}) %collective-permute-start.48) | collective-permute-done | bytes 1048608 | tf_op jit(solution)/shard_map/ppermute | solution.py:185
  371.9 5.4 %collective-permute-start.53 = (bf16[64,2048]{1,0:T(8,128)(2,1)S(1)}, bf16[64,2048]{1,0:T(8,128)(2,1)S(1)}, u32[]{:S(2)}, u32[]{:S(2)}) collective-permute-start(bf16[64,2048]{1,0:T(8,128)(2,1)S(1)} %get-tuple-element.279), channel_id=1, source_target_pairs={{0,12},{4,0},{8,4},{12,8},{1,13},{5,1},{9,5},{13,9},{2,14},{6,2},{... | collective-permute-start | bytes 786440 | tf_op jit(solution)/shard_map/ppermute | solution.py:233
  378.2 5.8 %collective-permute-done.53 = bf16[64,2048]{1,0:T(8,128)(2,1)S(1)} collective-permute-done((bf16[64,2048]{1,0:T(8,128)(2,1)S(1)}, bf16[64,2048]{1,0:T(8,128)(2,1)S(1)}, u32[]{:S(2)}, u32[]{:S(2)}) %collective-permute-start.53) | collective-permute-done | bytes 262176 | tf_op jit(solution)/shard_map/ppermute | solution.py:233
  384.0 6.1 %collective-permute-done.55 = bf16[64,2048]{1,0:T(8,128)(2,1)S(1)} collective-permute-done((bf16[64,2048]{1,0:T(8,128)(2,1)S(1)}, bf16[64,2048]{1,0:T(8,128)(2,1)S(1)}, u32[]{:S(2)}, u32[]{:S(2)}) %collective-permute-start.55) | collective-permute-done | bytes 262176 | tf_op jit(solution)/shard_map/ppermute | solution.py:233
  390.1 8.6 %collective-permute-done.54 = bf16[64,2048]{1,0:T(8,128)(2,1)S(1)} collective-permute-done((bf16[64,2048]{1,0:T(8,128)(2,1)S(1)}, bf16[64,2048]{1,0:T(8,128)(2,1)S(1)}, u32[]{:S(2)}, u32[]{:S(2)}) %collective-permute-start.54) | collective-permute-done | bytes 262176 | tf_op jit(solution)/shard_map/ppermute | solution.py:233
  (386 shorter events, 145.4 us)
Async XLA Ops:
  12.5 22.9 %collective-permute-start.5 = (bf16[64,2176]{1,0:T(8,128)(2,1)S(1)}, bf16[64,2176]{1,0:T(8,128)(2,1)S(1)}, u32[]{:S(2)}, u32[]{:S(2)}) collective-permute-start(bf16[64,2176]{1,0:T(8,128)(2,1)S(1)} %pad_maximum_fusion.5), channel_id=1, source_target_pairs={{0,12},{4,0},{8,4},{12,8},{1,13},{5,1},{9,5},{13,9},{2,14},{6,2},{... | collective-permute-start | bytes 835592 | tf_op jit(solution)/shard_map/ppermute | solution.py:79
  17.2 24.8 %collective-permute-start.4 = (bf16[64,2176]{1,0:T(8,128)(2,1)S(1)}, bf16[64,2176]{1,0:T(8,128)(2,1)S(1)}, u32[]{:S(2)}, u32[]{:S(2)}) collective-permute-start(bf16[64,2176]{1,0:T(8,128)(2,1)S(1)} %pad_maximum_fusion.5), channel_id=1, source_target_pairs={{0,8},{4,12},{8,0},{12,4},{1,9},{5,13},{9,1},{13,5},{2,10},{6,14},... | collective-permute-start | bytes 835592 | tf_op jit(solution)/shard_map/ppermute | solution.py:79
  17.2 24.8 %collective-permute-start.3 = (bf16[64,2176]{1,0:T(8,128)(2,1)S(1)}, bf16[64,2176]{1,0:T(8,128)(2,1)S(1)}, u32[]{:S(2)}, u32[]{:S(2)}) collective-permute-start(bf16[64,2176]{1,0:T(8,128)(2,1)S(1)} %pad_maximum_fusion.5), channel_id=1, source_target_pairs={{0,4},{4,8},{8,12},{12,0},{1,5},{5,9},{9,13},{13,1},{2,6},{6,10},{... | collective-permute-start | bytes 835592 | tf_op jit(solution)/shard_map/ppermute | solution.py:79
  42.2 44.3 %collective-permute-start.14 = (bf16[256,2176]{1,0:T(8,128)(2,1)S(1)}, bf16[256,2176]{1,0:T(8,128)(2,1)S(1)}, u32[]{:S(2)}, u32[]{:S(2)}) collective-permute-start(bf16[256,2176]{1,0:T(8,128)(2,1)S(1)} %constant_dynamic-update-slice_fusion.10.refs_0_.refs_5_.refs_1_), channel_id=1, source_target_pairs={{0,16},{16,0},{1,17},{17,1},{2,18},{18,2},{3,19},{19,3},{4,20},{20... | collective-permute-start | bytes 3342344 | tf_op jit(solution)/shard_map/ppermute | solution.py:73
  43.7 42.7 %collective-permute-start.13 = (bf16[256,2176]{1,0:T(8,128)(2,1)S(1)}, bf16[256,2176]{1,0:T(8,128)(2,1)S(1)}, u32[]{:S(2)}, u32[]{:S(2)}) collective-permute-start(bf16[256,2176]{1,0:T(8,128)(2,1)S(1)} %constant_dynamic-update-slice_fusion.10.refs_0_.refs_5_.refs_1_), channel_id=1, source_target_pairs={{0,2},{2,0},{1,3},{3,1},{4,6},{6,4},{5,7},{7,5},{8,10},{10,8},{9,1... | collective-permute-start | bytes 3342344 | tf_op jit(solution)/shard_map/ppermute | solution.py:73
  50.5 36.0 %collective-permute-start.11 = (bf16[64,2816]{1,0:T(8,128)(2,1)S(1)}, bf16[64,2816]{1,0:T(8,128)(2,1)S(1)}, u32[]{:S(2)}, u32[]{:S(2)}) collective-permute-start(bf16[64,2816]{1,0:T(8,128)(2,1)S(1)} %pad_maximum_fusion.3), channel_id=1, source_target_pairs={{0,8},{4,12},{8,0},{12,4},{1,9},{5,13},{9,1},{13,5},{2,10},{6,14},... | collective-permute-start | bytes 1081352 | tf_op jit(solution)/shard_map/ppermute | solution.py:79
  55.8 30.7 %collective-permute-start.10 = (bf16[64,2816]{1,0:T(8,128)(2,1)S(1)}, bf16[64,2816]{1,0:T(8,128)(2,1)S(1)}, u32[]{:S(2)}, u32[]{:S(2)}) collective-permute-start(bf16[64,2816]{1,0:T(8,128)(2,1)S(1)} %pad_maximum_fusion.3), channel_id=1, source_target_pairs={{0,4},{4,8},{8,12},{12,0},{1,5},{5,9},{9,13},{13,1},{2,6},{6,10},{... | collective-permute-start | bytes 1081352 | tf_op jit(solution)/shard_map/ppermute | solution.py:79
  89.8 70.6 %collective-permute-start.19 = (bf16[256,2816]{1,0:T(8,128)(2,1)}, bf16[256,2816]{1,0:T(8,128)(2,1)}, u32[]{:S(2)}, u32[]{:S(2)}) collective-permute-start(bf16[256,2816]{1,0:T(8,128)(2,1)} %constant_dynamic-update-slice_fusion.14.refs_0_.refs_2_), channel_id=1, source_target_pairs={{0,16},{16,0},{1,17},{17,1},{2,18},{18,2},{3,19},{19,3},{4,20},{20... | collective-permute-start | bytes 4325384 | tf_op jit(solution)/shard_map/ppermute | solution.py:73
  90.3 70.1 %collective-permute-start.18 = (bf16[256,2816]{1,0:T(8,128)(2,1)}, bf16[256,2816]{1,0:T(8,128)(2,1)}, u32[]{:S(2)}, u32[]{:S(2)}) collective-permute-start(bf16[256,2816]{1,0:T(8,128)(2,1)} %constant_dynamic-update-slice_fusion.14.refs_0_.refs_2_), channel_id=1, source_target_pairs={{0,2},{2,0},{1,3},{3,1},{4,6},{6,4},{5,7},{7,5},{8,10},{10,8},{9,1... | collective-permute-start | bytes 4325384 | tf_op jit(solution)/shard_map/ppermute | solution.py:73
  92.1 41.8 %collective-permute-start.15 = (bf16[128,2176]{1,0:T(8,128)(2,1)S(1)}, bf16[128,2176]{1,0:T(8,128)(2,1)S(1)}, u32[]{:S(2)}, u32[]{:S(2)}) collective-permute-start(bf16[128,2176]{1,0:T(8,128)(2,1)S(1)} %slice.187), channel_id=1, source_target_pairs={{0,2},{2,0},{1,3},{3,1},{4,6},{6,4},{5,7},{7,5},{8,10},{10,8},{9,1... | collective-permute-start | bytes 1671176 | tf_op jit(solution)/shard_map/ppermute | solution.py:73
  92.4 42.3 %collective-permute-start.16 = (bf16[128,2176]{1,0:T(8,128)(2,1)S(1)}, bf16[128,2176]{1,0:T(8,128)(2,1)S(1)}, u32[]{:S(2)}, u32[]{:S(2)}) collective-permute-start(bf16[128,2176]{1,0:T(8,128)(2,1)S(1)} %slice.188), channel_id=1, source_target_pairs={{0,16},{16,0},{1,17},{17,1},{2,18},{18,2},{3,19},{19,3},{4,20},{20... | collective-permute-start | bytes 1671176 | tf_op jit(solution)/shard_map/ppermute | solution.py:73
  135.6 24.7 %collective-permute-start.22 = (bf16[64,1408]{1,0:T(8,128)(2,1)}, bf16[64,1408]{1,0:T(8,128)(2,1)}, u32[]{:S(2)}, u32[]{:S(2)}) collective-permute-start(bf16[64,1408]{1,0:T(8,128)(2,1)} %pad_maximum_fusion.6), channel_id=1, source_target_pairs={{0,12},{4,0},{8,4},{12,8},{1,13},{5,1},{9,5},{13,9},{2,14},{6,2},{... | collective-permute-start | bytes 540680 | tf_op jit(solution)/shard_map/ppermute | solution.py:79
  135.6 24.7 %collective-permute-start.21 = (bf16[64,1408]{1,0:T(8,128)(2,1)}, bf16[64,1408]{1,0:T(8,128)(2,1)}, u32[]{:S(2)}, u32[]{:S(2)}) collective-permute-start(bf16[64,1408]{1,0:T(8,128)(2,1)} %pad_maximum_fusion.6), channel_id=1, source_target_pairs={{0,8},{4,12},{8,0},{12,4},{1,9},{5,13},{9,1},{13,5},{2,10},{6,14},... | collective-permute-start | bytes 540680 | tf_op jit(solution)/shard_map/ppermute | solution.py:79
  139.4 20.9 %collective-permute-start.20 = (bf16[64,1408]{1,0:T(8,128)(2,1)}, bf16[64,1408]{1,0:T(8,128)(2,1)}, u32[]{:S(2)}, u32[]{:S(2)}) collective-permute-start(bf16[64,1408]{1,0:T(8,128)(2,1)} %pad_maximum_fusion.6), channel_id=1, source_target_pairs={{0,4},{4,8},{8,12},{12,0},{1,5},{5,9},{9,13},{13,1},{2,6},{6,10},{... | collective-permute-start | bytes 540680 | tf_op jit(solution)/shard_map/ppermute | solution.py:79
  166.3 19.2 %collective-permute-start.24 = (bf16[128,2816]{1,0:T(8,128)(2,1)}, bf16[128,2816]{1,0:T(8,128)(2,1)S(1)}, u32[]{:S(2)}, u32[]{:S(2)}) collective-permute-start(bf16[128,2816]{1,0:T(8,128)(2,1)} %slice.194), channel_id=1, source_target_pairs={{0,2},{2,0},{1,3},{3,1},{4,6},{6,4},{5,7},{7,5},{8,10},{10,8},{9,1... | collective-permute-start | bytes 2162696 | tf_op jit(solution)/shard_map/ppermute | solution.py:73
  167.9 19.3 %collective-permute-start.25 = (bf16[128,2816]{1,0:T(8,128)(2,1)}, bf16[128,2816]{1,0:T(8,128)(2,1)}, u32[]{:S(2)}, u32[]{:S(2)}) collective-permute-start(bf16[128,2816]{1,0:T(8,128)(2,1)} %slice.195), channel_id=1, source_target_pairs={{0,16},{16,0},{1,17},{17,1},{2,18},{18,2},{3,19},{19,3},{4,20},{20... | collective-permute-start | bytes 2162696 | tf_op jit(solution)/shard_map/ppermute | solution.py:73
  174.2 27.3 %collective-permute-start.27 = (bf16[256,1408]{1,0:T(8,128)(2,1)}, bf16[256,1408]{1,0:T(8,128)(2,1)}, u32[]{:S(2)}, u32[]{:S(2)}) collective-permute-start(bf16[256,1408]{1,0:T(8,128)(2,1)} %constant_dynamic-update-slice_fusion.18.refs_0_.refs_1_), channel_id=1, source_target_pairs={{0,16},{16,0},{1,17},{17,1},{2,18},{18,2},{3,19},{19,3},{4,20},{20... | collective-permute-start | bytes 2162696 | tf_op jit(solution)/shard_map/ppermute | solution.py:73
  174.7 26.8 %collective-permute-start.26 = (bf16[256,1408]{1,0:T(8,128)(2,1)}, bf16[256,1408]{1,0:T(8,128)(2,1)}, u32[]{:S(2)}, u32[]{:S(2)}) collective-permute-start(bf16[256,1408]{1,0:T(8,128)(2,1)} %constant_dynamic-update-slice_fusion.18.refs_0_.refs_1_), channel_id=1, source_target_pairs={{0,2},{2,0},{1,3},{3,1},{4,6},{6,4},{5,7},{7,5},{8,10},{10,8},{9,1... | collective-permute-start | bytes 2162696 | tf_op jit(solution)/shard_map/ppermute | solution.py:73
  243.3 20.4 %collective-permute-start.35 = (bf16[128,2816]{1,0:T(8,128)(2,1)}, bf16[128,2816]{1,0:T(8,128)(2,1)S(1)}, u32[]{:S(2)}, u32[]{:S(2)}) collective-permute-start(bf16[128,2816]{1,0:T(8,128)(2,1)} %get-tuple-element.221), channel_id=1, source_target_pairs={{0,2},{2,0},{1,3},{3,1},{4,6},{6,4},{5,7},{7,5},{8,10},{10,8},{9,1... | collective-permute-start | bytes 2162696 | tf_op jit(solution)/shard_map/ppermute | solution.py:185
  244.1 19.6 %collective-permute-start.36 = (bf16[128,2816]{1,0:T(8,128)(2,1)S(1)}, bf16[128,2816]{1,0:T(8,128)(2,1)S(1)}, u32[]{:S(2)}, u32[]{:S(2)}) collective-permute-start(bf16[128,2816]{1,0:T(8,128)(2,1)S(1)} %get-tuple-element.222), channel_id=1, source_target_pairs={{0,16},{16,0},{1,17},{17,1},{2,18},{18,2},{3,19},{19,3},{4,20},{20... | collective-permute-start | bytes 2162696 | tf_op jit(solution)/shard_map/ppermute | solution.py:185
  266.7 43.0 %collective-permute-start.42 = (bf16[256,2816]{1,0:T(8,128)(2,1)}, bf16[256,2816]{1,0:T(8,128)(2,1)}, u32[]{:S(2)}, u32[]{:S(2)}) collective-permute-start(bf16[256,2816]{1,0:T(8,128)(2,1)} %get-tuple-element.232), channel_id=1, source_target_pairs={{0,2},{2,0},{1,3},{3,1},{4,6},{6,4},{5,7},{7,5},{8,10},{10,8},{9,1... | collective-permute-start | bytes 4325384 | tf_op jit(solution)/shard_map/ppermute | solution.py:185
  267.9 41.9 %collective-permute-start.43 = (bf16[256,2816]{1,0:T(8,128)(2,1)}, bf16[256,2816]{1,0:T(8,128)(2,1)}, u32[]{:S(2)}, u32[]{:S(2)}) collective-permute-start(bf16[256,2816]{1,0:T(8,128)(2,1)} %get-tuple-element.233), channel_id=1, source_target_pairs={{0,16},{16,0},{1,17},{17,1},{2,18},{18,2},{3,19},{19,3},{4,20},{20... | collective-permute-start | bytes 4325384 | tf_op jit(solution)/shard_map/ppermute | solution.py:185
  290.6 19.2 %collective-permute-start.40 = (bf16[2,2,64,512]{3,2,1,0:T(8,128)(2,1)S(1)}, bf16[2,2,64,512]{3,2,1,0:T(8,128)(2,1)S(1)}, u32[]{:S(2)}, u32[]{:S(2)}) collective-permute-start(bf16[2,2,64,512]{3,2,1,0:T(8,128)(2,1)S(1)} %get-tuple-element.228), channel_id=1, source_target_pairs={{0,2},{2,4},{4,6},{6,8},{8,10},{10,12},{12,14},{1,3},{3,5},{5,7},{... | collective-permute-start | bytes 786440 | tf_op jit(solution)/shard_map/ppermute | solution.py:805
  293.3 16.5 %collective-permute-start.41 = (bf16[2,2,64,512]{3,2,1,0:T(8,128)(2,1)S(1)}, bf16[2,2,64,512]{3,2,1,0:T(8,128)(2,1)S(1)}, u32[]{:S(2)}, u32[]{:S(2)}) collective-permute-start(bf16[2,2,64,512]{3,2,1,0:T(8,128)(2,1)S(1)} %get-tuple-element.229), channel_id=1, source_target_pairs={{2,0},{4,2},{6,4},{8,6},{10,8},{12,10},{14,12},{3,1},{5,3},{7,5},{... | collective-permute-start | bytes 786440 | tf_op jit(solution)/shard_map/ppermute | solution.py:806
  295.8 23.1 %collective-permute-start.58 = (f32[32,1408]{1,0:T(8,128)S(1)}, f32[32,1408]{1,0:T(8,128)S(1)}, u32[]{:S(2)}, u32[]{:S(2)}) collective-permute-start(f32[32,1408]{1,0:T(8,128)S(1)} %get-tuple-element.300), channel_id=1, source_target_pairs={{0,1},{1,0},{2,3},{3,2},{4,5},{5,4},{6,7},{7,6},{8,9},{9,8},{10,11... | collective-permute-start | bytes 540680 | tf_op jit(solution)/shard_map/ppermute | solution.py:55
  337.3 16.1 %collective-permute-start.52 = (bf16[64,2816]{1,0:T(8,128)(2,1)S(1)}, bf16[64,2816]{1,0:T(8,128)(2,1)S(1)}, u32[]{:S(2)}, u32[]{:S(2)}) collective-permute-start(bf16[64,2816]{1,0:T(8,128)(2,1)S(1)} %get-tuple-element.274), channel_id=1, source_target_pairs={{0,4},{4,8},{8,12},{12,0},{1,5},{5,9},{9,13},{13,1},{2,6},{6,10},{... | collective-permute-start | bytes 1081352 | tf_op jit(solution)/shard_map/ppermute | solution.py:233
  342.1 23.0 %collective-permute-start.51 = (bf16[64,2816]{1,0:T(8,128)(2,1)S(1)}, bf16[64,2816]{1,0:T(8,128)(2,1)S(1)}, u32[]{:S(2)}, u32[]{:S(2)}) collective-permute-start(bf16[64,2816]{1,0:T(8,128)(2,1)S(1)} %get-tuple-element.275), channel_id=1, source_target_pairs={{0,8},{4,12},{8,0},{12,4},{1,9},{5,13},{9,1},{13,5},{2,10},{6,14},... | collective-permute-start | bytes 1081352 | tf_op jit(solution)/shard_map/ppermute | solution.py:233
  342.1 23.4 %collective-permute-start.50 = (bf16[64,2816]{1,0:T(8,128)(2,1)S(1)}, bf16[64,2816]{1,0:T(8,128)(2,1)S(1)}, u32[]{:S(2)}, u32[]{:S(2)}) collective-permute-start(bf16[64,2816]{1,0:T(8,128)(2,1)S(1)} %get-tuple-element.276), channel_id=1, source_target_pairs={{0,12},{4,0},{8,4},{12,8},{1,13},{5,1},{9,5},{13,9},{2,14},{6,2},{... | collective-permute-start | bytes 1081352 | tf_op jit(solution)/shard_map/ppermute | solution.py:233
  345.9 24.6 %collective-permute-start.48 = (bf16[256,2048]{1,0:T(8,128)(2,1)S(1)}, bf16[256,2048]{1,0:T(8,128)(2,1)S(1)}, u32[]{:S(2)}, u32[]{:S(2)}) collective-permute-start(bf16[256,2048]{1,0:T(8,128)(2,1)S(1)} %get-tuple-element.259), channel_id=1, source_target_pairs={{0,2},{2,0},{1,3},{3,1},{4,6},{6,4},{5,7},{7,5},{8,10},{10,8},{9,1... | collective-permute-start | bytes 3145736 | tf_op jit(solution)/shard_map/ppermute | solution.py:185
  346.6 24.4 %collective-permute-start.49 = (bf16[256,2048]{1,0:T(8,128)(2,1)S(1)}, bf16[256,2048]{1,0:T(8,128)(2,1)S(1)}, u32[]{:S(2)}, u32[]{:S(2)}) collective-permute-start(bf16[256,2048]{1,0:T(8,128)(2,1)S(1)} %get-tuple-element.260), channel_id=1, source_target_pairs={{0,16},{16,0},{1,17},{17,1},{2,18},{18,2},{3,19},{19,3},{4,20},{20... | collective-permute-start | bytes 3145736 | tf_op jit(solution)/shard_map/ppermute | solution.py:185
  377.3 21.5 %collective-permute-start.54 = (bf16[64,2048]{1,0:T(8,128)(2,1)S(1)}, bf16[64,2048]{1,0:T(8,128)(2,1)S(1)}, u32[]{:S(2)}, u32[]{:S(2)}) collective-permute-start(bf16[64,2048]{1,0:T(8,128)(2,1)S(1)} %get-tuple-element.281), channel_id=1, source_target_pairs={{0,8},{4,12},{8,0},{12,4},{1,9},{5,13},{9,1},{13,5},{2,10},{6,14},... | collective-permute-start | bytes 786440 | tf_op jit(solution)/shard_map/ppermute | solution.py:233
  378.1 20.9 %collective-permute-start.57 = (f32[32,2816]{1,0:T(8,128)S(1)}, f32[32,2816]{1,0:T(8,128)S(1)}, u32[]{:S(2)}, u32[]{:S(2)}) collective-permute-start(f32[32,2816]{1,0:T(8,128)S(1)} %dynamic-slice_bitcast_fusion), channel_id=1, source_target_pairs={{0,1},{1,0},{2,3},{3,2},{4,5},{5,4},{6,7},{7,6},{8,9},{9,8},{10,11... | collective-permute-start | bytes 1081352 | tf_op jit(solution)/shard_map/ppermute | solution.py:55
  (114 other events, 990.2 us)
